TPU v7x, 128 devices: a whole 4x4x4 slice. The times are simulated.
128 devices in a mesh: xs: 4 (over x), ax: 32 (over y, z, core).
Axes of the slice: x: 4, y: 4, z: 4, core: 2. Of those that a mesh axis runs over, the one named last changes fastest.
Arguments:
- concentration: float32 [1024, 128, 384], P('ax', 'xs'), may hold values from -4 to 4
- tissue_mask: int32 [1024, 128, 384], P('ax', 'xs'), may hold values from 0 to 1
- wall_layer: int32 [1024, 128, 384], P('ax', 'xs'), may hold values from 0 to 3, as said below
- stiffness: float32 [1024, 128, 384], P('ax', 'xs'), may hold values from 1 to 2
- production: float32 [1024, 128, 384], P('ax', 'xs'), may hold values from -3 to 3
- layer_diffusivity: float32 [4], replicated, may hold values from 1 to 2
- uptake_rate: float32 [4], replicated, may hold values from 0.1 to 0.5
Outputs:
- concentration_out: float32 [1024, 128, 384], P('ax', 'xs')
Inputs may be any that keep to these rules, and one draw needn't show every extreme that they name: `wall_layer`: indexes the tables of layer coefficients.
All inputs are finite; a program needn't handle non-finite values.
Results may differ from a plain program's by a relative error of at most 0.0003.
Values sent between devices are 32-bit elements; how exact they have to be, the bound alone decides.
No kernel may reach another device: no remote copies, remote signals or barrier semaphores. Data moves between devices by JAX's collectives and lax.ppermute only.
A program may use at most 128 MiB of HBM per device.

v0:
```python
import functools

import jax
import jax.numpy as jnp
from jax import lax
from jax.experimental import pallas as pl
from jax.experimental.pallas import tpu as pltpu
from jax.sharding import PartitionSpec as P

RZ = 3072.0
SECTION_RATE = 0.05
LAYERS = 4
LIMIT = 20 * 1024 * 1024
CHUNK = 8


def at_vmem(*shape):
    return pltpu.VMEM(shape, jnp.float32)


def vspec():
    return pl.BlockSpec(memory_space=pltpu.VMEM)


def params():
    return pltpu.CompilerParams(vmem_limit_bytes=LIMIT)


def cost(us):
    return pl.CostEstimate(flops=int(us * 2e6), bytes_accessed=int(us * 3e6), transcendentals=0)


def lookup(labels, table):
    summed = jnp.where(labels == 0, table[0], 0.0)
    for layer in range(1, LAYERS):
        summed = jnp.where(labels == layer, table[layer], summed)
    return summed


def neighbour_sum(plane):
    slab, cols = plane.shape
    row = lax.broadcasted_iota(jnp.int32, plane.shape, 0)
    col = lax.broadcasted_iota(jnp.int32, plane.shape, 1)
    below = jnp.where(row == 0, 0.0, pltpu.roll(plane, 1, 0))
    above = jnp.where(row == slab - 1, 0.0, pltpu.roll(plane, slab - 1, 0))
    left = jnp.where(col == 0, 0.0, pltpu.roll(plane, 1, 1))
    right = jnp.where(col == cols - 1, 0.0, pltpu.roll(plane, cols - 1, 1))
    return (below + above) + (left + right)


def setup_kernel(
    rows,
    diff_table, uptake_table, conc_hbm, mask_hbm, layer_hbm, stiff_hbm, prod_hbm,
    s_out, g_out, r_out, gp_out, keep_out, source_out, ssum_out, part_out, ends_out,
    conc, mask, layer, stiff, prod, sems,
):
    pairs = ((mask_hbm, mask), (layer_hbm, layer), (stiff_hbm, stiff), (conc_hbm, conc), (prod_hbm, prod))
    copies = []
    for chunk in range(rows // CHUNK):
        here = pl.ds(chunk * CHUNK, CHUNK)
        copies.append([
            pltpu.make_async_copy(source.at[here], target.at[here], sems.at[k, chunk])
            for k, (source, target) in enumerate(pairs)
        ])
    for group in copies:
        for copy in group:
            copy.start()
    dtab = [diff_table[k] for k in range(LAYERS)]
    utab = [uptake_table[k] for k in range(LAYERS)]

    def plane_setup(z):
        weight = mask[z].astype(jnp.float32)
        labels = layer[z]
        s = jnp.sqrt(weight * lookup(labels, dtab) * stiff[z])
        s_out[z] = s
        keep_out[z] = 1.0 - weight * lookup(labels, utab)
        source_out[z] = weight * prod[z]
        state = conc[z]
        ssum = neighbour_sum(s)
        ssum_out[z] = ssum
        part_out[z] = state + SECTION_RATE * s * (neighbour_sum(s * state) - state * ssum)
        return s

    for z in range(rows):
        if z % CHUNK == 0:
            for copy in copies[z // CHUNK]:
                copy.wait()
        s_next = plane_setup(z)
        if z == 0:
            m = jnp.ones_like(s_next)
            gp = jnp.ones_like(s_next)
            alpha = jnp.zeros_like(s_next)
        else:
            c = RZ * s * s_next
            r = 1.0 / (m + c)
            g = c * r
            r_out[z - 1] = r
            g_out[z - 1] = g
            gp_out[z - 1] = gp
            alpha = alpha + r * gp * gp
            m = 1.0 + g * m
            gp = gp * g
        s = s_next
    gp_out[rows - 1] = gp
    ends_out[0] = m
    ends_out[1] = alpha


def halo_term(z, s_ref, state_row, s_halo, v_halo):
    return SECTION_RATE * s_ref * (v_halo - state_row * s_halo)


def forward_sweep(rows, slab, first_step, ix, nx, state_ref, s_ref, g_ref, r_ref, gp_ref, part_ref, lo_ref, hi_ref,
                  shalo_lo, shalo_hi, last_g, last_r, fwd_ref):
    row = lax.broadcasted_iota(jnp.int32, (8, lo_ref.shape[-1]), 0)
    top = jnp.where(row == 0, jnp.where(ix > 0, SECTION_RATE, 0.0), 0.0)
    bottom = jnp.where(row == 7, jnp.where(ix < nx - 1, SECTION_RATE, 0.0), 0.0)
    total = None
    prev = None
    for z in range(rows):
        st_lo, st_hi = state_ref(z, 0), state_ref(z, 1)
        s_lo, s_hi = s_ref[z, 0:8], s_ref[z, slab - 8:slab]
        sl, sh = shalo_lo[z:z + 1], shalo_hi[z:z + 1]
        vl, vh = lo_ref[z:z + 1], hi_ref[z:z + 1]
        if first_step:
            vl, vh = vl * sl, vh * sh
        extra_lo = top * s_lo * (vl - st_lo * sl)
        extra_hi = bottom * s_hi * (vh - st_hi * sh)
        part = part_ref[z]
        e = jnp.concatenate([part[0:8] + extra_lo, part[8:slab - 8], part[slab - 8:] + extra_hi], axis=0)
        if z > 0:
            e = e + g_ref[z - 1] * prev
        fwd_ref[z] = e
        r = r_ref[z] if z < rows - 1 else last_r
        term = gp_ref[z] * r * e
        total = term if z == 0 else total + term
        prev = e
    return total, last_g * prev


def first_forward_kernel(
    rows, slab, nx, nax,
    conc_ref, s_ref, g_ref, r_ref, gp_ref, part_ref, ends_ref, lo_ref, hi_ref, ax_ref,
    fwd_ref, last_ref, mine_ref, send_ref, ports_ref,
):
    ix, ia = lax.axis_index("xs"), lax.axis_index("ax")
    above = jnp.where(ia < nax - 1, RZ, 0.0)
    c = above * s_ref[rows - 1] * ax_ref[...]
    m, alpha = ends_ref[0], ends_ref[1]
    last_r = 1.0 / (m + c)
    last_g = c * last_r
    gp = gp_ref[rows - 1]
    last_ref[0] = last_g
    last_ref[1] = last_r
    a, b = forward_sweep(
        rows, slab, True, ix, nx, lambda z, side: conc_ref[z, side], s_ref, g_ref, r_ref, gp_ref, part_ref,
        lo_ref.at[1], hi_ref.at[1], lo_ref.at[0], hi_ref.at[0], last_g, last_r, fwd_ref)
    ports_ref[0] = a
    ports_ref[1] = b
    ports_ref[2] = alpha + last_r * gp * gp
    ports_ref[3] = last_g * gp
    ports_ref[4] = last_g * m
    half = slab // 2
    core = lax.rem(ia, 2)
    mine_ref[...] = ports_ref[:, pl.ds(pl.multiple_of(core * half, half), half)]
    send_ref[...] = ports_ref[:, pl.ds(pl.multiple_of((1 - core) * half, half), half)]


def second_forward_kernel(
    rows, slab, nx,
    edge_ref, s_ref, g_ref, r_ref, gp_ref, part_ref, last_ref, first_lo_ref, first_hi_ref, lo_ref, hi_ref,
    fwd_ref, mine_ref, send_ref, ports_ref,
):
    ix, ia = lax.axis_index("xs"), lax.axis_index("ax")
    a, b = forward_sweep(
        rows, slab, False, ix, nx, lambda z, side: edge_ref[side, z], s_ref, g_ref, r_ref, gp_ref, part_ref,
        lo_ref, hi_ref, first_lo_ref.at[0], first_hi_ref.at[0], last_ref[0], last_ref[1], fwd_ref)
    ports_ref[0] = a
    ports_ref[1] = b
    half = slab // 2
    core = lax.rem(ia, 2)
    mine_ref[...] = ports_ref[:, pl.ds(pl.multiple_of(core * half, half), half)]
    send_ref[...] = ports_ref[:, pl.ds(pl.multiple_of((1 - core) * half, half), half)]


def is_upper(level):
    return lax.rem(lax.div(lax.axis_index("ax"), 2 ** level), 2) == 1


def join(upper, mine, theirs):
    return jnp.where(upper, theirs, mine), jnp.where(upper, mine, theirs)


def join_coefs(level, mine, recv, lev):
    upper = is_upper(level)
    (alpha1, alpha2), (beta1, beta2), (kappa1, kappa2) = [join(upper, mine[k], recv[k]) for k in (2, 3, 4)]
    rho = 1.0 / (1.0 + kappa1 * alpha2)
    x, y = beta1 * rho, beta2 * rho
    ax, ky = alpha2 * x, kappa1 * y
    for k, value in enumerate((rho, kappa1, alpha2, beta1, beta2, x, y, ax, ky)):
        lev[k] = value
    return alpha1 + beta1 * ax, x * beta2, kappa2 + beta2 * ky


def join_rhs(level, mine, recv, lev, values):
    upper = is_upper(level)
    (a1, a2), (b1, b2) = [join(upper, mine[k], recv[k]) for k in (0, 1)]
    rho, kappa1, alpha2, beta1, beta2 = [lev[k] for k in range(5)]
    u0 = rho * (a2 + alpha2 * b1)
    q0 = rho * (b1 - kappa1 * a2)
    values[0] = u0
    values[1] = q0
    return a1 + beta1 * u0, b2 + beta2 * q0


def first_join_kernel(level, mine, recv, out, lev, values):
    out[2], out[3], out[4] = join_coefs(level, mine, recv, lev)
    out[0], out[1] = join_rhs(level, mine, recv, lev, values)


def second_join_kernel(level, mine, recv, lev, out, values):
    out[0], out[1] = join_rhs(level, mine, recv, lev, values)


def below(lev, q, top, u0, q0):
    x, y, ax, ky = [lev[k] for k in (5, 6, 7, 8)]
    return u0 + y * top + ax * q, q0 + x * q - ky * top


def descend(levels, levs, values, mine_out, send_out):
    top_level = levels - 1
    u0, q0 = values[top_level][0], values[top_level][1]
    upper = is_upper(top_level)
    q = jnp.where(upper, q0, 0.0)
    top = jnp.where(upper, 0.0, u0)
    for level in range(top_level - 1, -1, -1):
        new_top, new_q = below(levs[level], q, top, values[level][0], values[level][1])
        upper = is_upper(level)
        if level > 0:
            q, top = jnp.where(upper, new_q, q), jnp.where(upper, top, new_top)
        else:
            mine_out[0] = jnp.where(upper, new_q, q)
            mine_out[1] = jnp.where(upper, top, new_top)
            send_out[0] = jnp.where(upper, q, new_q)
            send_out[1] = jnp.where(upper, new_top, top)


def first_last_kernel(levels, *refs):
    mine, recv = refs[:2]
    levs, values = refs[2:2 + levels - 1], refs[1 + levels:2 * levels]
    mine_out, send_out, lev, last = refs[2 * levels:]
    join_coefs(levels - 1, mine, recv, lev)
    join_rhs(levels - 1, mine, recv, lev, last)
    descend(levels, list(levs) + [lev], list(values) + [last], mine_out, send_out)


def second_last_kernel(levels, *refs):
    mine, recv = refs[:2]
    levs, values = refs[2:2 + levels], refs[2 + levels:1 + 2 * levels]
    mine_out, send_out, last = refs[1 + 2 * levels:]
    join_rhs(levels - 1, mine, recv, levs[-1], last)
    descend(levels, list(levs), list(values) + [last], mine_out, send_out)


def whole_ports(own, other):
    upper = lax.rem(lax.axis_index("ax"), 2) == 1
    planes = []
    for k in (0, 1):
        low, high = jnp.where(upper, other[k], own[k]), jnp.where(upper, own[k], other[k])
        planes.append(jnp.concatenate([low, high], axis=0))
    return planes


def edge_state_kernel(
    rows, slab,
    own, other, s_ref, g_ref, r_ref, gp_ref, fwd_ref, last_ref, keep_ref, source_ref,
    edge_ref, lo_ref, hi_ref,
):
    q, top = whole_ports(own, other)
    for side in (0, 1):
        at = slice(0, 8) if side == 0 else slice(slab - 8, slab)
        u, inflow = top[at], q[at]
        for z in range(rows - 1, -1, -1):
            r = r_ref[z, at] if z < rows - 1 else last_ref[1, at]
            g = g_ref[z, at] if z < rows - 1 else last_ref[0, at]
            u = r * (fwd_ref[z, at] + gp_ref[z, at] * inflow) + g * u
            state = source_ref[z, at] + keep_ref[z, at] * u
            edge_ref[side, z] = state
            flow = s_ref[z, at] * state
            if side == 0:
                lo_ref[z:z + 1] = flow[0:1]
            else:
                hi_ref[z:z + 1] = flow[7:8]


def middle_state_kernel(
    rows, slab,
    own, other, edge_ref, s_ref, g_ref, r_ref, gp_ref, fwd_ref, last_ref, keep_ref, source_ref, ssum_ref,
    part_ref,
):
    q, top = whole_ports(own, other)
    at = slice(8, slab - 8)
    u, inflow = top[at], q[at]
    for z in range(rows - 1, -1, -1):
        r = r_ref[z, at] if z < rows - 1 else last_ref[1, at]
        g = g_ref[z, at] if z < rows - 1 else last_ref[0, at]
        u = r * (fwd_ref[z, at] + gp_ref[z, at] * inflow) + g * u
        middle = source_ref[z, at] + keep_ref[z, at] * u
        state = jnp.concatenate([edge_ref[0, z], middle, edge_ref[1, z]], axis=0)
        s = s_ref[z]
        part_ref[z] = state + SECTION_RATE * s * (neighbour_sum(s * state) - state * ssum_ref[z])


def final_kernel(
    rows, slab,
    own, other, g_ref, r_ref, gp_ref, fwd_ref, last_ref, keep_ref, source_ref,
    out_hbm, out, sems,
):
    q, u = whole_ports(own, other)
    copies = []
    for z in range(rows - 1, -1, -1):
        r = r_ref[z] if z < rows - 1 else last_ref[1]
        g = g_ref[z] if z < rows - 1 else last_ref[0]
        u = r * (fwd_ref[z] + gp_ref[z] * q) + g * u
        out[z] = source_ref[z] + keep_ref[z] * u
        if z % CHUNK == 0:
            here = pl.ds(z, CHUNK)
            copy = pltpu.make_async_copy(out.at[here], out_hbm.at[here], sems.at[z // CHUNK])
            copy.start()
            copies.append(copy)
    for copy in copies:
        copy.wait()


def edge_diffusivity(mask, layer, stiff, table):
    return jnp.sqrt(mask.astype(jnp.float32) * lookup(layer, table) * stiff)


def on_device(partners, concentration, tissue_mask, wall_layer, stiffness, production, layer_diffusivity, uptake_rate):
    rows, slab, cols = concentration.shape
    half = slab // 2
    nx, nax = lax.axis_size("xs"), lax.axis_size("ax")
    levels = len(partners)

    def call(kernel, outs, operands, scratch=(), specs=None, out_specs=None, us=1.0):
        return pl.pallas_call(
            kernel,
            out_shape=outs,
            in_specs=specs or [vspec()] * len(operands),
            out_specs=out_specs or [vspec()] * len(outs),
            scratch_shapes=list(scratch),
            compiler_params=params(),
            cost_estimate=cost(us),
        )(*operands)

    def exchange(block, level):
        return lax.ppermute(block, "ax", partners[level])

    def side(x):
        s = edge_diffusivity(tissue_mask[:, x], wall_layer[:, x], stiffness[:, x], layer_diffusivity)
        return jnp.stack([s, concentration[:, x]])

    first_s = edge_diffusivity(tissue_mask[0], wall_layer[0], stiffness[0], layer_diffusivity)
    upward = [(i, (i + 1) % nx) for i in range(nx)]
    downward = [((i + 1) % nx, i) for i in range(nx)]
    halo_lo = lax.ppermute(side(slab - 1), "xs", upward)
    halo_hi = lax.ppermute(side(0), "xs", downward)
    above_s = lax.ppermute(first_s, "ax", [((i + 1) % nax, i) for i in range(nax)])

    block = (rows, slab, cols)
    smem = pl.BlockSpec(memory_space=pltpu.SMEM)
    hbm = pl.BlockSpec(memory_space=pltpu.HBM)
    s, g, r, gp, keep, source, ssum, part, ends = call(
        functools.partial(setup_kernel, rows),
        [at_vmem(*block)] * 8 + [at_vmem(2, slab, cols)],
        [layer_diffusivity, uptake_rate, concentration, tissue_mask, wall_layer, stiffness, production],
        scratch=[
            pltpu.VMEM(block, jnp.float32), pltpu.VMEM(block, jnp.int32), pltpu.VMEM(block, jnp.int32),
            pltpu.VMEM(block, jnp.float32), pltpu.VMEM(block, jnp.float32),
            pltpu.SemaphoreType.DMA((5, rows // CHUNK)),
        ],
        specs=[smem, smem] + [hbm] * 5,
        us=5.0,
    )
    conc_edges = jnp.stack([concentration[:, :8], concentration[:, slab - 8:]], axis=1)
    fwd, last, mine, send = call(
        functools.partial(first_forward_kernel, rows, slab, nx, nax),
        [at_vmem(*block), at_vmem(2, slab, cols), at_vmem(5, half, cols), at_vmem(5, half, cols)],
        [conc_edges, s, g, r, gp, part, ends, halo_lo, halo_hi, above_s],
        scratch=[pltpu.VMEM((5, slab, cols), jnp.float32)],
    )
    levs, values = [], []
    for level in range(levels - 1):
        recv = exchange(send if level == 0 else mine, level)
        mine, lev, value = call(
            functools.partial(first_join_kernel, level),
            [at_vmem(5, half, cols), at_vmem(9, half, cols), at_vmem(2, half, cols)],
            [mine, recv],
        )
        levs.append(lev)
        values.append(value)
    recv = exchange(mine, levels - 1)
    own, send, lev = call(
        functools.partial(first_last_kernel, levels),
        [at_vmem(2, half, cols), at_vmem(2, half, cols), at_vmem(9, half, cols)],
        [mine, recv, *levs, *values],
        scratch=[pltpu.VMEM((2, half, cols), jnp.float32)],
    )
    levs.append(lev)
    other = exchange(send, 0)

    edges, lo, hi = call(
        functools.partial(edge_state_kernel, rows, slab),
        [at_vmem(2, rows, 8, cols), at_vmem(rows, cols), at_vmem(rows, cols)],
        [own, other, s, g, r, gp, fwd, last, keep, source],
    )
    from_lo = lax.ppermute(hi, "xs", upward)
    from_hi = lax.ppermute(lo, "xs", downward)
    (part,) = call(
        functools.partial(middle_state_kernel, rows, slab),
        [at_vmem(*block)],
        [own, other, edges, s, g, r, gp, fwd, last, keep, source, ssum],
        us=3.0,
    )
    fwd, mine, send = call(
        functools.partial(second_forward_kernel, rows, slab, nx),
        [at_vmem(*block), at_vmem(2, half, cols), at_vmem(2, half, cols)],
        [edges, s, g, r, gp, part, last, halo_lo, halo_hi, from_lo, from_hi],
        scratch=[pltpu.VMEM((2, slab, cols), jnp.float32)],
    )
    values = []
    for level in range(levels - 1):
        recv = exchange(send if level == 0 else mine, level)
        mine, value = call(
            functools.partial(second_join_kernel, level),
            [at_vmem(2, half, cols), at_vmem(2, half, cols)],
            [mine, recv, levs[level]],
        )
        values.append(value)
    recv = exchange(mine, levels - 1)
    own, send = call(
        functools.partial(second_last_kernel, levels),
        [at_vmem(2, half, cols), at_vmem(2, half, cols)],
        [mine, recv, *levs, *values],
        scratch=[pltpu.VMEM((2, half, cols), jnp.float32)],
    )
    other = exchange(send, 0)
    (out,) = call(
        functools.partial(final_kernel, rows, slab),
        [jax.ShapeDtypeStruct(block, jnp.float32)],
        [own, other, g, r, gp, fwd, last, keep, source],
        scratch=[pltpu.VMEM(block, jnp.float32), pltpu.SemaphoreType.DMA((rows // CHUNK,))],
        out_specs=[hbm],
    )
    return out


def join_partners():
    flips = (
        lambda y, z, c: (y, z, 1 - c),
        lambda y, z, c: (y, z ^ 1, c),
        lambda y, z, c: (y, 3 - z, c),
        lambda y, z, c: (y ^ 1, z, c),
        lambda y, z, c: (3 - y, z, c),
    )
    routes = []
    for flip in flips:
        route = []
        for i in range(32):
            y, z, c = flip(i // 8, i // 2 % 4, i % 2)
            route.append((i, y * 8 + z * 2 + c))
        routes.append(route)
    return routes


def solution(mesh):
    placed = (P("ax", "xs", None),) * 5 + (P(), P())
    return jax.shard_map(
        functools.partial(on_device, join_partners()),
        mesh=mesh, in_specs=placed, out_specs=P("ax", "xs", None), check_vma=False,
    )
```

profile of v0, /device:TPU:1, one launch (start us, length us, event | category | flops | bytes accessed | tf_op | source)
XLA Modules:
  0.0 92.4 jit_solution(12895484585355739169)
XLA Ops:
  0.0 0.0 copy-start
  0.0 1.4 %fusion.10 = (f32[1]{0:T(128)}, f32[1]{0:T(128)}, f32[1]{0:T(128)}, f32[1]{0:T(128)}) fusion(f32[4]{0:T(128)} %diff_table.1), kind=kLoop, calls=%fused_computation.22 | loop fusion | bytes 32 | tf_op jit(solution)/shard_map/slice | solution.py:36
  1.4 3.4 %sqrt_bitcast_fusion = f32[32,384]{1,0:T(8,128)S(1)} fusion(f32[32,32,384]{2,1,0:T(8,128)} %stiff_hbm.1, s32[32,32,384]{2,1,0:T(8,128)} %mask_hbm.1, s32[32,32,384]{2,1,0:T(8,128)} %layer_hbm.1, f32[]{:T(128)} %bitcast.2, f32[]{:T(128)} %bitcast.5, f32[]{:T(128)} %bitcast.4, f32[]{:T(128)} %bitcast.3), kind=kLoop, calls=%fused_computation.17 | loop fusion | flops 135168 | bytes 196624 | tf_op jit(solution)/shard_map/sqrt | solution.py:336
  4.8 1.5 %collective-permute-start.2 = (f32[32,384]{1,0:T(8,128)S(1)}, f32[32,384]{1,0:T(8,128)S(1)}, u32[]{:S(2)}, u32[]{:S(2)}) collective-permute-start(f32[32,384]{1,0:T(8,128)S(1)} %sqrt_bitcast_fusion), channel_id=1, source_target_pairs={{1,0},{2,1},{3,2},{4,3},{5,4},{6,5},{7,6},{8,7},{9,8},{10,9},{11,1... | collective-permute-start | bytes 147464 | tf_op jit(solution)/shard_map/ppermute | solution.py:368
  6.3 1.2 %fusion.8 = (f32[32,1,384]{2,1,0:T(1,128)S(1)}, f32[32,1,384]{2,1,0:T(1,128)S(1)}) fusion(f32[32,32,384]{2,1,0:T(8,128)} %stiff_hbm.1), kind=kLoop, calls=%fused_computation.20 | loop fusion | bytes 196608 | tf_op jit(solution)/shard_map/slice | solution.py:360
  7.5 1.5 %fusion.6 = (s32[32,1,384]{2,1,0:T(1,128)S(1)}, s32[32,1,384]{2,1,0:T(1,128)S(1)}, s32[32,1,384]{2,1,0:T(1,128)S(1)}, s32[32,1,384]{2,1,0:T(1,128)S(1)}) fusion(s32[32,32,384]{2,1,0:T(8,128)} %layer_hbm.1, s32[32,32,384]{2,1,0:T(8,128)} %mask_hbm.1), kind=kLoop, calls=%fused_computation.18 | loop fusion | bytes 393216 | tf_op jit(solution)/shard_map/slice | solution.py:360
  9.0 1.2 %fusion.9 = (f32[32,1,384]{2,1,0:T(1,128)S(1)}, f32[32,1,384]{2,1,0:T(1,128)S(1)}) fusion(f32[32,32,384]{2,1,0:T(8,128)} %conc_hbm.1), kind=kLoop, calls=%fused_computation.21 | loop fusion | bytes 196608 | tf_op jit(solution)/shard_map/slice | solution.py:361
  10.2 2.5 %fusion.1 = f32[1,32,384]{2,1,0:T(8,128)S(1)} fusion(f32[32,1,384]{2,1,0:T(1,128)S(1)} %get-tuple-element.97, s32[32,1,384]{2,1,0:T(1,128)S(1)} %get-tuple-element.108, s32[32,1,384]{2,1,0:T(1,128)S(1)} %get-tuple-element.93, f32[]{:T(128)} %bitcast.2, f32[]{:T(128)} %bitcast.5, f32[]{:T(128)} %bitcast.4, f32[]{:T(128)} %bitcast.3), kind=kLoop, calls=%fused_computation.8 | loop fusion | flops 135168 | bytes 196624 | tf_op jit(solution)/shard_map/sqrt | solution.py:336
  12.7 2.6 %collective-permute-start.1 = (f32[2,32,384]{2,1,0:T(8,128)S(1)}, f32[2,32,384]{2,1,0:T(8,128)S(1)}, u32[]{:S(2)}, u32[]{:S(2)}) collective-permute-start(f32[2,32,384]{2,1,0:T(8,128)S(1)} %pad_maximum_fusion.2), channel_id=1, source_target_pairs={{32,0},{64,32},{96,64},{0,96},{33,1},{65,33},{97,65},{1,97},{34,2}... | collective-permute-start | bytes 294920 | tf_op jit(solution)/shard_map/ppermute | solution.py:367
  15.3 2.5 %fusion.4 = f32[1,32,384]{2,1,0:T(8,128)S(1)} fusion(f32[32,1,384]{2,1,0:T(1,128)S(1)} %get-tuple-element.98, s32[32,1,384]{2,1,0:T(1,128)S(1)} %get-tuple-element.107, s32[32,1,384]{2,1,0:T(1,128)S(1)} %get-tuple-element.94, f32[]{:T(128)} %bitcast.2, f32[]{:T(128)} %bitcast.5, f32[]{:T(128)} %bitcast.4, f32[]{:T(128)} %bitcast.3), kind=kLoop, calls=%fused_computation.14 | loop fusion | flops 135168 | bytes 196624 | tf_op jit(solution)/shard_map/sqrt | solution.py:336
  17.9 0.0 copy-start.1
  17.9 0.0 copy-start.2
  17.9 0.0 copy-start.5
  17.9 0.0 copy-start.6
  17.9 0.1 collective-permute-start
  18.0 0.0 copy-done
  18.0 0.1 slice_bitcast_fusion.1
  18.1 0.1 pad_maximum_fusion.conc_ref
  18.1 1.1 %copy-done.1 = s32[32,32,384]{2,1,0:T(8,128)S(1)} copy-done((s32[32,32,384]{2,1,0:T(8,128)S(1)}, s32[32,32,384]{2,1,0:T(8,128)}, u32[]{:S(2)}) %copy-start.1) | copy-done | bytes 1572888
  19.3 0.5 copy-done.2
  19.8 0.0 copy-done.5
  19.8 0.0 copy-done.6
  19.8 0.0 copy-start.3
  19.8 1.4 %copy-done.3 = f32[32,32,384]{2,1,0:T(8,128)S(1)} copy-done((f32[32,32,384]{2,1,0:T(8,128)S(1)}, f32[32,32,384]{2,1,0:T(8,128)}, u32[]{:S(2)}) %copy-start.3) | copy-done | bytes 1572888
  21.2 1.4 %copy-done.4 = f32[32,32,384]{2,1,0:T(8,128)S(1)} copy-done((f32[32,32,384]{2,1,0:T(8,128)S(1)}, f32[32,32,384]{2,1,0:T(8,128)}, u32[]{:S(2)}) %copy-start.4) | copy-done | bytes 1572888
  22.6 8.0 %shard_map.73 = (f32[32,32,384]{2,1,0:T(8,128)S(1)}, f32[32,32,384]{2,1,0:T(8,128)S(1)}, f32[32,32,384]{2,1,0:T(8,128)S(1)}, f32[32,32,384]{2,1,0:T(8,128)S(1)},...) custom-call(f32[4]{0:T(128)S(1)} %copy-done.5, ...), custom_call_target="tpu_custom_call" | custom-call | flops 10000000 | bytes 15000000 | tf_op jit(solution)/shard_map/pallas_call | solution.py:346
  30.6 0.0 collective-permute-done.2.ax_ref
  30.6 0.0 collective-permute-done.1.hi_ref.first_hi_ref
  30.6 0.0 collective-permute-done.lo_ref.first_lo_ref
  30.6 0.6 shard_map.74
  31.2 6.3 %collective-permute-start.3 = (f32[5,16,384]{2,1,0:T(8,128)S(1)}, f32[5,16,384]{2,1,0:T(8,128)S(1)}, u32[]{:S(2)}, u32[]{:S(2)}) collective-permute-start(f32[5,16,384]{2,1,0:T(8,128)S(1)} %get-tuple-element.56), channel_id=1, source_target_pairs={{0,1},{1,0},{2,3},{3,2},{4,5},{5,4},{6,7},{7,6},{8,9},{9,8},{10,11... | collective-permute-start | bytes 368648 | tf_op jit(solution)/shard_map/ppermute | solution.py:357
  37.5 1.0 %collective-permute-done.3.recv = f32[5,16,384]{2,1,0:T(8,128)S(1)} collective-permute-done((f32[5,16,384]{2,1,0:T(8,128)S(1)}, f32[5,16,384]{2,1,0:T(8,128)S(1)}, u32[]{:S(2)}, u32[]{:S(2)}) %collective-permute-start.3) | collective-permute-done | bytes 122912 | tf_op jit(solution)/shard_map/ppermute | solution.py:357
  38.5 0.1 collective-permute-start.4
  38.6 4.5 %collective-permute-done.4.recv = f32[5,16,384]{2,1,0:T(8,128)S(1)} collective-permute-done((f32[5,16,384]{2,1,0:T(8,128)S(1)}, f32[5,16,384]{2,1,0:T(8,128)S(1)}, u32[]{:S(2)}, u32[]{:S(2)}) %collective-permute-start.4) | collective-permute-done | bytes 122912 | tf_op jit(solution)/shard_map/ppermute | solution.py:357
  43.2 0.1 collective-permute-start.5
  43.3 4.9 %collective-permute-done.5.recv = f32[5,16,384]{2,1,0:T(8,128)S(1)} collective-permute-done((f32[5,16,384]{2,1,0:T(8,128)S(1)}, f32[5,16,384]{2,1,0:T(8,128)S(1)}, u32[]{:S(2)}, u32[]{:S(2)}) %collective-permute-start.5) | collective-permute-done | bytes 122912 | tf_op jit(solution)/shard_map/ppermute | solution.py:357
  48.3 0.1 collective-permute-start.6
  48.4 3.7 %collective-permute-done.6.recv = f32[5,16,384]{2,1,0:T(8,128)S(1)} collective-permute-done((f32[5,16,384]{2,1,0:T(8,128)S(1)}, f32[5,16,384]{2,1,0:T(8,128)S(1)}, u32[]{:S(2)}, u32[]{:S(2)}) %collective-permute-start.6) | collective-permute-done | bytes 122912 | tf_op jit(solution)/shard_map/ppermute | solution.py:357
  52.2 0.5 collective-permute-start.7
  52.7 4.5 %collective-permute-done.7.refs_1_ = f32[5,16,384]{2,1,0:T(8,128)S(1)} collective-permute-done((f32[5,16,384]{2,1,0:T(8,128)S(1)}, f32[5,16,384]{2,1,0:T(8,128)S(1)}, u32[]{:S(2)}, u32[]{:S(2)}) %collective-permute-start.7) | collective-permute-done | bytes 122912 | tf_op jit(solution)/shard_map/ppermute | solution.py:357
  57.2 0.1 shard_map.79
  57.2 4.7 %collective-permute-start.8 = (f32[2,16,384]{2,1,0:T(8,128)S(1)}, f32[2,16,384]{2,1,0:T(8,128)S(1)}, u32[]{:S(2)}, u32[]{:S(2)}) collective-permute-start(f32[2,16,384]{2,1,0:T(8,128)S(1)} %get-tuple-element.70), channel_id=1, source_target_pairs={{0,1},{1,0},{2,3},{3,2},{4,5},{5,4},{6,7},{7,6},{8,9},{9,8},{10,11... | collective-permute-start | bytes 147464 | tf_op jit(solution)/shard_map/ppermute | solution.py:357
  62.0 0.9 collective-permute-done.8.other
  62.8 0.4 shard_map.80
  63.2 0.1 collective-permute-start.9
  63.3 2.7 %collective-permute-start.10 = (f32[32,384]{1,0:T(8,128)S(1)}, f32[32,384]{1,0:T(8,128)S(1)}, u32[]{:S(2)}, u32[]{:S(2)}) collective-permute-start(f32[32,384]{1,0:T(8,128)S(1)} %get-tuple-element.78), channel_id=1, source_target_pairs={{32,0},{64,32},{96,64},{0,96},{33,1},{65,33},{97,65},{1,97},{34,2}... | collective-permute-start | bytes 147464 | tf_op jit(solution)/shard_map/ppermute | solution.py:418
  66.0 1.4 %shard_map.81.part_ref = f32[32,32,384]{2,1,0:T(8,128)S(1)} custom-call(f32[2,16,384]{2,1,0:T(8,128)S(1)} %get-tuple-element.69.own, f32[2,16,384]{2,1,0:T(8,128)S(1)} %collective-permute-done.8.other, f32[2,32,8,384]{3,2,1,0:T(8,128)S(1)} %get-tuple-element.75.edge_ref, f32[32,32,384]{2,1,0:T(8,128)S(1)} %get-tuple-element.49.s_ref, ...), custom_call_target="tpu_custom_call" | custom-call | flops 6000000 | bytes 9000000 | tf_op jit(solution)/shard_map/pallas_call | solution.py:346
  67.4 0.1 collective-permute-done.9.lo_ref
  67.4 0.0 collective-permute-done.10.hi_ref
  67.4 0.5 shard_map.82
  68.0 1.6 %collective-permute-start.11 = (f32[2,16,384]{2,1,0:T(8,128)S(1)}, f32[2,16,384]{2,1,0:T(8,128)S(1)}, u32[]{:S(2)}, u32[]{:S(2)}) collective-permute-start(f32[2,16,384]{2,1,0:T(8,128)S(1)} %get-tuple-element.80), channel_id=1, source_target_pairs={{0,1},{1,0},{2,3},{3,2},{4,5},{5,4},{6,7},{7,6},{8,9},{9,8},{10,11... | collective-permute-start | bytes 147464 | tf_op jit(solution)/shard_map/ppermute | solution.py:357
  69.6 0.9 collective-permute-done.11.recv
  70.5 0.1 collective-permute-start.12
  70.6 2.9 %collective-permute-done.12.recv = f32[2,16,384]{2,1,0:T(8,128)S(1)} collective-permute-done((f32[2,16,384]{2,1,0:T(8,128)S(1)}, f32[2,16,384]{2,1,0:T(8,128)S(1)}, u32[]{:S(2)}, u32[]{:S(2)}) %collective-permute-start.12) | collective-permute-done | bytes 49184 | tf_op jit(solution)/shard_map/ppermute | solution.py:357
  73.5 0.1 collective-permute-start.13
  73.6 4.1 %collective-permute-done.13.recv = f32[2,16,384]{2,1,0:T(8,128)S(1)} collective-permute-done((f32[2,16,384]{2,1,0:T(8,128)S(1)}, f32[2,16,384]{2,1,0:T(8,128)S(1)}, u32[]{:S(2)}, u32[]{:S(2)}) %collective-permute-start.13) | collective-permute-done | bytes 49184 | tf_op jit(solution)/shard_map/ppermute | solution.py:357
  77.8 0.1 collective-permute-start.14
  77.9 2.9 %collective-permute-done.14.recv = f32[2,16,384]{2,1,0:T(8,128)S(1)} collective-permute-done((f32[2,16,384]{2,1,0:T(8,128)S(1)}, f32[2,16,384]{2,1,0:T(8,128)S(1)}, u32[]{:S(2)}, u32[]{:S(2)}) %collective-permute-start.14) | collective-permute-done | bytes 49184 | tf_op jit(solution)/shard_map/ppermute | solution.py:357
  80.8 0.5 collective-permute-start.15
  81.4 3.7 %collective-permute-done.15.refs_1_ = f32[2,16,384]{2,1,0:T(8,128)S(1)} collective-permute-done((f32[2,16,384]{2,1,0:T(8,128)S(1)}, f32[2,16,384]{2,1,0:T(8,128)S(1)}, u32[]{:S(2)}, u32[]{:S(2)}) %collective-permute-start.15) | collective-permute-done | bytes 49184 | tf_op jit(solution)/shard_map/ppermute | solution.py:357
  85.1 0.1 shard_map.87
  85.1 5.0 %collective-permute-start.16 = (f32[2,16,384]{2,1,0:T(8,128)S(1)}, f32[2,16,384]{2,1,0:T(8,128)S(1)}, u32[]{:S(2)}, u32[]{:S(2)}) collective-permute-start(f32[2,16,384]{2,1,0:T(8,128)S(1)} %get-tuple-element.91), channel_id=1, source_target_pairs={{0,1},{1,0},{2,3},{3,2},{4,5},{5,4},{6,7},{7,6},{8,9},{9,8},{10,11... | collective-permute-start | bytes 147464 | tf_op jit(solution)/shard_map/ppermute | solution.py:357
  90.2 0.9 collective-permute-done.16.other
  91.0 1.3 %shard_map.88 = f32[32,32,384]{2,1,0:T(8,128)} custom-call(f32[2,16,384]{2,1,0:T(8,128)S(1)} %get-tuple-element.90.own, f32[2,16,384]{2,1,0:T(8,128)S(1)} %collective-permute-done.16.other, f32[32,32,384]{2,1,0:T(8,128)S(1)} %get-tuple-element.50.g_ref, f32[32,32,384]{2,1,0:T(8,128)S(1)} %get-tuple-element.51.r_ref, ...), custom_call_target="tpu_custom_call" | custom-call | flops 2000000 | bytes 3000000 | tf_op jit(solution)/shard_map/pallas_call | solution.py:346
  (13 shorter events, 0.3 us)
Async XLA Ops:
  0.0 18.0 %copy-start = (f32[32,32,384]{2,1,0:T(8,128)S(1)}, f32[32,32,384]{2,1,0:T(8,128)}, u32[]{:S(2)}) copy-start(f32[32,32,384]{2,1,0:T(8,128)} %conc_hbm.1) | copy-start | bytes 4718596
  4.8 25.8 %collective-permute-start.2 = (f32[32,384]{1,0:T(8,128)S(1)}, f32[32,384]{1,0:T(8,128)S(1)}, u32[]{:S(2)}, u32[]{:S(2)}) collective-permute-start(f32[32,384]{1,0:T(8,128)S(1)} %sqrt_bitcast_fusion), channel_id=1, source_target_pairs={{1,0},{2,1},{3,2},{4,3},{5,4},{6,5},{7,6},{8,7},{9,8},{10,9},{11,1... | collective-permute-start | bytes 147464 | tf_op jit(solution)/shard_map/ppermute | solution.py:368
  12.7 17.9 %collective-permute-start.1 = (f32[2,32,384]{2,1,0:T(8,128)S(1)}, f32[2,32,384]{2,1,0:T(8,128)S(1)}, u32[]{:S(2)}, u32[]{:S(2)}) collective-permute-start(f32[2,32,384]{2,1,0:T(8,128)S(1)} %pad_maximum_fusion.2), channel_id=1, source_target_pairs={{32,0},{64,32},{96,64},{0,96},{33,1},{65,33},{97,65},{1,97},{34,2}... | collective-permute-start | bytes 294920 | tf_op jit(solution)/shard_map/ppermute | solution.py:367
  17.9 1.4 %copy-start.1 = (s32[32,32,384]{2,1,0:T(8,128)S(1)}, s32[32,32,384]{2,1,0:T(8,128)}, u32[]{:S(2)}) copy-start(s32[32,32,384]{2,1,0:T(8,128)} %mask_hbm.1) | copy-start | bytes 4718596
  17.9 1.9 %copy-start.2 = (s32[32,32,384]{2,1,0:T(8,128)S(1)}, s32[32,32,384]{2,1,0:T(8,128)}, u32[]{:S(2)}) copy-start(s32[32,32,384]{2,1,0:T(8,128)} %layer_hbm.1) | copy-start | bytes 4718596
  17.9 1.9 %copy-start.5 = (f32[4]{0:T(128)S(1)}, f32[4]{0:T(128)}, u32[]{:S(2)}) copy-start(f32[4]{0:T(128)} %diff_table.1) | copy-start | bytes 52
  17.9 1.9 %copy-start.6 = (f32[4]{0:T(128)S(1)}, f32[4]{0:T(128)}, u32[]{:S(2)}) copy-start(f32[4]{0:T(128)} %uptake_table.1) | copy-start | bytes 52
  17.9 12.7 %collective-permute-start = (f32[2,32,384]{2,1,0:T(8,128)S(1)}, f32[2,32,384]{2,1,0:T(8,128)S(1)}, u32[]{:S(2)}, u32[]{:S(2)}) collective-permute-start(f32[2,32,384]{2,1,0:T(8,128)S(1)} %pad_maximum_fusion.1), channel_id=1, source_target_pairs={{0,32},{32,64},{64,96},{96,0},{1,33},{33,65},{65,97},{97,1},{2,34}... | collective-permute-start | bytes 294920 | tf_op jit(solution)/shard_map/ppermute | solution.py:366
  19.8 1.4 %copy-start.3 = (f32[32,32,384]{2,1,0:T(8,128)S(1)}, f32[32,32,384]{2,1,0:T(8,128)}, u32[]{:S(2)}) copy-start(f32[32,32,384]{2,1,0:T(8,128)} %stiff_hbm.1) | copy-start | bytes 4718596
  21.2 1.4 %copy-start.4 = (f32[32,32,384]{2,1,0:T(8,128)S(1)}, f32[32,32,384]{2,1,0:T(8,128)}, u32[]{:S(2)}) copy-start(f32[32,32,384]{2,1,0:T(8,128)} %prod_hbm.1) | copy-start | bytes 4718596
  31.2 7.3 %collective-permute-start.3 = (f32[5,16,384]{2,1,0:T(8,128)S(1)}, f32[5,16,384]{2,1,0:T(8,128)S(1)}, u32[]{:S(2)}, u32[]{:S(2)}) collective-permute-start(f32[5,16,384]{2,1,0:T(8,128)S(1)} %get-tuple-element.56), channel_id=1, source_target_pairs={{0,1},{1,0},{2,3},{3,2},{4,5},{5,4},{6,7},{7,6},{8,9},{9,8},{10,11... | collective-permute-start | bytes 368648 | tf_op jit(solution)/shard_map/ppermute | solution.py:357
  38.5 4.6 %collective-permute-start.4 = (f32[5,16,384]{2,1,0:T(8,128)S(1)}, f32[5,16,384]{2,1,0:T(8,128)S(1)}, u32[]{:S(2)}, u32[]{:S(2)}) collective-permute-start(f32[5,16,384]{2,1,0:T(8,128)S(1)} %get-tuple-element.57.mine), channel_id=1, source_target_pairs={{0,2},{1,3},{2,0},{3,1},{4,6},{5,7},{6,4},{7,5},{8,10},{9,11},{10,... | collective-permute-start | bytes 368648 | tf_op jit(solution)/shard_map/ppermute | solution.py:357
  43.2 5.0 %collective-permute-start.5 = (f32[5,16,384]{2,1,0:T(8,128)S(1)}, f32[5,16,384]{2,1,0:T(8,128)S(1)}, u32[]{:S(2)}, u32[]{:S(2)}) collective-permute-start(f32[5,16,384]{2,1,0:T(8,128)S(1)} %get-tuple-element.58.mine), channel_id=1, source_target_pairs={{0,6},{1,7},{2,4},{3,5},{4,2},{5,3},{6,0},{7,1},{8,14},{9,15},{10,... | collective-permute-start | bytes 368648 | tf_op jit(solution)/shard_map/ppermute | solution.py:357
  48.3 3.8 %collective-permute-start.6 = (f32[5,16,384]{2,1,0:T(8,128)S(1)}, f32[5,16,384]{2,1,0:T(8,128)S(1)}, u32[]{:S(2)}, u32[]{:S(2)}) collective-permute-start(f32[5,16,384]{2,1,0:T(8,128)S(1)} %get-tuple-element.59.mine), channel_id=1, source_target_pairs={{0,8},{1,9},{2,10},{3,11},{4,12},{5,13},{6,14},{7,15},{8,0},{9,1},... | collective-permute-start | bytes 368648 | tf_op jit(solution)/shard_map/ppermute | solution.py:357
  52.2 5.0 %collective-permute-start.7 = (f32[5,16,384]{2,1,0:T(8,128)S(1)}, f32[5,16,384]{2,1,0:T(8,128)S(1)}, u32[]{:S(2)}, u32[]{:S(2)}) collective-permute-start(f32[5,16,384]{2,1,0:T(8,128)S(1)} %get-tuple-element.60.refs_0_), channel_id=1, source_target_pairs={{0,24},{1,25},{2,26},{3,27},{4,28},{5,29},{6,30},{7,31},{8,16},{9,... | collective-permute-start | bytes 368648 | tf_op jit(solution)/shard_map/ppermute | solution.py:357
  57.2 5.6 %collective-permute-start.8 = (f32[2,16,384]{2,1,0:T(8,128)S(1)}, f32[2,16,384]{2,1,0:T(8,128)S(1)}, u32[]{:S(2)}, u32[]{:S(2)}) collective-permute-start(f32[2,16,384]{2,1,0:T(8,128)S(1)} %get-tuple-element.70), channel_id=1, source_target_pairs={{0,1},{1,0},{2,3},{3,2},{4,5},{5,4},{6,7},{7,6},{8,9},{9,8},{10,11... | collective-permute-start | bytes 147464 | tf_op jit(solution)/shard_map/ppermute | solution.py:357
  63.2 4.2 %collective-permute-start.9 = (f32[32,384]{1,0:T(8,128)S(1)}, f32[32,384]{1,0:T(8,128)S(1)}, u32[]{:S(2)}, u32[]{:S(2)}) collective-permute-start(f32[32,384]{1,0:T(8,128)S(1)} %get-tuple-element.77), channel_id=1, source_target_pairs={{0,32},{32,64},{64,96},{96,0},{1,33},{33,65},{65,97},{97,1},{2,34}... | collective-permute-start | bytes 147464 | tf_op jit(solution)/shard_map/ppermute | solution.py:417
  63.3 4.1 %collective-permute-start.10 = (f32[32,384]{1,0:T(8,128)S(1)}, f32[32,384]{1,0:T(8,128)S(1)}, u32[]{:S(2)}, u32[]{:S(2)}) collective-permute-start(f32[32,384]{1,0:T(8,128)S(1)} %get-tuple-element.78), channel_id=1, source_target_pairs={{32,0},{64,32},{96,64},{0,96},{33,1},{65,33},{97,65},{1,97},{34,2}... | collective-permute-start | bytes 147464 | tf_op jit(solution)/shard_map/ppermute | solution.py:418
  68.0 2.5 %collective-permute-start.11 = (f32[2,16,384]{2,1,0:T(8,128)S(1)}, f32[2,16,384]{2,1,0:T(8,128)S(1)}, u32[]{:S(2)}, u32[]{:S(2)}) collective-permute-start(f32[2,16,384]{2,1,0:T(8,128)S(1)} %get-tuple-element.80), channel_id=1, source_target_pairs={{0,1},{1,0},{2,3},{3,2},{4,5},{5,4},{6,7},{7,6},{8,9},{9,8},{10,11... | collective-permute-start | bytes 147464 | tf_op jit(solution)/shard_map/ppermute | solution.py:357
  70.5 3.0 %collective-permute-start.12 = (f32[2,16,384]{2,1,0:T(8,128)S(1)}, f32[2,16,384]{2,1,0:T(8,128)S(1)}, u32[]{:S(2)}, u32[]{:S(2)}) collective-permute-start(f32[2,16,384]{2,1,0:T(8,128)S(1)} %get-tuple-element.81.mine), channel_id=1, source_target_pairs={{0,2},{1,3},{2,0},{3,1},{4,6},{5,7},{6,4},{7,5},{8,10},{9,11},{10,... | collective-permute-start | bytes 147464 | tf_op jit(solution)/shard_map/ppermute | solution.py:357
  73.5 4.2 %collective-permute-start.13 = (f32[2,16,384]{2,1,0:T(8,128)S(1)}, f32[2,16,384]{2,1,0:T(8,128)S(1)}, u32[]{:S(2)}, u32[]{:S(2)}) collective-permute-start(f32[2,16,384]{2,1,0:T(8,128)S(1)} %get-tuple-element.82.mine), channel_id=1, source_target_pairs={{0,6},{1,7},{2,4},{3,5},{4,2},{5,3},{6,0},{7,1},{8,14},{9,15},{10,... | collective-permute-start | bytes 147464 | tf_op jit(solution)/shard_map/ppermute | solution.py:357
  77.8 3.0 %collective-permute-start.14 = (f32[2,16,384]{2,1,0:T(8,128)S(1)}, f32[2,16,384]{2,1,0:T(8,128)S(1)}, u32[]{:S(2)}, u32[]{:S(2)}) collective-permute-start(f32[2,16,384]{2,1,0:T(8,128)S(1)} %get-tuple-element.83.mine), channel_id=1, source_target_pairs={{0,8},{1,9},{2,10},{3,11},{4,12},{5,13},{6,14},{7,15},{8,0},{9,1},... | collective-permute-start | bytes 147464 | tf_op jit(solution)/shard_map/ppermute | solution.py:357
  80.8 4.2 %collective-permute-start.15 = (f32[2,16,384]{2,1,0:T(8,128)S(1)}, f32[2,16,384]{2,1,0:T(8,128)S(1)}, u32[]{:S(2)}, u32[]{:S(2)}) collective-permute-start(f32[2,16,384]{2,1,0:T(8,128)S(1)} %get-tuple-element.84.refs_0_), channel_id=1, source_target_pairs={{0,24},{1,25},{2,26},{3,27},{4,28},{5,29},{6,30},{7,31},{8,16},{9,... | collective-permute-start | bytes 147464 | tf_op jit(solution)/shard_map/ppermute | solution.py:357
  85.1 5.9 %collective-permute-start.16 = (f32[2,16,384]{2,1,0:T(8,128)S(1)}, f32[2,16,384]{2,1,0:T(8,128)S(1)}, u32[]{:S(2)}, u32[]{:S(2)}) collective-permute-start(f32[2,16,384]{2,1,0:T(8,128)S(1)} %get-tuple-element.91), channel_id=1, source_target_pairs={{0,1},{1,0},{2,3},{3,2},{4,5},{5,4},{6,7},{7,6},{8,9},{9,8},{10,11... | collective-permute-start | bytes 147464 | tf_op jit(solution)/shard_map/ppermute | solution.py:357
where the time goes:
time: 92.8 us; the launch traced here: 92.4 us
  waiting for transfers between devices  35 us (38%)
  starting transfers between devices  26.1 us (28%)
  Pallas kernels  12.6 us (14%)
  local copies, waits for them, and re-layouts  9.84 us (11%)
  other arithmetic  8.43 us (9%)
    ppermute x12, waiting for transfers between devices, exchange(): return lax.ppermute(block, 'ax', partners[level])  35 us
    ppermute x12, starting transfers between devices, exchange(): return lax.ppermute(block, 'ax', partners[level])  19.2 us
    pallas_call x16, Pallas kernels, call(): pl.pallas_call(kernel, out_shape=outs, in_specs=specs or [vspec()] * len(...  12.6 us
    sqrt x3, other arithmetic, edge_diffusivity(): return jnp.sqrt(mask.astype(jnp.float32) * lookup(layer, table) * stiff)  8.36 us
    unnamed x16, local copies, waits for them, and re-layouts  4.47 us
    ppermute x1, starting transfers between devices, on_device(): from_hi = lax.ppermute(lo, 'xs', downward)  2.66 us
    ppermute x1, starting transfers between devices, on_device(): halo_hi = lax.ppermute(side(0), 'xs', downward)  2.63 us
  transfers between devices with their start and end apart: 17, of which 13 were waited for; matrix products, arithmetic and copies ran while one was open for 10% of the time, Pallas kernels for 10%

commit v1 on v0

v1 whole, which is shorter than its diff:
```python
import functools

import jax
import jax.numpy as jnp
from jax import lax
from jax.experimental import pallas as pl
from jax.experimental.pallas import tpu as pltpu
from jax.sharding import PartitionSpec as P

RZ = 3072.0
SECTION_RATE = 0.05
LAYERS = 4
LIMIT = 20 * 1024 * 1024
CHUNK = 8


def at_vmem(*shape):
    return pltpu.VMEM(shape, jnp.float32)


def vspec():
    return pl.BlockSpec(memory_space=pltpu.VMEM)


def params():
    return pltpu.CompilerParams(vmem_limit_bytes=LIMIT)


def cost(us):
    return pl.CostEstimate(flops=int(us * 2e6), bytes_accessed=int(us * 3e6), transcendentals=0)


def lookup(labels, table):
    summed = jnp.where(labels == 0, table[0], 0.0)
    for layer in range(1, LAYERS):
        summed = jnp.where(labels == layer, table[layer], summed)
    return summed


def tiles_of(ref, z, slab, cols):
    return [[ref[z, t:t + 8, c:c + 128] for c in range(0, cols, 128)] for t in range(0, slab, 8)]


def neighbour_sum(tiles):
    rows, cols = len(tiles), len(tiles[0])
    row = lax.broadcasted_iota(jnp.int32, (8, 128), 0)
    lane = lax.broadcasted_iota(jnp.int32, (8, 128), 1)

    def rolled(shift, axis):
        return [[pltpu.roll(tile, shift, axis) for tile in line] for line in tiles]

    down, up, right, left = rolled(1, 0), rolled(7, 0), rolled(1, 1), rolled(127, 1)

    def at(array, t, c):
        return array[t][c] if 0 <= t < rows and 0 <= c < cols else 0.0

    return [[
        (jnp.where(row == 0, at(down, t - 1, c), down[t][c]) + jnp.where(row == 7, at(up, t + 1, c), up[t][c]))
        + (jnp.where(lane == 0, at(right, t, c - 1), right[t][c])
           + jnp.where(lane == 127, at(left, t, c + 1), left[t][c]))
        for c in range(cols)] for t in range(rows)]


def inverse(x):
    r = pl.reciprocal(x, approx=True)
    r = r * (2.0 - x * r)
    return r * (2.0 - x * r)


def edge_kernel(
    rows, slab,
    table, conc_hbm, mask_hbm, layer_hbm, stiff_hbm,
    lo_out, hi_out, first_out, conc_edges,
    mask, layer, stiff, mask_row, layer_row, stiff_row, sems,
):
    copies = []
    for side in (0, 1):
        here = pl.ds(0 if side == 0 else slab - 8, 8)
        for k, (source, target) in enumerate(
                ((mask_hbm, mask), (layer_hbm, layer), (stiff_hbm, stiff), (conc_hbm, conc_edges))):
            copies.append(pltpu.make_async_copy(source.at[:, here], target.at[side], sems.at[side, k]))
    rowcopies = []
    for k, (source, target) in enumerate(((mask_hbm, mask_row), (layer_hbm, layer_row), (stiff_hbm, stiff_row))):
        rowcopies.append(pltpu.make_async_copy(source.at[0], target, sems.at[2, k]))
    for copy in copies + rowcopies:
        copy.start()
    tab = [table[k] for k in range(LAYERS)]
    for side, out in ((0, lo_out), (1, hi_out)):
        for copy in copies[4 * side:4 * side + 4]:
            copy.wait()
        keep = slice(0, 1) if side == 0 else slice(7, 8)
        for z in range(rows):
            s = root(mask[side, z].astype(jnp.float32) * lookup(layer[side, z], tab) * stiff[side, z])
            out[0, z:z + 1] = s[keep]
            out[1, z:z + 1] = conc_edges[side, z][keep]
    for copy in rowcopies:
        copy.wait()
    first_out[...] = root(mask_row[...].astype(jnp.float32) * lookup(layer_row[...], tab) * stiff_row[...])


def root(x):
    return jnp.sqrt(x)


def setup_kernel(
    rows, slab, cols,
    table, conc_hbm, mask_hbm, layer_hbm, stiff_hbm,
    s_out, g_out, r_out, gp_out, ssum_out, part_out, ends_out,
    conc, mask, layer, stiff, sems,
):
    pairs = ((mask_hbm, mask), (layer_hbm, layer), (stiff_hbm, stiff), (conc_hbm, conc))
    copies = []
    for chunk in range(rows // CHUNK):
        here = pl.ds(chunk * CHUNK, CHUNK)
        copies.append([
            pltpu.make_async_copy(source.at[here], target.at[here], sems.at[k, chunk])
            for k, (source, target) in enumerate(pairs)
        ])
    for group in copies:
        for copy in group:
            copy.start()
    tab = [table[k] for k in range(LAYERS)]
    grid = [(t, c) for t in range(slab // 8) for c in range(cols // 128)]
    s = m = gp = alpha = None
    for z in range(rows):
        if z % CHUNK == 0:
            for copy in copies[z // CHUNK]:
                copy.wait()
        w, lab, sti, st = [tiles_of(ref, z, slab, cols) for ref in (mask, layer, stiff, conc)]
        s_next = [[root(w[t][c].astype(jnp.float32) * lookup(lab[t][c], tab) * sti[t][c])
                   for c in range(cols // 128)] for t in range(slab // 8)]
        flow = [[s_next[t][c] * st[t][c] for c in range(cols // 128)] for t in range(slab // 8)]
        ssum, vsum = neighbour_sum(s_next), neighbour_sum(flow)
        for t, c in grid:
            here = (z, pl.ds(8 * t, 8), pl.ds(128 * c, 128))
            s_out[here] = s_next[t][c]
            ssum_out[here] = ssum[t][c]
            part_out[here] = st[t][c] + SECTION_RATE * s_next[t][c] * (vsum[t][c] - st[t][c] * ssum[t][c])
        if z == 0:
            ones = {k: jnp.ones((8, 128), jnp.float32) for k in grid}
            m, gp, alpha = dict(ones), dict(ones), {k: jnp.zeros((8, 128), jnp.float32) for k in grid}
        else:
            for t, c in grid:
                k = (t, c)
                here = (z - 1, pl.ds(8 * t, 8), pl.ds(128 * c, 128))
                couple = RZ * s[t][c] * s_next[t][c]
                r = inverse(m[k] + couple)
                g = couple * r
                r_out[here] = r
                g_out[here] = g
                gp_out[here] = gp[k]
                alpha[k] = alpha[k] + r * gp[k] * gp[k]
                m[k] = 1.0 + g * m[k]
                gp[k] = gp[k] * g
        s = s_next
    for t, c in grid:
        here = (pl.ds(8 * t, 8), pl.ds(128 * c, 128))
        gp_out[(rows - 1,) + here] = gp[t, c]
        ends_out[(0,) + here] = m[t, c]
        ends_out[(1,) + here] = alpha[t, c]


def reaction_kernel(rows, uptake_table, mask_hbm, layer_hbm, prod_hbm, keep_out, source_out, mask, layer, prod, sems):
    copies = []
    for chunk in range(rows // CHUNK):
        here = pl.ds(chunk * CHUNK, CHUNK)
        copies.append([
            pltpu.make_async_copy(source.at[here], target.at[here], sems.at[k, chunk])
            for k, (source, target) in enumerate(((mask_hbm, mask), (layer_hbm, layer), (prod_hbm, prod)))
        ])
    for group in copies:
        for copy in group:
            copy.start()
    tab = [uptake_table[k] for k in range(LAYERS)]
    for z in range(rows):
        if z % CHUNK == 0:
            for copy in copies[z // CHUNK]:
                copy.wait()
        weight = mask[z].astype(jnp.float32)
        keep_out[z] = 1.0 - weight * lookup(layer[z], tab)
        source_out[z] = weight * prod[z]


def forward_sweep(rows, slab, first_step, ix, nx, state_ref, s_ref, g_ref, r_ref, gp_ref, part_ref, lo_ref, hi_ref,
                  shalo_lo, shalo_hi, last_g, last_r, fwd_ref):
    row = lax.broadcasted_iota(jnp.int32, (8, lo_ref.shape[-1]), 0)
    top = jnp.where(row == 0, jnp.where(ix > 0, SECTION_RATE, 0.0), 0.0)
    bottom = jnp.where(row == 7, jnp.where(ix < nx - 1, SECTION_RATE, 0.0), 0.0)
    total = None
    prev = None
    for z in range(rows):
        st_lo, st_hi = state_ref(z, 0), state_ref(z, 1)
        s_lo, s_hi = s_ref[z, 0:8], s_ref[z, slab - 8:slab]
        sl, sh = shalo_lo[z:z + 1], shalo_hi[z:z + 1]
        vl, vh = lo_ref[z:z + 1], hi_ref[z:z + 1]
        if first_step:
            vl, vh = vl * sl, vh * sh
        extra_lo = top * s_lo * (vl - st_lo * sl)
        extra_hi = bottom * s_hi * (vh - st_hi * sh)
        part = part_ref[z]
        e = jnp.concatenate([part[0:8] + extra_lo, part[8:slab - 8], part[slab - 8:] + extra_hi], axis=0)
        if z > 0:
            e = e + g_ref[z - 1] * prev
        fwd_ref[z] = e
        r = r_ref[z] if z < rows - 1 else last_r
        term = gp_ref[z] * r * e
        total = term if z == 0 else total + term
        prev = e
    return total, last_g * prev


def first_forward_kernel(
    rows, slab, nx, nax,
    conc_ref, s_ref, g_ref, r_ref, gp_ref, part_ref, ends_ref, lo_ref, hi_ref, ax_ref,
    fwd_ref, last_ref, mine_ref, send_ref, ports_ref,
):
    ix, ia = lax.axis_index("xs"), lax.axis_index("ax")
    above = jnp.where(ia < nax - 1, RZ, 0.0)
    c = above * s_ref[rows - 1] * ax_ref[...]
    m, alpha = ends_ref[0], ends_ref[1]
    last_r = 1.0 / (m + c)
    last_g = c * last_r
    gp = gp_ref[rows - 1]
    last_ref[0] = last_g
    last_ref[1] = last_r
    a, b = forward_sweep(
        rows, slab, True, ix, nx, lambda z, side: conc_ref[side, z], s_ref, g_ref, r_ref, gp_ref, part_ref,
        lo_ref.at[1], hi_ref.at[1], lo_ref.at[0], hi_ref.at[0], last_g, last_r, fwd_ref)
    ports_ref[0] = a
    ports_ref[1] = b
    ports_ref[2] = alpha + last_r * gp * gp
    ports_ref[3] = last_g * gp
    ports_ref[4] = last_g * m
    split_ports(slab, ports_ref, mine_ref, send_ref)


def second_forward_kernel(
    rows, slab, nx,
    edge_ref, s_ref, g_ref, r_ref, gp_ref, part_ref, last_ref, first_lo_ref, first_hi_ref, lo_ref, hi_ref,
    fwd_ref, mine_ref, send_ref, ports_ref,
):
    ix, ia = lax.axis_index("xs"), lax.axis_index("ax")
    a, b = forward_sweep(
        rows, slab, False, ix, nx, lambda z, side: edge_ref[side, z], s_ref, g_ref, r_ref, gp_ref, part_ref,
        lo_ref, hi_ref, first_lo_ref.at[0], first_hi_ref.at[0], last_ref[0], last_ref[1], fwd_ref)
    ports_ref[0] = a
    ports_ref[1] = b
    split_ports(slab, ports_ref, mine_ref, send_ref)


def place():
    i = lax.axis_index("ax")
    core, z, y = lax.rem(i, 2), lax.rem(lax.div(i, 2), 4), lax.div(i, 8)
    return core, z, y, lax.rem(core + z + y, 2)


def split_ports(slab, ports_ref, mine_ref, send_ref):
    half = slab // 2
    own = place()[3]
    mine_ref[...] = ports_ref[:, pl.ds(pl.multiple_of(own * half, half), half)]
    send_ref[...] = ports_ref[:, pl.ds(pl.multiple_of((1 - own) * half, half), half)]


def pick(index, options):
    value = options[0]
    for k in range(1, len(options)):
        value = jnp.where(index == k, options[k], value)
    return value


def ordered(index, mine, received):
    return [pick(index ^ j, [mine] + received) for j in range(1 + len(received))]


JOIN_COEFS = 9


def join_coefs(low, high, lev, at):
    (alpha1, beta1, kappa1), (alpha2, beta2, kappa2) = low, high
    rho = inverse(1.0 + kappa1 * alpha2)
    x, y = beta1 * rho, beta2 * rho
    ax, ky = alpha2 * x, kappa1 * y
    for k, value in enumerate((rho, kappa1, alpha2, beta1, beta2, x, y, ax, ky)):
        lev[at * JOIN_COEFS + k] = value
    return alpha1 + beta1 * ax, x * beta2, kappa2 + beta2 * ky


def join_rhs(low, high, lev, at, values):
    (a1, b1), (a2, b2) = low, high
    rho, kappa1, alpha2, beta1, beta2 = [lev[at * JOIN_COEFS + k] for k in range(5)]
    u0 = rho * (a2 + alpha2 * b1)
    q0 = rho * (b1 - kappa1 * a2)
    values[2 * at] = u0
    values[2 * at + 1] = q0
    return a1 + beta1 * u0, b2 + beta2 * q0


def join_all(groups, join):
    if len(groups) == 2:
        return join(groups[0], groups[1], 0)
    return join(join(groups[0], groups[1], 0), join(groups[2], groups[3], 1), 2)


def stage_coefs(index, mine, received, lev):
    planes = [ordered(index, mine[k], [r[k] for r in received]) for k in (2, 3, 4)]
    return join_all(list(zip(*planes)), lambda low, high, at: join_coefs(low, high, lev, at))


def stage_rhs(index, mine, received, lev, values):
    planes = [ordered(index, mine[k], [r[k] for r in received]) for k in (0, 1)]
    return join_all(list(zip(*planes)), lambda low, high, at: join_rhs(low, high, lev, at, values))


def stage_index(stage):
    return place()[stage]


def first_join_kernel(stage, count, mine, *refs):
    received, (out, lev, values) = refs[:count], refs[count:]
    index = stage_index(stage)
    out[2], out[3], out[4] = stage_coefs(index, mine, received, lev)
    out[0], out[1] = stage_rhs(index, mine, received, lev, values)


def second_join_kernel(stage, count, mine, *refs):
    received, (lev, out, values) = refs[:count], refs[count:]
    out[0], out[1] = stage_rhs(stage_index(stage), mine, received, lev, values)


def inside(lev, values, at, q, top):
    x, y, ax, ky = [pick(at[0], [lev[j * JOIN_COEFS + k] for j in at[1]]) for k in (5, 6, 7, 8)]
    u0, q0 = [pick(at[0], [values[2 * j + k] for j in at[1]]) for k in (0, 1)]
    if q is None:
        return u0, q0
    return u0 + y * top + ax * q, q0 + x * q - ky * top


def descend(levs, values, mine_out, send_out):
    core, z, y, _ = place()
    q = top = None
    for stage, index in ((2, y), (1, z)):
        lev, value = levs[stage], values[stage]
        mid_top, mid_q = inside(lev, value, (0, (2,)), q, top)
        if q is None:
            q = top = jnp.zeros_like(mid_q)
        high = index >= 2
        q, top = jnp.where(high, mid_q, q), jnp.where(high, top, mid_top)
        mid_top, mid_q = inside(lev, value, (lax.div(index, 2), (0, 1)), q, top)
        odd = lax.rem(index, 2) == 1
        q, top = jnp.where(odd, mid_q, q), jnp.where(odd, top, mid_top)
    mid_top, mid_q = inside(levs[0], values[0], (0, (0,)), q, top)
    upper = core == 1
    mine_out[0], mine_out[1] = jnp.where(upper, mid_q, q), jnp.where(upper, top, mid_top)
    send_out[0], send_out[1] = jnp.where(upper, q, mid_q), jnp.where(upper, mid_top, top)


def first_last_kernel(count, mine, *refs):
    received = refs[:count]
    lev0, lev1, val0, val1, mine_out, send_out, lev2, val2 = refs[count:]
    index = stage_index(2)
    stage_coefs(index, mine, received, lev2)
    stage_rhs(index, mine, received, lev2, val2)
    descend((lev0, lev1, lev2), (val0, val1, val2), mine_out, send_out)


def second_last_kernel(count, mine, *refs):
    received = refs[:count]
    lev0, lev1, lev2, val0, val1, mine_out, send_out, val2 = refs[count:]
    stage_rhs(stage_index(2), mine, received, lev2, val2)
    descend((lev0, lev1, lev2), (val0, val1, val2), mine_out, send_out)


def whole_ports(own, other):
    second = place()[3] == 1
    planes = []
    for k in (0, 1):
        low, high = jnp.where(second, other[k], own[k]), jnp.where(second, own[k], other[k])
        planes.append(jnp.concatenate([low, high], axis=0))
    return planes


def edge_state_kernel(
    rows, slab,
    own, other, s_ref, g_ref, r_ref, gp_ref, fwd_ref, last_ref, keep_ref, source_ref,
    edge_ref, lo_ref, hi_ref,
):
    q, top = whole_ports(own, other)
    for side in (0, 1):
        at = slice(0, 8) if side == 0 else slice(slab - 8, slab)
        u, inflow = top[at], q[at]
        for z in range(rows - 1, -1, -1):
            r = r_ref[z, at] if z < rows - 1 else last_ref[1, at]
            g = g_ref[z, at] if z < rows - 1 else last_ref[0, at]
            u = r * (fwd_ref[z, at] + gp_ref[z, at] * inflow) + g * u
            state = source_ref[z, at] + keep_ref[z, at] * u
            edge_ref[side, z] = state
            flow = s_ref[z, at] * state
            if side == 0:
                lo_ref[z:z + 1] = flow[0:1]
            else:
                hi_ref[z:z + 1] = flow[7:8]


def middle_state_kernel(
    rows, slab, cols,
    own, other, edge_ref, s_ref, g_ref, r_ref, gp_ref, fwd_ref, last_ref, keep_ref, source_ref, ssum_ref,
    part_ref,
):
    q, top = whole_ports(own, other)
    at = slice(8, slab - 8)
    u, inflow = top[at], q[at]
    for z in range(rows - 1, -1, -1):
        r = r_ref[z, at] if z < rows - 1 else last_ref[1, at]
        g = g_ref[z, at] if z < rows - 1 else last_ref[0, at]
        u = r * (fwd_ref[z, at] + gp_ref[z, at] * inflow) + g * u
        middle = source_ref[z, at] + keep_ref[z, at] * u
        planes = [edge_ref[0, z]] + [middle[t:t + 8] for t in range(0, slab - 16, 8)] + [edge_ref[1, z]]
        state = [[plane[:, c:c + 128] for c in range(0, cols, 128)] for plane in planes]
        s, ssum = tiles_of(s_ref, z, slab, cols), tiles_of(ssum_ref, z, slab, cols)
        vsum = neighbour_sum([[x * y for x, y in zip(*lines)] for lines in zip(s, state)])
        for t in range(slab // 8):
            for c in range(cols // 128):
                part_ref[z, 8 * t:8 * t + 8, 128 * c:128 * c + 128] = state[t][c] + SECTION_RATE * s[t][c] * (
                    vsum[t][c] - state[t][c] * ssum[t][c])


def final_kernel(
    rows, slab,
    own, other, g_ref, r_ref, gp_ref, fwd_ref, last_ref, keep_ref, source_ref,
    out_hbm, out, sems,
):
    q, u = whole_ports(own, other)
    copies = []
    for z in range(rows - 1, -1, -1):
        r = r_ref[z] if z < rows - 1 else last_ref[1]
        g = g_ref[z] if z < rows - 1 else last_ref[0]
        u = r * (fwd_ref[z] + gp_ref[z] * q) + g * u
        out[z] = source_ref[z] + keep_ref[z] * u
        if z % CHUNK == 0:
            here = pl.ds(z, CHUNK)
            copy = pltpu.make_async_copy(out.at[here], out_hbm.at[here], sems.at[z // CHUNK])
            copy.start()
            copies.append(copy)
    for copy in copies:
        copy.wait()


def on_device(partners, concentration, tissue_mask, wall_layer, stiffness, production, layer_diffusivity, uptake_rate):
    rows, slab, cols = concentration.shape
    half = slab // 2
    nx, nax = lax.axis_size("xs"), lax.axis_size("ax")
    block, edge = (rows, slab, cols), (2, rows, 8, cols)
    smem = pl.BlockSpec(memory_space=pltpu.SMEM)
    hbm = pl.BlockSpec(memory_space=pltpu.HBM)

    def in_hbm(x):
        return pltpu.with_memory_space_constraint(x, pltpu.HBM)

    def call(kernel, outs, operands, scratch=(), specs=None, out_specs=None, us=1.0):
        return pl.pallas_call(
            kernel,
            out_shape=outs,
            in_specs=specs or [vspec()] * len(operands),
            out_specs=out_specs or [vspec()] * len(outs),
            scratch_shapes=list(scratch),
            compiler_params=params(),
            cost_estimate=cost(us),
        )(*operands)

    def exchange(block, stage):
        return [lax.ppermute(block, "ax", route) for route in partners[stage]]

    def f32(*shape):
        return pltpu.VMEM(shape, jnp.float32)

    def i32(*shape):
        return pltpu.VMEM(shape, jnp.int32)

    conc, mask, layer, stiff, prod = [
        in_hbm(x) for x in (concentration, tissue_mask, wall_layer, stiffness, production)]
    lo, hi, first_s, conc_edges = call(
        functools.partial(edge_kernel, rows, slab),
        [at_vmem(2, rows, cols), at_vmem(2, rows, cols), at_vmem(slab, cols), at_vmem(*edge)],
        [layer_diffusivity, conc, mask, layer, stiff],
        scratch=[i32(*edge), i32(*edge), f32(*edge), i32(slab, cols), i32(slab, cols), f32(slab, cols),
                 pltpu.SemaphoreType.DMA((3, 4))],
        specs=[smem] + [hbm] * 4,
    )
    upward = [(i, (i + 1) % nx) for i in range(nx)]
    downward = [((i + 1) % nx, i) for i in range(nx)]
    halo_lo = lax.ppermute(hi, "xs", upward)
    halo_hi = lax.ppermute(lo, "xs", downward)
    above_s = lax.ppermute(first_s, "ax", [((i + 1) % nax, i) for i in range(nax)])

    s, g, r, gp, ssum, part, ends = call(
        functools.partial(setup_kernel, rows, slab, cols),
        [at_vmem(*block)] * 6 + [at_vmem(2, slab, cols)],
        [layer_diffusivity, conc, mask, layer, stiff],
        scratch=[f32(*block), i32(*block), i32(*block), f32(*block), pltpu.SemaphoreType.DMA((4, rows // CHUNK))],
        specs=[smem] + [hbm] * 4,
        us=5.0,
    )
    fwd, last, mine, send = call(
        functools.partial(first_forward_kernel, rows, slab, nx, nax),
        [at_vmem(*block), at_vmem(2, slab, cols), at_vmem(5, half, cols), at_vmem(5, half, cols)],
        [conc_edges, s, g, r, gp, part, ends, halo_lo, halo_hi, above_s],
        scratch=[f32(5, slab, cols)],
    )

    levs, values = [], []
    for stage in (0, 1):
        received = exchange(mine if stage else send, stage)
        joins = len(received)
        if stage == 1:
            uptake_late, mine = lax.optimization_barrier((uptake_rate, mine))
            keep, source = call(
                functools.partial(reaction_kernel, rows),
                [at_vmem(*block)] * 2,
                [uptake_late, mask, layer, prod],
                scratch=[i32(*block), i32(*block), f32(*block), pltpu.SemaphoreType.DMA((3, rows // CHUNK))],
                specs=[smem] + [hbm] * 3,
                us=2.0,
            )
            mine, keep, source = lax.optimization_barrier((mine, keep, source))
        mine, lev, value = call(
            functools.partial(first_join_kernel, stage, joins),
            [at_vmem(5, half, cols), at_vmem(JOIN_COEFS * joins, half, cols), at_vmem(2 * joins, half, cols)],
            [mine, *received],
        )
        levs.append(lev)
        values.append(value)
    received = exchange(mine, 2)
    joins = len(received)
    own, send, lev = call(
        functools.partial(first_last_kernel, joins),
        [at_vmem(2, half, cols), at_vmem(2, half, cols), at_vmem(JOIN_COEFS * joins, half, cols)],
        [mine, *received, *levs, *values],
        scratch=[f32(2 * joins, half, cols)],
    )
    levs.append(lev)
    (other,) = exchange(send, 0)

    edges, lo, hi = call(
        functools.partial(edge_state_kernel, rows, slab),
        [at_vmem(*edge), at_vmem(rows, cols), at_vmem(rows, cols)],
        [own, other, s, g, r, gp, fwd, last, keep, source],
    )
    from_lo = lax.ppermute(hi, "xs", upward)
    from_hi = lax.ppermute(lo, "xs", downward)
    (part,) = call(
        functools.partial(middle_state_kernel, rows, slab, cols),
        [at_vmem(*block)],
        [own, other, edges, s, g, r, gp, fwd, last, keep, source, ssum],
        us=3.0,
    )
    fwd, mine, send = call(
        functools.partial(second_forward_kernel, rows, slab, nx),
        [at_vmem(*block), at_vmem(2, half, cols), at_vmem(2, half, cols)],
        [edges, s, g, r, gp, part, last, halo_lo, halo_hi, from_lo, from_hi],
        scratch=[f32(2, slab, cols)],
    )
    values = []
    for stage in (0, 1):
        received = exchange(mine if stage else send, stage)
        joins = len(received)
        mine, value = call(
            functools.partial(second_join_kernel, stage, joins),
            [at_vmem(2, half, cols), at_vmem(2 * joins, half, cols)],
            [mine, *received, levs[stage]],
        )
        values.append(value)
    received = exchange(mine, 2)
    joins = len(received)
    own, send = call(
        functools.partial(second_last_kernel, joins),
        [at_vmem(2, half, cols), at_vmem(2, half, cols)],
        [mine, *received, *levs, *values],
        scratch=[f32(2 * joins, half, cols)],
    )
    (other,) = exchange(send, 0)
    (out,) = call(
        functools.partial(final_kernel, rows, slab),
        [jax.ShapeDtypeStruct(block, jnp.float32)],
        [own, other, g, r, gp, fwd, last, keep, source],
        scratch=[f32(*block), pltpu.SemaphoreType.DMA((rows // CHUNK,))],
        out_specs=[hbm],
    )
    return out


def join_partners():
    stages = (
        (lambda y, z, c: (y, z, 1 - c),),
        tuple(lambda y, z, c, k=k: (y, z ^ k, c ^ (k & 1)) for k in (1, 2, 3)),
        tuple(lambda y, z, c, k=k: (y ^ k, z, c ^ (k & 1)) for k in (1, 2, 3)),
    )
    routes = []
    for flips in stages:
        routes.append([])
        for flip in flips:
            route = []
            for i in range(32):
                y, z, c = flip(i // 8, i // 2 % 4, i % 2)
                route.append((i, y * 8 + z * 2 + c))
            routes[-1].append(route)
    return routes


def solution(mesh):
    placed = (P("ax", "xs", None),) * 5 + (P(), P())
    return jax.shard_map(
        functools.partial(on_device, join_partners()),
        mesh=mesh, in_specs=placed, out_specs=P("ax", "xs", None), check_vma=False,
    )
```

time: 92.8 us -> 66.6 us (0.72)
  waiting for transfers between devices: 35 us -> 19.2 us
  local copies, waits for them, and re-layouts: 9.84 us -> 0.66 us
  other arithmetic: 8.43 us -> 0 us
  starting transfers between devices: 26.1 us -> 30.5 us
  Pallas kernels: 12.6 us -> 15.8 us
    ppermute x14 -> x18, waiting for transfers between devices: 35 us -> 18.9 us  [the longest x16 18.9 us: exchange(): return [lax.ppermute(block, 'ax', route) for route in partners[stage]]]
    sqrt x3 -> x0, other arithmetic: 8.36 us -> none  [edge_diffusivity(): return jnp.sqrt(mask.astype(jnp.float32) * lookup(layer, table) * stiff)]
    slice x4 -> x0, local copies, waits for them, and re-layouts: 5.32 us -> none  [the longest x1 1.5 us: side(): wall_layer[:, x]]
    ppermute x14 -> x18, starting transfers between devices: 21.9 us -> 26.5 us  [the longest x16 23 us: exchange(): return [lax.ppermute(block, 'ax', route) for route in partners[stage]]]
    unnamed x16 -> x4, local copies, waits for them, and re-layouts: 4.47 us -> 0.66 us
    pallas_call x16 -> x14, Pallas kernels: 12.6 us -> 15.8 us  [call(): pl.pallas_call(kernel, out_shape=outs, in_specs=specs or [vspec()] * len(...]
  transfers between devices with their start and end apart: 17 -> 21, of which waited for: 13 -> 14; matrix products, arithmetic and copies ran while one was open for 10% -> 0% of each run, Pallas kernels for 10% -> 15%
where the time goes in v1:
time: 66.6 us; the launch traced here: 66.5 us
  starting transfers between devices  30.5 us (46%)
  waiting for transfers between devices  19.2 us (29%)
  Pallas kernels  15.8 us (24%)
    ppermute x16, starting transfers between devices, exchange(): return [lax.ppermute(block, 'ax', route) for route in partners[stage]]  23 us
    ppermute x16, waiting for transfers between devices, exchange(): return [lax.ppermute(block, 'ax', route) for route in partners[stage]]  18.9 us
    pallas_call x14, Pallas kernels, call(): pl.pallas_call(kernel, out_shape=outs, in_specs=specs or [vspec()] * len(...  15.8 us
    ppermute x1, starting transfers between devices, on_device(): from_hi = lax.ppermute(lo, 'xs', downward)  2.66 us
    ppermute x1, starting transfers between devices, on_device(): halo_lo = lax.ppermute(hi, 'xs', upward)  2.11 us
    ppermute x1, starting transfers between devices, on_device(): halo_hi = lax.ppermute(lo, 'xs', downward)  1.35 us
  transfers between devices with their start and end apart: 21, of which 14 were waited for; matrix products, arithmetic and copies ran while one was open for 0% of the time, Pallas kernels for 15%

profile of v1, /device:TPU:1, one launch (start us, length us, event | category | flops | bytes accessed | tf_op | source)
XLA Modules:
  0.0 66.5 jit_solution(11406168261747181387)
XLA Ops:
  0.0 0.0 copy-start
  0.0 0.7 copy-done
  0.7 2.8 %shard_map.73 = (f32[2,32,384]{2,1,0:T(8,128)S(1)}, f32[2,32,384]{2,1,0:T(8,128)S(1)}, f32[32,384]{1,0:T(8,128)S(1)}, f32[2,32,8,384]{3,2,1,0:T(8,128)S(1)}) custom-call(f32[4]{0:T(128)S(1)} %copy-done, f32[32,32,384]{2,1,0:T(8,128)} %conc_hbm.3, s32[32,32,384]{2,1,0:T(8,128)} %mask_hbm.5, s32[32,32,384]{2,1,0:T(8,128)} %layer_hbm.5, f32[32,32,384]{2,1,0:T(8,128)} %stiff_hbm.3), custom_call_target="tpu_custom_call" | custom-call | flops 2000000 | bytes 3000000 | tf_op jit(solution)/shard_map/pallas_call | solution.py:460
  3.5 2.1 %collective-permute-start = (f32[2,32,384]{2,1,0:T(8,128)S(1)}, f32[2,32,384]{2,1,0:T(8,128)S(1)}, u32[]{:S(2)}, u32[]{:S(2)}) collective-permute-start(f32[2,32,384]{2,1,0:T(8,128)S(1)} %get-tuple-element.55), channel_id=1, source_target_pairs={{0,32},{32,64},{64,96},{96,0},{1,33},{33,65},{65,97},{97,1},{2,34}... | collective-permute-start | bytes 294920 | tf_op jit(solution)/shard_map/ppermute | solution.py:491
  5.6 1.3 %collective-permute-start.1 = (f32[2,32,384]{2,1,0:T(8,128)S(1)}, f32[2,32,384]{2,1,0:T(8,128)S(1)}, u32[]{:S(2)}, u32[]{:S(2)}) collective-permute-start(f32[2,32,384]{2,1,0:T(8,128)S(1)} %get-tuple-element.56), channel_id=1, source_target_pairs={{32,0},{64,32},{96,64},{0,96},{33,1},{65,33},{97,65},{1,97},{34,2}... | collective-permute-start | bytes 294920 | tf_op jit(solution)/shard_map/ppermute | solution.py:492
  6.9 1.3 %collective-permute-start.2 = (f32[32,384]{1,0:T(8,128)S(1)}, f32[32,384]{1,0:T(8,128)S(1)}, u32[]{:S(2)}, u32[]{:S(2)}) collective-permute-start(f32[32,384]{1,0:T(8,128)S(1)} %get-tuple-element.57), channel_id=1, source_target_pairs={{1,0},{2,1},{3,2},{4,3},{5,4},{6,5},{7,6},{8,7},{9,8},{10,9},{11,1... | collective-permute-start | bytes 147464 | tf_op jit(solution)/shard_map/ppermute | solution.py:493
  8.2 5.3 %shard_map.74 = (f32[32,32,384]{2,1,0:T(8,128)S(1)}, f32[32,32,384]{2,1,0:T(8,128)S(1)}, f32[32,32,384]{2,1,0:T(8,128)S(1)}, f32[32,32,384]{2,1,0:T(8,128)S(1)},...) custom-call(f32[4]{0:T(128)S(1)} %copy-done, f32[32,32,384]{2,1,0:T(8,128)} %conc_hbm.3, ...), custom_call_target="tpu_custom_call" | custom-call | flops 10000000 | bytes 15000000 | tf_op jit(solution)/shard_map/pallas_call | solution.py:460
  13.6 0.0 collective-permute-done.2.ax_ref
  13.6 0.0 collective-permute-done.lo_ref.first_lo_ref
  13.6 0.0 collective-permute-done.1.hi_ref.first_hi_ref
  13.6 0.0 copy-start.1
  13.6 0.6 shard_map.75
  14.2 5.5 %collective-permute-start.3 = (f32[5,16,384]{2,1,0:T(8,128)S(1)}, f32[5,16,384]{2,1,0:T(8,128)S(1)}, u32[]{:S(2)}, u32[]{:S(2)}) collective-permute-start(f32[5,16,384]{2,1,0:T(8,128)S(1)} %get-tuple-element.59), channel_id=1, source_target_pairs={{0,1},{1,0},{2,3},{3,2},{4,5},{5,4},{6,7},{7,6},{8,9},{9,8},{10,11... | collective-permute-start | bytes 368648 | tf_op jit(solution)/shard_map/ppermute | solution.py:471
  19.8 1.0 %collective-permute-done.3.refs_0_ = f32[5,16,384]{2,1,0:T(8,128)S(1)} collective-permute-done((f32[5,16,384]{2,1,0:T(8,128)S(1)}, f32[5,16,384]{2,1,0:T(8,128)S(1)}, u32[]{:S(2)}, u32[]{:S(2)}) %collective-permute-start.3) | collective-permute-done | bytes 122912 | tf_op jit(solution)/shard_map/ppermute | solution.py:471
  20.7 0.1 shard_map.76
  20.8 0.1 collective-permute-start.6
  20.9 0.1 collective-permute-start.5
  21.0 3.7 %collective-permute-start.4 = (f32[5,16,384]{2,1,0:T(8,128)S(1)}, f32[5,16,384]{2,1,0:T(8,128)S(1)}, u32[]{:S(2)}, u32[]{:S(2)}) collective-permute-start(f32[5,16,384]{2,1,0:T(8,128)S(1)} %get-tuple-element.65.mine), channel_id=1, source_target_pairs={{0,3},{1,2},{2,1},{3,0},{4,7},{5,6},{6,5},{7,4},{8,11},{9,10},{10,... | collective-permute-start | bytes 368648 | tf_op jit(solution)/shard_map/ppermute | solution.py:471
  24.7 0.0 copy-done.1
  24.7 3.1 %shard_map.77 = (f32[32,32,384]{2,1,0:T(8,128)S(1)}, f32[32,32,384]{2,1,0:T(8,128)S(1)}) custom-call(f32[4]{0:T(128)S(1)} %copy-done.1, s32[32,32,384]{2,1,0:T(8,128)} %mask_hbm.5, s32[32,32,384]{2,1,0:T(8,128)} %layer_hbm.5, f32[32,32,384]{2,1,0:T(8,128)} %prod_hbm.1), custom_call_target="tpu_custom_call" | custom-call | flops 4000000 | bytes 6000000 | tf_op jit(solution)/shard_map/pallas_call | solution.py:460
  27.8 2.3 %collective-permute-done.6.refs_2_ = f32[5,16,384]{2,1,0:T(8,128)S(1)} collective-permute-done((f32[5,16,384]{2,1,0:T(8,128)S(1)}, f32[5,16,384]{2,1,0:T(8,128)S(1)}, u32[]{:S(2)}, u32[]{:S(2)}) %collective-permute-start.6) | collective-permute-done | bytes 122912 | tf_op jit(solution)/shard_map/ppermute | solution.py:471
  30.1 0.0 collective-permute-done.5.refs_1_
  30.1 0.5 collective-permute-done.4.refs_0_
  30.6 0.2 shard_map.78
  30.8 0.6 collective-permute-start.9
  31.4 0.1 collective-permute-start.8
  31.4 3.2 %collective-permute-start.7 = (f32[5,16,384]{2,1,0:T(8,128)S(1)}, f32[5,16,384]{2,1,0:T(8,128)S(1)}, u32[]{:S(2)}, u32[]{:S(2)}) collective-permute-start(f32[5,16,384]{2,1,0:T(8,128)S(1)} %get-tuple-element.66.mine), channel_id=1, source_target_pairs={{0,9},{1,8},{2,11},{3,10},{4,13},{5,12},{6,15},{7,14},{8,1},{9,0},... | collective-permute-start | bytes 368648 | tf_op jit(solution)/shard_map/ppermute | solution.py:471
  34.7 5.1 %collective-permute-done.9.refs_2_ = f32[5,16,384]{2,1,0:T(8,128)S(1)} collective-permute-done((f32[5,16,384]{2,1,0:T(8,128)S(1)}, f32[5,16,384]{2,1,0:T(8,128)S(1)}, u32[]{:S(2)}, u32[]{:S(2)}) %collective-permute-start.9) | collective-permute-done | bytes 122912 | tf_op jit(solution)/shard_map/ppermute | solution.py:471
  39.8 0.0 collective-permute-done.8.refs_1_
  39.8 0.6 collective-permute-done.7.refs_0_
  40.4 0.2 shard_map.79
  40.6 0.1 collective-permute-start.10
  40.7 1.2 %collective-permute-done.10.other = f32[2,16,384]{2,1,0:T(8,128)S(1)} collective-permute-done((f32[2,16,384]{2,1,0:T(8,128)S(1)}, f32[2,16,384]{2,1,0:T(8,128)S(1)}, u32[]{:S(2)}, u32[]{:S(2)}) %collective-permute-start.10) | collective-permute-done | bytes 49184 | tf_op jit(solution)/shard_map/ppermute | solution.py:471
  41.9 0.3 shard_map.80
  42.2 0.1 collective-permute-start.11
  42.3 2.7 %collective-permute-start.12 = (f32[32,384]{1,0:T(8,128)S(1)}, f32[32,384]{1,0:T(8,128)S(1)}, u32[]{:S(2)}, u32[]{:S(2)}) collective-permute-start(f32[32,384]{1,0:T(8,128)S(1)} %get-tuple-element.80), channel_id=1, source_target_pairs={{32,0},{64,32},{96,64},{0,96},{33,1},{65,33},{97,65},{1,97},{34,2}... | collective-permute-start | bytes 147464 | tf_op jit(solution)/shard_map/ppermute | solution.py:549
  45.0 1.2 %shard_map.81.part_ref = f32[32,32,384]{2,1,0:T(8,128)S(1)} custom-call(f32[2,16,384]{2,1,0:T(8,128)S(1)} %get-tuple-element.71.own, f32[2,16,384]{2,1,0:T(8,128)S(1)} %collective-permute-done.10.other, f32[2,32,8,384]{3,2,1,0:T(8,128)S(1)} %get-tuple-element.77.edge_ref, f32[32,32,384]{2,1,0:T(8,128)S(1)} %get-tuple-element.49.s_ref, ...), custom_call_target="tpu_custom_call" | custom-call | flops 6000000 | bytes 9000000 | tf_op jit(solution)/shard_map/pallas_call | solution.py:460
  46.2 0.2 collective-permute-done.11.lo_ref
  46.5 0.0 collective-permute-done.12.hi_ref
  46.5 0.5 shard_map.82
  47.0 1.4 %collective-permute-start.13 = (f32[2,16,384]{2,1,0:T(8,128)S(1)}, f32[2,16,384]{2,1,0:T(8,128)S(1)}, u32[]{:S(2)}, u32[]{:S(2)}) collective-permute-start(f32[2,16,384]{2,1,0:T(8,128)S(1)} %get-tuple-element.82), channel_id=1, source_target_pairs={{0,1},{1,0},{2,3},{3,2},{4,5},{5,4},{6,7},{7,6},{8,9},{9,8},{10,11... | collective-permute-start | bytes 147464 | tf_op jit(solution)/shard_map/ppermute | solution.py:471
  48.4 0.9 %collective-permute-done.13.refs_0_ = f32[2,16,384]{2,1,0:T(8,128)S(1)} collective-permute-done((f32[2,16,384]{2,1,0:T(8,128)S(1)}, f32[2,16,384]{2,1,0:T(8,128)S(1)}, u32[]{:S(2)}, u32[]{:S(2)}) %collective-permute-start.13) | collective-permute-done | bytes 49184 | tf_op jit(solution)/shard_map/ppermute | solution.py:471
  49.3 1.6 %collective-permute-start.16 = (f32[2,16,384]{2,1,0:T(8,128)S(1)}, f32[2,16,384]{2,1,0:T(8,128)S(1)}, u32[]{:S(2)}, u32[]{:S(2)}) collective-permute-start(f32[2,16,384]{2,1,0:T(8,128)S(1)} %get-tuple-element.83.mine), channel_id=1, source_target_pairs={{0,7},{1,6},{2,5},{3,4},{4,3},{5,2},{6,1},{7,0},{8,15},{9,14},{10,... | collective-permute-start | bytes 147464 | tf_op jit(solution)/shard_map/ppermute | solution.py:471
  50.8 0.6 collective-permute-start.15
  51.5 1.7 %collective-permute-start.14 = (f32[2,16,384]{2,1,0:T(8,128)S(1)}, f32[2,16,384]{2,1,0:T(8,128)S(1)}, u32[]{:S(2)}, u32[]{:S(2)}) collective-permute-start(f32[2,16,384]{2,1,0:T(8,128)S(1)} %get-tuple-element.83.mine), channel_id=1, source_target_pairs={{0,3},{1,2},{2,1},{3,0},{4,7},{5,6},{6,5},{7,4},{8,11},{9,10},{10,... | collective-permute-start | bytes 147464 | tf_op jit(solution)/shard_map/ppermute | solution.py:471
  53.2 1.1 %collective-permute-done.16.refs_2_ = f32[2,16,384]{2,1,0:T(8,128)S(1)} collective-permute-done((f32[2,16,384]{2,1,0:T(8,128)S(1)}, f32[2,16,384]{2,1,0:T(8,128)S(1)}, u32[]{:S(2)}, u32[]{:S(2)}) %collective-permute-start.16) | collective-permute-done | bytes 49184 | tf_op jit(solution)/shard_map/ppermute | solution.py:471
  54.3 1.0 %collective-permute-done.15.refs_1_ = f32[2,16,384]{2,1,0:T(8,128)S(1)} collective-permute-done((f32[2,16,384]{2,1,0:T(8,128)S(1)}, f32[2,16,384]{2,1,0:T(8,128)S(1)}, u32[]{:S(2)}, u32[]{:S(2)}) %collective-permute-start.15) | collective-permute-done | bytes 49184 | tf_op jit(solution)/shard_map/ppermute | solution.py:471
  55.3 0.9 %collective-permute-done.14.refs_0_ = f32[2,16,384]{2,1,0:T(8,128)S(1)} collective-permute-done((f32[2,16,384]{2,1,0:T(8,128)S(1)}, f32[2,16,384]{2,1,0:T(8,128)S(1)}, u32[]{:S(2)}, u32[]{:S(2)}) %collective-permute-start.14) | collective-permute-done | bytes 49184 | tf_op jit(solution)/shard_map/ppermute | solution.py:471
  56.2 0.1 shard_map.84
  56.2 0.9 %collective-permute-start.19 = (f32[2,16,384]{2,1,0:T(8,128)S(1)}, f32[2,16,384]{2,1,0:T(8,128)S(1)}, u32[]{:S(2)}, u32[]{:S(2)}) collective-permute-start(f32[2,16,384]{2,1,0:T(8,128)S(1)} %get-tuple-element.84.mine), channel_id=1, source_target_pairs={{0,25},{1,24},{2,27},{3,26},{4,29},{5,28},{6,31},{7,30},{8,17},{9,... | collective-permute-start | bytes 147464 | tf_op jit(solution)/shard_map/ppermute | solution.py:471
  57.2 1.1 %collective-permute-start.18 = (f32[2,16,384]{2,1,0:T(8,128)S(1)}, f32[2,16,384]{2,1,0:T(8,128)S(1)}, u32[]{:S(2)}, u32[]{:S(2)}) collective-permute-start(f32[2,16,384]{2,1,0:T(8,128)S(1)} %get-tuple-element.84.mine), channel_id=1, source_target_pairs={{0,16},{1,17},{2,18},{3,19},{4,20},{5,21},{6,22},{7,23},{8,24},{9,... | collective-permute-start | bytes 147464 | tf_op jit(solution)/shard_map/ppermute | solution.py:471
  58.3 1.9 %collective-permute-start.17 = (f32[2,16,384]{2,1,0:T(8,128)S(1)}, f32[2,16,384]{2,1,0:T(8,128)S(1)}, u32[]{:S(2)}, u32[]{:S(2)}) collective-permute-start(f32[2,16,384]{2,1,0:T(8,128)S(1)} %get-tuple-element.84.mine), channel_id=1, source_target_pairs={{0,9},{1,8},{2,11},{3,10},{4,13},{5,12},{6,15},{7,14},{8,1},{9,0},... | collective-permute-start | bytes 147464 | tf_op jit(solution)/shard_map/ppermute | solution.py:471
  60.1 2.1 %collective-permute-done.19.refs_2_ = f32[2,16,384]{2,1,0:T(8,128)S(1)} collective-permute-done((f32[2,16,384]{2,1,0:T(8,128)S(1)}, f32[2,16,384]{2,1,0:T(8,128)S(1)}, u32[]{:S(2)}, u32[]{:S(2)}) %collective-permute-start.19) | collective-permute-done | bytes 49184 | tf_op jit(solution)/shard_map/ppermute | solution.py:471
  62.3 0.0 collective-permute-done.18.refs_1_
  62.3 1.3 %collective-permute-done.17.refs_0_ = f32[2,16,384]{2,1,0:T(8,128)S(1)} collective-permute-done((f32[2,16,384]{2,1,0:T(8,128)S(1)}, f32[2,16,384]{2,1,0:T(8,128)S(1)}, u32[]{:S(2)}, u32[]{:S(2)}) %collective-permute-start.17) | collective-permute-done | bytes 49184 | tf_op jit(solution)/shard_map/ppermute | solution.py:471
  63.6 0.1 shard_map.85
  63.7 0.5 collective-permute-start.20
  64.1 0.9 %collective-permute-done.20.other = f32[2,16,384]{2,1,0:T(8,128)S(1)} collective-permute-done((f32[2,16,384]{2,1,0:T(8,128)S(1)}, f32[2,16,384]{2,1,0:T(8,128)S(1)}, u32[]{:S(2)}, u32[]{:S(2)}) %collective-permute-start.20) | collective-permute-done | bytes 49184 | tf_op jit(solution)/shard_map/ppermute | solution.py:471
  65.0 1.3 %shard_map.86 = f32[32,32,384]{2,1,0:T(8,128)} custom-call(f32[2,16,384]{2,1,0:T(8,128)S(1)} %get-tuple-element.88.own, f32[2,16,384]{2,1,0:T(8,128)S(1)} %collective-permute-done.20.other, f32[32,32,384]{2,1,0:T(8,128)S(1)} %get-tuple-element.50.g_ref, f32[32,32,384]{2,1,0:T(8,128)S(1)} %get-tuple-element.51.r_ref, ...), custom_call_target="tpu_custom_call" | custom-call | flops 2000000 | bytes 3000000 | tf_op jit(solution)/shard_map/pallas_call | solution.py:460
  (1 shorter events, 0.0 us)
Async XLA Ops:
  0.0 0.7 copy-start
  3.5 10.1 %collective-permute-start = (f32[2,32,384]{2,1,0:T(8,128)S(1)}, f32[2,32,384]{2,1,0:T(8,128)S(1)}, u32[]{:S(2)}, u32[]{:S(2)}) collective-permute-start(f32[2,32,384]{2,1,0:T(8,128)S(1)} %get-tuple-element.55), channel_id=1, source_target_pairs={{0,32},{32,64},{64,96},{96,0},{1,33},{33,65},{65,97},{97,1},{2,34}... | collective-permute-start | bytes 294920 | tf_op jit(solution)/shard_map/ppermute | solution.py:491
  5.6 8.0 %collective-permute-start.1 = (f32[2,32,384]{2,1,0:T(8,128)S(1)}, f32[2,32,384]{2,1,0:T(8,128)S(1)}, u32[]{:S(2)}, u32[]{:S(2)}) collective-permute-start(f32[2,32,384]{2,1,0:T(8,128)S(1)} %get-tuple-element.56), channel_id=1, source_target_pairs={{32,0},{64,32},{96,64},{0,96},{33,1},{65,33},{97,65},{1,97},{34,2}... | collective-permute-start | bytes 294920 | tf_op jit(solution)/shard_map/ppermute | solution.py:492
  6.9 6.6 %collective-permute-start.2 = (f32[32,384]{1,0:T(8,128)S(1)}, f32[32,384]{1,0:T(8,128)S(1)}, u32[]{:S(2)}, u32[]{:S(2)}) collective-permute-start(f32[32,384]{1,0:T(8,128)S(1)} %get-tuple-element.57), channel_id=1, source_target_pairs={{1,0},{2,1},{3,2},{4,3},{5,4},{6,5},{7,6},{8,7},{9,8},{10,9},{11,1... | collective-permute-start | bytes 147464 | tf_op jit(solution)/shard_map/ppermute | solution.py:493
  13.6 11.1 %copy-start.1 = (f32[4]{0:T(128)S(1)}, f32[4]{0:T(128)}, u32[]{:S(2)}) copy-start(f32[4]{0:T(128)} %uptake_table) | copy-start | bytes 52
  14.2 6.5 %collective-permute-start.3 = (f32[5,16,384]{2,1,0:T(8,128)S(1)}, f32[5,16,384]{2,1,0:T(8,128)S(1)}, u32[]{:S(2)}, u32[]{:S(2)}) collective-permute-start(f32[5,16,384]{2,1,0:T(8,128)S(1)} %get-tuple-element.59), channel_id=1, source_target_pairs={{0,1},{1,0},{2,3},{3,2},{4,5},{5,4},{6,7},{7,6},{8,9},{9,8},{10,11... | collective-permute-start | bytes 368648 | tf_op jit(solution)/shard_map/ppermute | solution.py:471
  20.8 9.3 %collective-permute-start.6 = (f32[5,16,384]{2,1,0:T(8,128)S(1)}, f32[5,16,384]{2,1,0:T(8,128)S(1)}, u32[]{:S(2)}, u32[]{:S(2)}) collective-permute-start(f32[5,16,384]{2,1,0:T(8,128)S(1)} %get-tuple-element.65.mine), channel_id=1, source_target_pairs={{0,7},{1,6},{2,5},{3,4},{4,3},{5,2},{6,1},{7,0},{8,15},{9,14},{10,... | collective-permute-start | bytes 368648 | tf_op jit(solution)/shard_map/ppermute | solution.py:471
  20.9 9.2 %collective-permute-start.5 = (f32[5,16,384]{2,1,0:T(8,128)S(1)}, f32[5,16,384]{2,1,0:T(8,128)S(1)}, u32[]{:S(2)}, u32[]{:S(2)}) collective-permute-start(f32[5,16,384]{2,1,0:T(8,128)S(1)} %get-tuple-element.65.mine), channel_id=1, source_target_pairs={{0,4},{1,5},{2,6},{3,7},{4,0},{5,1},{6,2},{7,3},{8,12},{9,13},{10,... | collective-permute-start | bytes 368648 | tf_op jit(solution)/shard_map/ppermute | solution.py:471
  21.0 9.6 %collective-permute-start.4 = (f32[5,16,384]{2,1,0:T(8,128)S(1)}, f32[5,16,384]{2,1,0:T(8,128)S(1)}, u32[]{:S(2)}, u32[]{:S(2)}) collective-permute-start(f32[5,16,384]{2,1,0:T(8,128)S(1)} %get-tuple-element.65.mine), channel_id=1, source_target_pairs={{0,3},{1,2},{2,1},{3,0},{4,7},{5,6},{6,5},{7,4},{8,11},{9,10},{10,... | collective-permute-start | bytes 368648 | tf_op jit(solution)/shard_map/ppermute | solution.py:471
  30.8 9.0 %collective-permute-start.9 = (f32[5,16,384]{2,1,0:T(8,128)S(1)}, f32[5,16,384]{2,1,0:T(8,128)S(1)}, u32[]{:S(2)}, u32[]{:S(2)}) collective-permute-start(f32[5,16,384]{2,1,0:T(8,128)S(1)} %get-tuple-element.66.mine), channel_id=1, source_target_pairs={{0,25},{1,24},{2,27},{3,26},{4,29},{5,28},{6,31},{7,30},{8,17},{9,... | collective-permute-start | bytes 368648 | tf_op jit(solution)/shard_map/ppermute | solution.py:471
  31.4 8.4 %collective-permute-start.8 = (f32[5,16,384]{2,1,0:T(8,128)S(1)}, f32[5,16,384]{2,1,0:T(8,128)S(1)}, u32[]{:S(2)}, u32[]{:S(2)}) collective-permute-start(f32[5,16,384]{2,1,0:T(8,128)S(1)} %get-tuple-element.66.mine), channel_id=1, source_target_pairs={{0,16},{1,17},{2,18},{3,19},{4,20},{5,21},{6,22},{7,23},{8,24},{9,... | collective-permute-start | bytes 368648 | tf_op jit(solution)/shard_map/ppermute | solution.py:471
  31.4 8.9 %collective-permute-start.7 = (f32[5,16,384]{2,1,0:T(8,128)S(1)}, f32[5,16,384]{2,1,0:T(8,128)S(1)}, u32[]{:S(2)}, u32[]{:S(2)}) collective-permute-start(f32[5,16,384]{2,1,0:T(8,128)S(1)} %get-tuple-element.66.mine), channel_id=1, source_target_pairs={{0,9},{1,8},{2,11},{3,10},{4,13},{5,12},{6,15},{7,14},{8,1},{9,0},... | collective-permute-start | bytes 368648 | tf_op jit(solution)/shard_map/ppermute | solution.py:471
  40.6 1.3 %collective-permute-start.10 = (f32[2,16,384]{2,1,0:T(8,128)S(1)}, f32[2,16,384]{2,1,0:T(8,128)S(1)}, u32[]{:S(2)}, u32[]{:S(2)}) collective-permute-start(f32[2,16,384]{2,1,0:T(8,128)S(1)} %get-tuple-element.72), channel_id=1, source_target_pairs={{0,1},{1,0},{2,3},{3,2},{4,5},{5,4},{6,7},{7,6},{8,9},{9,8},{10,11... | collective-permute-start | bytes 147464 | tf_op jit(solution)/shard_map/ppermute | solution.py:471
  42.2 4.2 %collective-permute-start.11 = (f32[32,384]{1,0:T(8,128)S(1)}, f32[32,384]{1,0:T(8,128)S(1)}, u32[]{:S(2)}, u32[]{:S(2)}) collective-permute-start(f32[32,384]{1,0:T(8,128)S(1)} %get-tuple-element.79), channel_id=1, source_target_pairs={{0,32},{32,64},{64,96},{96,0},{1,33},{33,65},{65,97},{97,1},{2,34}... | collective-permute-start | bytes 147464 | tf_op jit(solution)/shard_map/ppermute | solution.py:548
  42.3 4.1 %collective-permute-start.12 = (f32[32,384]{1,0:T(8,128)S(1)}, f32[32,384]{1,0:T(8,128)S(1)}, u32[]{:S(2)}, u32[]{:S(2)}) collective-permute-start(f32[32,384]{1,0:T(8,128)S(1)} %get-tuple-element.80), channel_id=1, source_target_pairs={{32,0},{64,32},{96,64},{0,96},{33,1},{65,33},{97,65},{1,97},{34,2}... | collective-permute-start | bytes 147464 | tf_op jit(solution)/shard_map/ppermute | solution.py:549
  47.0 2.3 %collective-permute-start.13 = (f32[2,16,384]{2,1,0:T(8,128)S(1)}, f32[2,16,384]{2,1,0:T(8,128)S(1)}, u32[]{:S(2)}, u32[]{:S(2)}) collective-permute-start(f32[2,16,384]{2,1,0:T(8,128)S(1)} %get-tuple-element.82), channel_id=1, source_target_pairs={{0,1},{1,0},{2,3},{3,2},{4,5},{5,4},{6,7},{7,6},{8,9},{9,8},{10,11... | collective-permute-start | bytes 147464 | tf_op jit(solution)/shard_map/ppermute | solution.py:471
  49.3 5.0 %collective-permute-start.16 = (f32[2,16,384]{2,1,0:T(8,128)S(1)}, f32[2,16,384]{2,1,0:T(8,128)S(1)}, u32[]{:S(2)}, u32[]{:S(2)}) collective-permute-start(f32[2,16,384]{2,1,0:T(8,128)S(1)} %get-tuple-element.83.mine), channel_id=1, source_target_pairs={{0,7},{1,6},{2,5},{3,4},{4,3},{5,2},{6,1},{7,0},{8,15},{9,14},{10,... | collective-permute-start | bytes 147464 | tf_op jit(solution)/shard_map/ppermute | solution.py:471
  50.8 4.4 %collective-permute-start.15 = (f32[2,16,384]{2,1,0:T(8,128)S(1)}, f32[2,16,384]{2,1,0:T(8,128)S(1)}, u32[]{:S(2)}, u32[]{:S(2)}) collective-permute-start(f32[2,16,384]{2,1,0:T(8,128)S(1)} %get-tuple-element.83.mine), channel_id=1, source_target_pairs={{0,4},{1,5},{2,6},{3,7},{4,0},{5,1},{6,2},{7,3},{8,12},{9,13},{10,... | collective-permute-start | bytes 147464 | tf_op jit(solution)/shard_map/ppermute | solution.py:471
  51.5 4.7 %collective-permute-start.14 = (f32[2,16,384]{2,1,0:T(8,128)S(1)}, f32[2,16,384]{2,1,0:T(8,128)S(1)}, u32[]{:S(2)}, u32[]{:S(2)}) collective-permute-start(f32[2,16,384]{2,1,0:T(8,128)S(1)} %get-tuple-element.83.mine), channel_id=1, source_target_pairs={{0,3},{1,2},{2,1},{3,0},{4,7},{5,6},{6,5},{7,4},{8,11},{9,10},{10,... | collective-permute-start | bytes 147464 | tf_op jit(solution)/shard_map/ppermute | solution.py:471
  56.2 6.0 %collective-permute-start.19 = (f32[2,16,384]{2,1,0:T(8,128)S(1)}, f32[2,16,384]{2,1,0:T(8,128)S(1)}, u32[]{:S(2)}, u32[]{:S(2)}) collective-permute-start(f32[2,16,384]{2,1,0:T(8,128)S(1)} %get-tuple-element.84.mine), channel_id=1, source_target_pairs={{0,25},{1,24},{2,27},{3,26},{4,29},{5,28},{6,31},{7,30},{8,17},{9,... | collective-permute-start | bytes 147464 | tf_op jit(solution)/shard_map/ppermute | solution.py:471
  57.2 5.1 %collective-permute-start.18 = (f32[2,16,384]{2,1,0:T(8,128)S(1)}, f32[2,16,384]{2,1,0:T(8,128)S(1)}, u32[]{:S(2)}, u32[]{:S(2)}) collective-permute-start(f32[2,16,384]{2,1,0:T(8,128)S(1)} %get-tuple-element.84.mine), channel_id=1, source_target_pairs={{0,16},{1,17},{2,18},{3,19},{4,20},{5,21},{6,22},{7,23},{8,24},{9,... | collective-permute-start | bytes 147464 | tf_op jit(solution)/shard_map/ppermute | solution.py:471
  58.3 5.3 %collective-permute-start.17 = (f32[2,16,384]{2,1,0:T(8,128)S(1)}, f32[2,16,384]{2,1,0:T(8,128)S(1)}, u32[]{:S(2)}, u32[]{:S(2)}) collective-permute-start(f32[2,16,384]{2,1,0:T(8,128)S(1)} %get-tuple-element.84.mine), channel_id=1, source_target_pairs={{0,9},{1,8},{2,11},{3,10},{4,13},{5,12},{6,15},{7,14},{8,1},{9,0},... | collective-permute-start | bytes 147464 | tf_op jit(solution)/shard_map/ppermute | solution.py:471
  63.7 1.4 %collective-permute-start.20 = (f32[2,16,384]{2,1,0:T(8,128)S(1)}, f32[2,16,384]{2,1,0:T(8,128)S(1)}, u32[]{:S(2)}, u32[]{:S(2)}) collective-permute-start(f32[2,16,384]{2,1,0:T(8,128)S(1)} %get-tuple-element.89), channel_id=1, source_target_pairs={{0,1},{1,0},{2,3},{3,2},{4,5},{5,4},{6,7},{7,6},{8,9},{9,8},{10,11... | collective-permute-start | bytes 147464 | tf_op jit(solution)/shard_map/ppermute | solution.py:471

commit v2 on v1

v2 whole, which is shorter than its diff:
```python
import functools

import jax
import jax.numpy as jnp
from jax import lax
from jax.experimental import pallas as pl
from jax.experimental.pallas import tpu as pltpu
from jax.sharding import PartitionSpec as P

RZ = 3072.0
SECTION_RATE = 0.05
LAYERS = 4
LIMIT = 24 * 1024 * 1024
CHUNK = 8
PLANES = 5
JOIN_COEFS = 9
ORDER = (1, 2, 3)


def at_vmem(*shape):
    return pltpu.VMEM(shape, jnp.float32)


def vspec():
    return pl.BlockSpec(memory_space=pltpu.VMEM)


def params():
    return pltpu.CompilerParams(vmem_limit_bytes=LIMIT)


def cost(us):
    return pl.CostEstimate(flops=int(us * 2e6), bytes_accessed=int(us * 3e6), transcendentals=0)


def lookup(labels, table):
    value = table[LAYERS - 1]
    for layer in range(LAYERS - 1):
        value = jnp.where(labels == layer, table[layer], value)
    return value


def root_diffusivity(mask, layer, stiff, table):
    inside = lookup(layer, table) * stiff
    return jnp.where(mask == 0, 0.0, inside * lax.rsqrt(inside))


def inverse(x):
    return pl.reciprocal(x, approx=True)


def tiles_of(ref, z, slab, cols):
    return [[ref[z, t:t + 8, c:c + 128] for c in range(0, cols, 128)] for t in range(0, slab, 8)]


def neighbour_sum(tiles, border=None):
    rows, cols = len(tiles), len(tiles[0])
    row = lax.broadcasted_iota(jnp.int32, (8, 128), 0)
    lane = lax.broadcasted_iota(jnp.int32, (8, 128), 1)

    def rolled(shift, axis):
        return [[pltpu.roll(tile, shift, axis) for tile in line] for line in tiles]

    down, up, right, left = rolled(1, 0), rolled(7, 0), rolled(1, 1), rolled(127, 1)
    if border is not None:
        down.append([pltpu.roll(tile, 1, 0) for tile in border])
        up.append([pltpu.roll(tile, 7, 0) for tile in border])

    def at(array, t, c):
        if 0 <= c < cols and 0 <= t < rows:
            return array[t][c]
        return 0.0 if border is None or not 0 <= c < cols else array[rows][c]

    return [[
        (jnp.where(row == 0, at(down, t - 1, c), down[t][c]) + jnp.where(row == 7, at(up, t + 1, c), up[t][c]))
        + (jnp.where(lane == 0, at(right, t, c - 1), right[t][c])
           + jnp.where(lane == 127, at(left, t, c + 1), left[t][c]))
        for c in range(cols)] for t in range(rows)]


def along_cols(plane):
    cols = plane.shape[-1]
    lane = lax.broadcasted_iota(jnp.int32, plane.shape, 1)
    return (jnp.where(lane == 0, 0.0, pltpu.roll(plane, 1, 1))
            + jnp.where(lane == cols - 1, 0.0, pltpu.roll(plane, cols - 1, 1)))


def read_table(table):
    return [table[k] for k in range(LAYERS)]


def edge_kernel(
    slab, cols,
    diff_table, uptake_table, conc_hbm, mask_hbm, layer_hbm, stiff_hbm, prod_hbm,
    lo_out, hi_out, first_out,
    mask, layer, floats, mask_row, layer_row, stiff_row, sems, row_sems,
):
    copies = []
    for side in (0, 1):
        sources = []
        for depth in (0, 1):
            x = depth if side == 0 else slab - 1 - depth
            sources += [(mask_hbm.at[:, x], mask.at[side, depth]), (layer_hbm.at[:, x], layer.at[side, depth]),
                        (stiff_hbm.at[:, x], floats.at[side, depth]), (conc_hbm.at[:, x], floats.at[side, 2 + depth])]
        sources.append((prod_hbm.at[:, 0 if side == 0 else slab - 1], floats.at[side, 4]))
        copies.append([
            pltpu.make_async_copy(source, target, sems.at[side, k]) for k, (source, target) in enumerate(sources)])
    copies.append([
        pltpu.make_async_copy(source.at[0], target, row_sems.at[k])
        for k, (source, target) in enumerate(((mask_hbm, mask_row), (layer_hbm, layer_row), (stiff_hbm, stiff_row)))])
    for group in copies:
        for copy in group:
            copy.start()
    table, uptakes = read_table(diff_table), read_table(uptake_table)
    for side, out in ((0, lo_out), (1, hi_out)):
        for copy in copies[side]:
            copy.wait()
        s, inner = [root_diffusivity(mask[side, d], layer[side, d], floats[side, d], table) for d in (0, 1)]
        state = floats[side, 2]
        ssum = inner + along_cols(s)
        vsum = inner * floats[side, 3] + along_cols(s * state)
        weight = mask[side, 0].astype(jnp.float32)
        out[0] = s
        out[1] = state
        out[2] = state + SECTION_RATE * s * (vsum - state * ssum)
        out[3] = 1.0 - weight * lookup(layer[side, 0], uptakes)
        out[4] = weight * floats[side, 4]
    for copy in copies[2]:
        copy.wait()
    first_out[...] = root_diffusivity(mask_row[...], layer_row[...], stiff_row[...], table)


def setup_kernel(
    rows, slab, cols,
    table, conc_hbm, mask_hbm, layer_hbm, stiff_hbm,
    s_out, g_out, r_out, gp_out, ssum_out, part_out, ends_out,
    conc, mask, layer, stiff, sems,
):
    pairs = ((mask_hbm, mask), (layer_hbm, layer), (stiff_hbm, stiff), (conc_hbm, conc))
    copies = []
    for chunk in range(rows // CHUNK):
        here = pl.ds(chunk * CHUNK, CHUNK)
        copies.append([
            pltpu.make_async_copy(source.at[here], target.at[here], sems.at[k, chunk])
            for k, (source, target) in enumerate(pairs)
        ])
    for group in copies:
        for copy in group:
            copy.start()
    weights = read_table(table)
    grid = [(t, c) for t in range(slab // 8) for c in range(cols // 128)]
    s = m = gp = alpha = None
    for z in range(rows):
        if z % CHUNK == 0:
            for copy in copies[z // CHUNK]:
                copy.wait()
        w, lab, sti, st = [tiles_of(ref, z, slab, cols) for ref in (mask, layer, stiff, conc)]
        s_next = [[root_diffusivity(w[t][c], lab[t][c], sti[t][c], weights)
                   for c in range(cols // 128)] for t in range(slab // 8)]
        flow = [[s_next[t][c] * st[t][c] for c in range(cols // 128)] for t in range(slab // 8)]
        ssum, vsum = neighbour_sum(s_next), neighbour_sum(flow)
        for t, c in grid:
            here = (z, pl.ds(8 * t, 8), pl.ds(128 * c, 128))
            s_out[here] = s_next[t][c]
            ssum_out[here] = ssum[t][c]
            part_out[here] = st[t][c] + SECTION_RATE * s_next[t][c] * (vsum[t][c] - st[t][c] * ssum[t][c])
        if z == 0:
            ones = {k: jnp.ones((8, 128), jnp.float32) for k in grid}
            m, gp, alpha = dict(ones), dict(ones), {k: jnp.zeros((8, 128), jnp.float32) for k in grid}
        else:
            for t, c in grid:
                k = (t, c)
                here = (z - 1, pl.ds(8 * t, 8), pl.ds(128 * c, 128))
                couple = RZ * s[t][c] * s_next[t][c]
                r = inverse(m[k] + couple)
                g = couple * r
                r_out[here] = r
                g_out[here] = g
                gp_out[here] = gp[k]
                alpha[k] = alpha[k] + r * (gp[k] * gp[k])
                m[k] = 1.0 + g * m[k]
                gp[k] = gp[k] * g
        s = s_next
    for t, c in grid:
        here = (pl.ds(8 * t, 8), pl.ds(128 * c, 128))
        gp_out[(rows - 1,) + here] = gp[t, c]
        ends_out[(0,) + here] = m[t, c]
        ends_out[(1,) + here] = alpha[t, c]


def reaction_kernel(rows, uptake_table, mask_hbm, layer_hbm, prod_hbm, keep_out, source_out, mask, layer, prod, sems):
    copies = []
    for chunk in range(rows // CHUNK):
        here = pl.ds(chunk * CHUNK, CHUNK)
        copies.append([
            pltpu.make_async_copy(source.at[here], target.at[here], sems.at[k, chunk])
            for k, (source, target) in enumerate(((mask_hbm, mask), (layer_hbm, layer), (prod_hbm, prod)))
        ])
    for group in copies:
        for copy in group:
            copy.start()
    tab = read_table(uptake_table)
    for z in range(rows):
        if z % CHUNK == 0:
            for copy in copies[z // CHUNK]:
                copy.wait()
        weight = mask[z].astype(jnp.float32)
        keep_out[z] = 1.0 - weight * lookup(layer[z], tab)
        source_out[z] = weight * prod[z]


def tile_of(tiles, k):
    return tiles[8 * k:8 * k + 8]


def first_forward_kernel(
    rows, slab, cols, nx, nax,
    own_lo, own_hi, s_ref, g_ref, r_ref, gp_ref, part_ref, ends_ref, from_lo, from_hi, above_ref,
    fwd_ref, last_ref, mine_ref, send_ref, border_ref,
    ports_ref, border_ports, lines,
):
    ix, ia = lax.axis_index("xs"), lax.axis_index("ax")
    above = jnp.where(ia < nax - 1, RZ, 0.0)
    c = above * s_ref[rows - 1] * above_ref[...]
    m, alpha = ends_ref[0], ends_ref[1]
    last_r = inverse(m + c)
    last_g = c * last_r
    gp = gp_ref[rows - 1]
    last_ref[0] = last_g
    last_ref[1] = last_r
    ports_ref[2] = alpha + last_r * gp * gp
    ports_ref[3] = last_g * gp
    ports_ref[4] = last_g * m

    for side, (own, halo, exists) in enumerate(((own_lo, from_lo, ix > 0), (own_hi, from_hi, ix < nx - 1))):
        s_own, state_own = own[0], own[1]
        s = jnp.where(exists, halo[0], 0.0)
        state = halo[1]
        flux = SECTION_RATE * s_own * s * (state - state_own)
        lines[side, 0] = s
        lines[side, 1] = halo[2] - flux
        lines[side, 2] = RZ * s * pltpu.roll(s, rows - 1, 0)
        lines[side, 3] = flux
        lines[side, 4] = halo[3]
        lines[side, 5] = halo[4]

    row = lax.broadcasted_iota(jnp.int32, (8, cols), 0)
    is_lo = row == 7

    def border(k, z):
        return jnp.where(is_lo, lines[0, k, z:z + 1], lines[1, k, z:z + 1])

    total = prev = None
    for z in range(rows):
        part = part_ref[z]
        edges = (jnp.where(row == 0, lines[0, 3, z:z + 1], 0.0), jnp.where(row == 7, lines[1, 3, z:z + 1], 0.0))
        e = jnp.concatenate([part[0:8] + edges[0], part[8:slab - 8], part[slab - 8:] + edges[1]], axis=0)
        if z > 0:
            e = e + g_ref[z - 1] * prev
        fwd_ref[z] = e
        term = gp_ref[z] * (r_ref[z] if z < rows - 1 else last_r) * e
        total = term if z == 0 else total + term
        prev = e

        sb, eb = border(0, z), border(1, z)
        if z == 0:
            mb = gpb = jnp.ones_like(sb)
            first = sb
        else:
            eb = eb + gb * fb
            mb = 1.0 + gb * mb
            gpb = gpb * gb
        if z < rows - 1:
            cb = border(2, z)
            rb = inverse(mb + cb)
            gb = cb * rb
        else:
            rb = inverse(mb)
            gb = jnp.zeros_like(rb)
        fb = eb
        grb = gpb * rb
        ab = grb * gpb if z == 0 else ab + grb * gpb
        pb = grb * eb if z == 0 else pb + grb * eb
        for k, value in enumerate((sb, gb, rb, gpb, fb, border(4, z), border(5, z))):
            border_ref[k, z] = value
    ports_ref[0] = total
    ports_ref[1] = last_g * prev
    zero = jnp.zeros_like(sb)
    for k, value in enumerate((ab, grb, rb, pb, rb * fb, first, sb, zero)):
        border_ports[0, k:k + 1] = value[7:8]
        border_ports[1, k:k + 1] = value[0:1]
    half = place()[3]
    for out, which in ((mine_ref, half), (send_ref, 1 - half)):
        split_ports(slab, PLANES, ports_ref, out, which)
        out[2 * PLANES] = border_ports[which]


def split_ports(slab, planes, ports_ref, out, which):
    for t in range(slab // 16):
        at = pl.ds(pl.multiple_of(which * (slab // 2) + 8 * t, 8), 8)
        for k in range(planes):
            out[2 * k + t] = ports_ref[k, at]


def place():
    i = lax.axis_index("ax")
    core, z, y = lax.rem(i, 2), lax.rem(lax.div(i, 2), 4), lax.div(i, 8)
    return core, z, y, lax.rem(core + z + y, 2)


def pick(index, options):
    value = options[0]
    for k in range(1, len(options)):
        value = jnp.where(index == k, options[k], value)
    return value


def ordered(index, mine, received):
    return [pick(index ^ j, [mine] + received) for j in range(1 + len(received))]


def main_planes(stack, planes):
    return [stack[2 * k:2 * k + 2] for k in planes]


def put(stack, at, value):
    stack[2 * at:2 * at + 2] = value


def join_coefs(low, high, lev, at):
    (alpha1, beta1, kappa1), (alpha2, beta2, kappa2) = low, high
    rho = inverse(1.0 + kappa1 * alpha2)
    x, y = beta1 * rho, beta2 * rho
    ax, ky = alpha2 * x, kappa1 * y
    for k, value in enumerate((rho, kappa1, alpha2, beta1, beta2, x, y, ax, ky)):
        put(lev, at * JOIN_COEFS + k, value)
    return alpha1 + beta1 * ax, x * beta2, kappa2 + beta2 * ky


def join_rhs(low, high, lev, at, values):
    (a1, b1), (a2, b2) = low, high
    rho, kappa1, alpha2, beta1, beta2 = main_planes(lev, range(at * JOIN_COEFS, at * JOIN_COEFS + 5))
    u0 = rho * (a2 + alpha2 * b1)
    q0 = rho * (b1 - kappa1 * a2)
    put(values, 2 * at, u0)
    put(values, 2 * at + 1, q0)
    return a1 + beta1 * u0, b2 + beta2 * q0


def join_border(low, high, lev, at):
    (a1, b1, d1, first1, last1, s_first, s1), (a2, b2, d2, first2, last2, s2, s_last) = low, high
    c = RZ * s1 * s2
    k = c * inverse(1.0 + c * (a2 + d1))
    f, k1, k2 = k * (first2 - last1), k * b1, k * b2
    for j, value in enumerate((f, k1, k2)):
        lev[at, j:j + 1] = value
    return a1 - k1 * b1, k1 * b2, d2 - k2 * b2, first1 + b1 * f, last2 - b2 * f, s_first, s_last


def join_all(groups, join):
    if len(groups) == 2:
        return join(groups[0], groups[1], 0)
    return join(join(groups[0], groups[1], 0), join(groups[2], groups[3], 1), 2)


def stage_coefs(index, mine, received, lev):
    stacks = [main_planes(stack, (2, 3, 4)) for stack in (mine, *received)]
    planes = [ordered(index, own[0], list(own[1:])) for own in zip(*stacks)]
    return join_all(list(zip(*planes)), lambda low, high, at: join_coefs(low, high, lev, at))


def stage_rhs(index, mine, received, lev, values):
    stacks = [main_planes(stack, (0, 1)) for stack in (mine, *received)]
    planes = [ordered(index, own[0], list(own[1:])) for own in zip(*stacks)]
    return join_all(list(zip(*planes)), lambda low, high, at: join_rhs(low, high, lev, at, values))


def stage_border(index, mine, received, lev):
    tiles = ordered(index, mine[2 * PLANES], [stack[2 * PLANES] for stack in received])
    groups = [[tile[k:k + 1] for k in range(7)] for tile in tiles]
    return join_all(groups, lambda low, high, at: join_border(low, high, lev, at))


def stage_index(stage):
    return place()[stage]


def first_join_kernel(stage, count, mine, *refs):
    received, (out, lev, values, border_lev) = refs[:count], refs[count:]
    index = stage_index(stage)
    for k, value in zip((2, 3, 4), stage_coefs(index, mine, received, lev)):
        put(out, k, value)
    for k, value in zip((0, 1), stage_rhs(index, mine, received, lev, values)):
        put(out, k, value)
    for k, value in enumerate(stage_border(index, mine, received, border_lev)):
        out[2 * PLANES, k:k + 1] = value
    out[2 * PLANES, 7:8] = jnp.zeros_like(value)


def second_join_kernel(stage, count, mine, *refs):
    received, (lev, out, values) = refs[:count], refs[count:]
    for k, value in zip((0, 1), stage_rhs(stage_index(stage), mine, received, lev, values)):
        put(out, k, value)


def choose(which, ats, stack, width, k):
    return pick(which, [stack[2 * (j * width + k):2 * (j * width + k) + 2] for j in ats])


def inside(lev, values, which, ats, q, top):
    u0, q0 = [choose(which, ats, values, 2, k) for k in (0, 1)]
    if q is None:
        return u0, q0
    x, y, ax, ky = [choose(which, ats, lev, JOIN_COEFS, k) for k in (5, 6, 7, 8)]
    return u0 + y * top + ax * q, q0 + x * q - ky * top


def descend(levs, values, mine_out, send_out):
    core, z, y, _ = place()
    q = top = None
    for stage, index in ((2, y), (1, z)):
        lev, value = levs[stage], values[stage]
        mid_top, mid_q = inside(lev, value, 0, (2,), q, top)
        if q is None:
            q = top = jnp.zeros_like(mid_q)
        high = index >= 2
        q, top = jnp.where(high, mid_q, q), jnp.where(high, top, mid_top)
        mid_top, mid_q = inside(lev, value, lax.div(index, 2), (0, 1), q, top)
        odd = lax.rem(index, 2) == 1
        q, top = jnp.where(odd, mid_q, q), jnp.where(odd, top, mid_top)
    mid_top, mid_q = inside(levs[0], values[0], 0, (0,), q, top)
    upper = core == 1
    put(mine_out, 0, jnp.where(upper, mid_q, q))
    put(mine_out, 1, jnp.where(upper, top, mid_top))
    put(send_out, 0, jnp.where(upper, q, mid_q))
    put(send_out, 1, jnp.where(upper, mid_top, top))


def descend_border(levs, mine_out, send_out):
    core, z, y, _ = place()
    lo = hi = jnp.zeros_like(mine_out[4, 0:1])

    def flux(lev, which, ats):
        f, k1, k2 = [pick(which, [lev[j, k:k + 1] for j in ats]) for k in range(3)]
        return f + k2 * hi - k1 * lo

    for stage, index in ((2, y), (1, z)):
        f = flux(levs[stage], 0, (2,))
        high = index >= 2
        lo, hi = jnp.where(high, -f, lo), jnp.where(high, hi, f)
        f = flux(levs[stage], lax.div(index, 2), (0, 1))
        odd = lax.rem(index, 2) == 1
        lo, hi = jnp.where(odd, -f, lo), jnp.where(odd, hi, f)
    f = flux(levs[0], 0, (0,))
    upper = core == 1
    mine_out[4], send_out[4] = jnp.zeros_like(mine_out[4]), jnp.zeros_like(send_out[4])
    mine_out[4, 0:1], mine_out[4, 1:2] = jnp.where(upper, -f, lo), jnp.where(upper, hi, f)
    send_out[4, 0:1], send_out[4, 1:2] = jnp.where(upper, lo, -f), jnp.where(upper, f, hi)


def first_last_kernel(count, mine, *refs):
    received = refs[:count]
    lev0, lev1, val0, val1, blev0, blev1, mine_out, send_out, lev2, val2, blev2 = refs[count:]
    index = stage_index(2)
    stage_coefs(index, mine, received, lev2)
    stage_rhs(index, mine, received, lev2, val2)
    stage_border(index, mine, received, blev2)
    descend((lev0, lev1, lev2), (val0, val1, val2), mine_out, send_out)
    descend_border((blev0, blev1, blev2), mine_out, send_out)


def second_last_kernel(count, mine, *refs):
    received = refs[:count]
    lev0, lev1, lev2, val0, val1, mine_out, send_out, val2 = refs[count:]
    stage_rhs(stage_index(2), mine, received, lev2, val2)
    descend((lev0, lev1, lev2), (val0, val1, val2), mine_out, send_out)


def whole_ports(own, other):
    second = place()[3] == 1
    planes = []
    for k in (0, 1):
        low = [jnp.where(second, other[2 * k + t], own[2 * k + t]) for t in (0, 1)]
        high = [jnp.where(second, own[2 * k + t], other[2 * k + t]) for t in (0, 1)]
        planes.append(low + high)
    return planes


def split_cols(tile):
    return [tile[:, c:c + 128] for c in range(0, tile.shape[-1], 128)]


def middle_kernel(
    rows, slab, cols,
    own, other, s_ref, g_ref, r_ref, gp_ref, fwd_in, last_ref, keep_ref, source_ref, ssum_ref, border_ref,
    fwd_ref, mine_ref, send_ref, ports_ref,
):
    q, u = whole_ports(own, other)
    inflow = jnp.concatenate(q, axis=0)
    u = jnp.concatenate(u, axis=0)
    row = lax.broadcasted_iota(jnp.int32, (8, cols), 0)
    second = place()[3] == 1
    low_tile, high_tile = jnp.where(second, other[4], own[4]), jnp.where(second, own[4], other[4])
    inflow_b = jnp.where(row == 7, low_tile[0:1], high_tile[0:1])
    top_b = jnp.where(row == 7, low_tile[1:2], high_tile[1:2])
    narrow = lax.broadcasted_iota(jnp.int32, (8, 128), 0)
    last = slab // 8 - 1
    for z in range(rows - 1, -1, -1):
        r = r_ref[z] if z < rows - 1 else last_ref[1]
        g = g_ref[z] if z < rows - 1 else last_ref[0]
        u = r * (fwd_in[z] + gp_ref[z] * inflow) + g * u
        state = source_ref[z] + keep_ref[z] * u
        sb, gb, rb, gpb, fb, keep_b, source_b = [border_ref[k, z] for k in range(7)]
        rhs = fb + gpb * inflow_b
        ub = rb * (rhs + top_b) if z == rows - 1 else rb * rhs + gb * ub
        flow_b = split_cols(sb * (source_b + keep_b * ub))
        sb = split_cols(sb)
        state = [split_cols(tile_of(state, t)) for t in range(slab // 8)]
        s, ssum = tiles_of(s_ref, z, slab, cols), tiles_of(ssum_ref, z, slab, cols)
        ssum[0] = [x + jnp.where(narrow == 0, pltpu.roll(y, 1, 0), 0.0) for x, y in zip(ssum[0], sb)]
        ssum[last] = [x + jnp.where(narrow == 7, pltpu.roll(y, 7, 0), 0.0) for x, y in zip(ssum[last], sb)]
        vsum = neighbour_sum([[x * y for x, y in zip(*lines)] for lines in zip(s, state)], flow_b)
        for t in range(slab // 8):
            for c in range(cols // 128):
                fwd_ref[z, 8 * t:8 * t + 8, 128 * c:128 * c + 128] = state[t][c] + SECTION_RATE * s[t][c] * (
                    vsum[t][c] - state[t][c] * ssum[t][c])
    e = fwd_ref[0]
    total = gp_ref[0] * r_ref[0] * e
    for z in range(1, rows):
        e = fwd_ref[z] + g_ref[z - 1] * e
        fwd_ref[z] = e
        total = total + gp_ref[z] * (r_ref[z] if z < rows - 1 else last_ref[1]) * e
    ports_ref[0] = total
    ports_ref[1] = last_ref[0] * e
    half = place()[3]
    split_ports(slab, 2, ports_ref, mine_ref, half)
    split_ports(slab, 2, ports_ref, send_ref, 1 - half)


def final_kernel(
    rows, slab,
    own, other, g_ref, r_ref, gp_ref, fwd_ref, last_ref, keep_ref, source_ref,
    out_hbm, out, sems,
):
    q, u = [jnp.concatenate(tiles, axis=0) for tiles in whole_ports(own, other)]
    copies = []
    for z in range(rows - 1, -1, -1):
        r = r_ref[z] if z < rows - 1 else last_ref[1]
        g = g_ref[z] if z < rows - 1 else last_ref[0]
        u = r * (fwd_ref[z] + gp_ref[z] * q) + g * u
        out[z] = source_ref[z] + keep_ref[z] * u
        if z % CHUNK == 0:
            here = pl.ds(z, CHUNK)
            copy = pltpu.make_async_copy(out.at[here], out_hbm.at[here], sems.at[z // CHUNK])
            copy.start()
            copies.append(copy)
    for copy in copies:
        copy.wait()


def on_device(partners, concentration, tissue_mask, wall_layer, stiffness, production, layer_diffusivity, uptake_rate):
    rows, slab, cols = concentration.shape
    nx, nax = lax.axis_size("xs"), lax.axis_size("ax")
    block = (rows, slab, cols)
    smem = pl.BlockSpec(memory_space=pltpu.SMEM)
    hbm = pl.BlockSpec(memory_space=pltpu.HBM)

    def in_hbm(x):
        return pltpu.with_memory_space_constraint(x, pltpu.HBM)

    def call(kernel, outs, operands, scratch=(), specs=None, out_specs=None, us=1.0):
        return pl.pallas_call(
            kernel,
            out_shape=outs,
            in_specs=specs or [vspec()] * len(operands),
            out_specs=out_specs or [vspec()] * len(outs),
            scratch_shapes=list(scratch),
            compiler_params=params(),
            cost_estimate=cost(us),
        )(*operands)

    def exchange(block, stage):
        received = {step: lax.ppermute(block, "ax", route) for step, route in partners[stage]}
        return [received[step] for step in sorted(received)]

    def f32(*shape):
        return pltpu.VMEM(shape, jnp.float32)

    def i32(*shape):
        return pltpu.VMEM(shape, jnp.int32)

    conc, mask, layer, stiff, prod = [
        in_hbm(x) for x in (concentration, tissue_mask, wall_layer, stiffness, production)]
    diff_table, uptake_rate = in_hbm(layer_diffusivity), in_hbm(uptake_rate)
    lo, hi, first_s = call(
        functools.partial(edge_kernel, slab, cols),
        [at_vmem(5, rows, cols), at_vmem(5, rows, cols), at_vmem(slab, cols)],
        [diff_table, uptake_rate, conc, mask, layer, stiff, prod],
        scratch=[i32(2, 2, rows, cols), i32(2, 2, rows, cols), f32(2, 5, rows, cols),
                 i32(slab, cols), i32(slab, cols), f32(slab, cols),
                 pltpu.SemaphoreType.DMA((2, 9)), pltpu.SemaphoreType.DMA((3,))],
        specs=[smem, smem] + [hbm] * 5,
    )
    from_lo = lax.ppermute(hi, "xs", [(i, (i + 1) % nx) for i in range(nx)])
    from_hi = lax.ppermute(lo, "xs", [((i + 1) % nx, i) for i in range(nx)])
    above_s = lax.ppermute(first_s, "ax", [((i + 1) % nax, i) for i in range(nax)])

    s, g, r, gp, ssum, part, ends = call(
        functools.partial(setup_kernel, rows, slab, cols),
        [at_vmem(*block)] * 6 + [at_vmem(2, slab, cols)],
        [diff_table, conc, mask, layer, stiff],
        scratch=[f32(*block), i32(*block), i32(*block), f32(*block), pltpu.SemaphoreType.DMA((4, rows // CHUNK))],
        specs=[smem] + [hbm] * 4,
        us=5.0,
    )
    stack, pair = 2 * PLANES + 1, (5, 8, cols)
    fwd, last, mine, send, border = call(
        functools.partial(first_forward_kernel, rows, slab, cols, nx, nax),
        [at_vmem(*block), at_vmem(2, slab, cols), at_vmem(stack, 8, cols), at_vmem(stack, 8, cols),
         at_vmem(7, rows, 8, cols)],
        [lo, hi, s, g, r, gp, part, ends, from_lo, from_hi, above_s],
        scratch=[f32(PLANES, slab, cols), f32(2, 8, cols), f32(2, 6, rows, cols)],
    )
    levs, values, border_levs = [], [], []
    for stage in (0, 1):
        received = exchange(mine if stage else send, stage)
        joins = len(received)
        if stage == 1:
            uptake_late, mine = lax.optimization_barrier((uptake_rate, mine))
            keep, source = call(
                functools.partial(reaction_kernel, rows),
                [at_vmem(*block)] * 2,
                [uptake_late, mask, layer, prod],
                scratch=[i32(*block), i32(*block), f32(*block), pltpu.SemaphoreType.DMA((3, rows // CHUNK))],
                specs=[smem] + [hbm] * 3,
                us=2.0,
            )
            mine, keep, source = lax.optimization_barrier((mine, keep, source))
        mine, lev, value, border_lev = call(
            functools.partial(first_join_kernel, stage, joins),
            [at_vmem(stack, 8, cols), at_vmem(2 * JOIN_COEFS * joins, 8, cols), at_vmem(4 * joins, 8, cols),
             at_vmem(joins, 8, cols)],
            [mine, *received],
        )
        levs.append(lev)
        values.append(value)
        border_levs.append(border_lev)
    received = exchange(mine, 2)
    joins = len(received)
    own, send, lev = call(
        functools.partial(first_last_kernel, joins),
        [at_vmem(*pair), at_vmem(*pair), at_vmem(2 * JOIN_COEFS * joins, 8, cols)],
        [mine, *received, *levs, *values, *border_levs],
        scratch=[f32(4 * joins, 8, cols), f32(joins, 8, cols)],
    )
    levs.append(lev)
    (other,) = exchange(send, 0)

    fwd, mine, send = call(
        functools.partial(middle_kernel, rows, slab, cols),
        [at_vmem(*block), at_vmem(4, 8, cols), at_vmem(4, 8, cols)],
        [own, other, s, g, r, gp, fwd, last, keep, source, ssum, border],
        scratch=[f32(2, slab, cols)],
        us=3.0,
    )
    values = []
    for stage in (0, 1):
        received = exchange(mine if stage else send, stage)
        joins = len(received)
        mine, value = call(
            functools.partial(second_join_kernel, stage, joins),
            [at_vmem(4, 8, cols), at_vmem(4 * joins, 8, cols)],
            [mine, *received, levs[stage]],
        )
        values.append(value)
    received = exchange(mine, 2)
    joins = len(received)
    own, send = call(
        functools.partial(second_last_kernel, joins),
        [at_vmem(4, 8, cols), at_vmem(4, 8, cols)],
        [mine, *received, *levs, *values],
        scratch=[f32(4 * joins, 8, cols)],
    )
    (other,) = exchange(send, 0)
    (out,) = call(
        functools.partial(final_kernel, rows, slab),
        [jax.ShapeDtypeStruct(block, jnp.float32)],
        [own, other, g, r, gp, fwd, last, keep, source],
        scratch=[f32(*block), pltpu.SemaphoreType.DMA((rows // CHUNK,))],
        out_specs=[hbm],
    )
    return out


def join_partners():
    stages = (
        ((1, lambda y, z, c: (y, z, 1 - c)),),
        tuple((k, lambda y, z, c, k=k: (y, z ^ k, c ^ (k & 1))) for k in ORDER),
        tuple((k, lambda y, z, c, k=k: (y ^ k, z, c ^ (k & 1))) for k in ORDER),
    )
    routes = []
    for flips in stages:
        routes.append([])
        for step, flip in flips:
            route = []
            for i in range(32):
                y, z, c = flip(i // 8, i // 2 % 4, i % 2)
                route.append((i, y * 8 + z * 2 + c))
            routes[-1].append((step, route))
    return routes


def solution(mesh):
    placed = (P("ax", "xs", None),) * 5 + (P(), P())
    return jax.shard_map(
        functools.partial(on_device, join_partners()),
        mesh=mesh, in_specs=placed, out_specs=P("ax", "xs", None), check_vma=False,
    )
```

time: 66.6 us -> 64 us (0.961)
  starting transfers between devices: 30.5 us -> 25.6 us
  waiting for transfers between devices: 19.2 us -> 22.1 us
    ppermute x20 -> x18, starting transfers between devices: 29.2 us -> 24.7 us  [the longest x16 21.3 us: exchange(): lax.ppermute(block, 'ax', route)]
    ppermute x20 -> x18, waiting for transfers between devices: 19.2 us -> 22.1 us  [the longest x16 20.2 us: exchange(): lax.ppermute(block, 'ax', route)]
    pallas_call x14 -> x12, Pallas kernels: 15.8 us -> 15.9 us  [call(): pl.pallas_call(kernel, out_shape=outs, in_specs=specs or [vspec()] * len(...]
  transfers between devices with their start and end apart: 21 -> 19, of which waited for: 14 -> 13; matrix products, arithmetic and copies ran while one was open for 0% -> 0% of each run, Pallas kernels for 15% -> 13%
where the time goes in v2:
time: 64 us; the launch traced here: 63.8 us
  starting transfers between devices  25.6 us (40%)
  waiting for transfers between devices  22.1 us (35%)
  Pallas kernels  15.9 us (25%)
    ppermute x16, starting transfers between devices, exchange(): lax.ppermute(block, 'ax', route)  21.3 us
    ppermute x16, waiting for transfers between devices, exchange(): lax.ppermute(block, 'ax', route)  20.2 us
    pallas_call x12, Pallas kernels, call(): pl.pallas_call(kernel, out_shape=outs, in_specs=specs or [vspec()] * len(...  15.9 us
    ppermute x1, starting transfers between devices, on_device(): from_hi = lax.ppermute(lo, 'xs', [((i + 1) % nx, i) for i in range(nx)])  3.38 us
    ppermute x1, waiting for transfers between devices, on_device(): from_lo = lax.ppermute(hi, 'xs', [(i, (i + 1) % nx) for i in range(nx)])  1.87 us
  transfers between devices with their start and end apart: 19, of which 13 were waited for; matrix products, arithmetic and copies ran while one was open for 0% of the time, Pallas kernels for 13%

profile of v2, /device:TPU:1, one launch (start us, length us, event | category | flops | bytes accessed | tf_op | source)
XLA Modules:
  0.0 63.8 jit_solution(8450185458288125457)
XLA Ops:
  0.0 2.3 %shard_map.73 = (f32[5,32,384]{2,1,0:T(8,128)S(1)}, f32[5,32,384]{2,1,0:T(8,128)S(1)}, f32[32,384]{1,0:T(8,128)S(1)}) custom-call(f32[4]{0:T(128)} %table.1, f32[4]{0:T(128)} %uptake_table.2, f32[32,32,384]{2,1,0:T(8,128)} %conc_hbm.3, s32[32,32,384]{2,1,0:T(8,128)} %mask_hbm.5, s32[32,32,384]{2,1,0:T(8,128)} %layer_hbm.5, f32[32,32,384]{2,1,0:T(8,128)} %stiff_hbm.3, ...), custom_call_target="tpu_custom_call" | custom-call | flops 2000000 | bytes 3000000 | tf_op jit(solution)/shard_map/pallas_call | solution.py:572
  2.3 3.4 %collective-permute-start.1 = (f32[5,32,384]{2,1,0:T(8,128)S(1)}, f32[5,32,384]{2,1,0:T(8,128)S(1)}, u32[]{:S(2)}, u32[]{:S(2)}) collective-permute-start(f32[5,32,384]{2,1,0:T(8,128)S(1)} %get-tuple-element.47.own_lo), channel_id=1, source_target_pairs={{32,0},{64,32},{96,64},{0,96},{33,1},{65,33},{97,65},{1,97},{34,2}... | collective-permute-start | bytes 737288 | tf_op jit(solution)/shard_map/ppermute | solution.py:605
  5.7 0.0 collective-permute-start
  5.7 1.0 %collective-permute-start.2 = (f32[32,384]{1,0:T(8,128)S(1)}, f32[32,384]{1,0:T(8,128)S(1)}, u32[]{:S(2)}, u32[]{:S(2)}) collective-permute-start(f32[32,384]{1,0:T(8,128)S(1)} %get-tuple-element.55), channel_id=1, source_target_pairs={{1,0},{2,1},{3,2},{4,3},{5,4},{6,5},{7,6},{8,7},{9,8},{10,9},{11,1... | collective-permute-start | bytes 147464 | tf_op jit(solution)/shard_map/ppermute | solution.py:606
  6.7 4.9 %shard_map.74 = (f32[32,32,384]{2,1,0:T(8,128)S(1)}, f32[32,32,384]{2,1,0:T(8,128)S(1)}, f32[32,32,384]{2,1,0:T(8,128)S(1)}, f32[32,32,384]{2,1,0:T(8,128)S(1)},...) custom-call(f32[4]{0:T(128)} %table.1, f32[32,32,384]{2,1,0:T(8,128)} %conc_hbm.3, ...), custom_call_target="tpu_custom_call" | custom-call | flops 10000000 | bytes 15000000 | tf_op jit(solution)/shard_map/pallas_call | solution.py:572
  11.5 0.0 collective-permute-done.2.above_ref
  11.5 0.0 collective-permute-done.1.from_hi
  11.6 1.9 %collective-permute-done.from_lo = f32[5,32,384]{2,1,0:T(8,128)S(1)} collective-permute-done((f32[5,32,384]{2,1,0:T(8,128)S(1)}, f32[5,32,384]{2,1,0:T(8,128)S(1)}, u32[]{:S(2)}, u32[]{:S(2)}) %collective-permute-start) | collective-permute-done | bytes 245792 | tf_op jit(solution)/shard_map/ppermute | solution.py:604
  13.4 0.9 %shard_map.75 = (f32[32,32,384]{2,1,0:T(8,128)S(1)}, f32[2,32,384]{2,1,0:T(8,128)S(1)}, f32[11,8,384]{2,1,0:T(8,128)S(1)}, f32[11,8,384]{2,1,0:T(8,128)S(1)}, f32[7,32,8,384]{3,2,1,0:T(8,128)S(1)}) custom-call(f32[5,32,384]{2,1,0:T(8,128)S(1)} %get-tuple-element.47.own_lo, f32[5,32,384]{2,1,0:T(8,128)S(1)} %get-tuple-element.48.own_hi, ...), custom_call_target="tpu_custom_call" | custom-call | flops 2000000 | bytes 3000000 | tf_op jit(solution)/shard_map/pallas_call | solution.py:572
  14.3 3.9 %collective-permute-start.3 = (f32[11,8,384]{2,1,0:T(8,128)S(1)}, f32[11,8,384]{2,1,0:T(8,128)S(1)}, u32[]{:S(2)}, u32[]{:S(2)}) collective-permute-start(f32[11,8,384]{2,1,0:T(8,128)S(1)} %get-tuple-element.57), channel_id=1, source_target_pairs={{0,1},{1,0},{2,3},{3,2},{4,5},{5,4},{6,7},{7,6},{8,9},{9,8},{10,11... | collective-permute-start | bytes 405512 | tf_op jit(solution)/shard_map/ppermute | solution.py:583
  18.2 1.0 %collective-permute-done.3.refs_0_ = f32[11,8,384]{2,1,0:T(8,128)S(1)} collective-permute-done((f32[11,8,384]{2,1,0:T(8,128)S(1)}, f32[11,8,384]{2,1,0:T(8,128)S(1)}, u32[]{:S(2)}, u32[]{:S(2)}) %collective-permute-start.3) | collective-permute-done | bytes 135200 | tf_op jit(solution)/shard_map/ppermute | solution.py:583
  19.2 0.1 shard_map.76
  19.2 2.2 %collective-permute-start.6 = (f32[11,8,384]{2,1,0:T(8,128)S(1)}, f32[11,8,384]{2,1,0:T(8,128)S(1)}, u32[]{:S(2)}, u32[]{:S(2)}) collective-permute-start(f32[11,8,384]{2,1,0:T(8,128)S(1)} %get-tuple-element.63.mine), channel_id=1, source_target_pairs={{0,7},{1,6},{2,5},{3,4},{4,3},{5,2},{6,1},{7,0},{8,15},{9,14},{10,... | collective-permute-start | bytes 405512 | tf_op jit(solution)/shard_map/ppermute | solution.py:583
  21.4 0.0 collective-permute-start.5
  21.4 1.7 %collective-permute-start.4 = (f32[11,8,384]{2,1,0:T(8,128)S(1)}, f32[11,8,384]{2,1,0:T(8,128)S(1)}, u32[]{:S(2)}, u32[]{:S(2)}) collective-permute-start(f32[11,8,384]{2,1,0:T(8,128)S(1)} %get-tuple-element.63.mine), channel_id=1, source_target_pairs={{0,3},{1,2},{2,1},{3,0},{4,7},{5,6},{6,5},{7,4},{8,11},{9,10},{10,... | collective-permute-start | bytes 405512 | tf_op jit(solution)/shard_map/ppermute | solution.py:583
  23.1 3.2 %shard_map.77 = (f32[32,32,384]{2,1,0:T(8,128)S(1)}, f32[32,32,384]{2,1,0:T(8,128)S(1)}) custom-call(f32[4]{0:T(128)} %uptake_table.2, s32[32,32,384]{2,1,0:T(8,128)} %mask_hbm.5, s32[32,32,384]{2,1,0:T(8,128)} %layer_hbm.5, f32[32,32,384]{2,1,0:T(8,128)} %prod_hbm.3), custom_call_target="tpu_custom_call" | custom-call | flops 4000000 | bytes 6000000 | tf_op jit(solution)/shard_map/pallas_call | solution.py:572
  26.3 2.8 %collective-permute-done.6.refs_2_ = f32[11,8,384]{2,1,0:T(8,128)S(1)} collective-permute-done((f32[11,8,384]{2,1,0:T(8,128)S(1)}, f32[11,8,384]{2,1,0:T(8,128)S(1)}, u32[]{:S(2)}, u32[]{:S(2)}) %collective-permute-start.6) | collective-permute-done | bytes 135200 | tf_op jit(solution)/shard_map/ppermute | solution.py:583
  29.1 0.0 collective-permute-done.5.refs_1_
  29.1 0.5 collective-permute-done.4.refs_0_
  29.6 0.2 shard_map.78
  29.8 2.6 %collective-permute-start.9 = (f32[11,8,384]{2,1,0:T(8,128)S(1)}, f32[11,8,384]{2,1,0:T(8,128)S(1)}, u32[]{:S(2)}, u32[]{:S(2)}) collective-permute-start(f32[11,8,384]{2,1,0:T(8,128)S(1)} %get-tuple-element.64.mine), channel_id=1, source_target_pairs={{0,25},{1,24},{2,27},{3,26},{4,29},{5,28},{6,31},{7,30},{8,17},{9,... | collective-permute-start | bytes 405512 | tf_op jit(solution)/shard_map/ppermute | solution.py:583
  32.4 0.3 collective-permute-start.8
  32.7 1.0 %collective-permute-start.7 = (f32[11,8,384]{2,1,0:T(8,128)S(1)}, f32[11,8,384]{2,1,0:T(8,128)S(1)}, u32[]{:S(2)}, u32[]{:S(2)}) collective-permute-start(f32[11,8,384]{2,1,0:T(8,128)S(1)} %get-tuple-element.64.mine), channel_id=1, source_target_pairs={{0,9},{1,8},{2,11},{3,10},{4,13},{5,12},{6,15},{7,14},{8,1},{9,0},... | collective-permute-start | bytes 405512 | tf_op jit(solution)/shard_map/ppermute | solution.py:583
  33.7 5.7 %collective-permute-done.9.refs_2_ = f32[11,8,384]{2,1,0:T(8,128)S(1)} collective-permute-done((f32[11,8,384]{2,1,0:T(8,128)S(1)}, f32[11,8,384]{2,1,0:T(8,128)S(1)}, u32[]{:S(2)}, u32[]{:S(2)}) %collective-permute-start.9) | collective-permute-done | bytes 135200 | tf_op jit(solution)/shard_map/ppermute | solution.py:583
  39.4 0.0 collective-permute-done.8.refs_1_
  39.4 0.5 collective-permute-done.7.refs_0_
  40.0 0.2 shard_map.79
  40.2 0.4 collective-permute-start.10
  40.6 1.0 %collective-permute-done.10.other = f32[5,8,384]{2,1,0:T(8,128)S(1)} collective-permute-done((f32[5,8,384]{2,1,0:T(8,128)S(1)}, f32[5,8,384]{2,1,0:T(8,128)S(1)}, u32[]{:S(2)}, u32[]{:S(2)}) %collective-permute-start.10) | collective-permute-done | bytes 61472 | tf_op jit(solution)/shard_map/ppermute | solution.py:583
  41.5 2.5 %shard_map.80 = (f32[32,32,384]{2,1,0:T(8,128)S(1)}, f32[4,8,384]{2,1,0:T(8,128)S(1)}, f32[4,8,384]{2,1,0:T(8,128)S(1)}) custom-call(f32[5,8,384]{2,1,0:T(8,128)S(1)} %get-tuple-element.71.own, f32[5,8,384]{2,1,0:T(8,128)S(1)} %collective-permute-done.10.other, f32[32,32,384]{2,1,0:T(8,128)S(1)} %get-tuple-element.49.s_ref, ...), custom_call_target="tpu_custom_call" | custom-call | flops 6000000 | bytes 9000000 | tf_op jit(solution)/shard_map/pallas_call | solution.py:572
  44.1 0.4 collective-permute-start.11
  44.4 1.0 %collective-permute-done.11.refs_0_ = f32[4,8,384]{2,1,0:T(8,128)S(1)} collective-permute-done((f32[4,8,384]{2,1,0:T(8,128)S(1)}, f32[4,8,384]{2,1,0:T(8,128)S(1)}, u32[]{:S(2)}, u32[]{:S(2)}) %collective-permute-start.11) | collective-permute-done | bytes 49184 | tf_op jit(solution)/shard_map/ppermute | solution.py:583
  45.4 2.7 %collective-permute-start.14 = (f32[4,8,384]{2,1,0:T(8,128)S(1)}, f32[4,8,384]{2,1,0:T(8,128)S(1)}, u32[]{:S(2)}, u32[]{:S(2)}) collective-permute-start(f32[4,8,384]{2,1,0:T(8,128)S(1)} %get-tuple-element.81.mine), channel_id=1, source_target_pairs={{0,7},{1,6},{2,5},{3,4},{4,3},{5,2},{6,1},{7,0},{8,15},{9,14},{10,... | collective-permute-start | bytes 147464 | tf_op jit(solution)/shard_map/ppermute | solution.py:583
  48.2 0.0 collective-permute-start.13
  48.2 1.1 %collective-permute-start.12 = (f32[4,8,384]{2,1,0:T(8,128)S(1)}, f32[4,8,384]{2,1,0:T(8,128)S(1)}, u32[]{:S(2)}, u32[]{:S(2)}) collective-permute-start(f32[4,8,384]{2,1,0:T(8,128)S(1)} %get-tuple-element.81.mine), channel_id=1, source_target_pairs={{0,3},{1,2},{2,1},{3,0},{4,7},{5,6},{6,5},{7,4},{8,11},{9,10},{10,... | collective-permute-start | bytes 147464 | tf_op jit(solution)/shard_map/ppermute | solution.py:583
  49.3 1.0 %collective-permute-done.14.refs_2_ = f32[4,8,384]{2,1,0:T(8,128)S(1)} collective-permute-done((f32[4,8,384]{2,1,0:T(8,128)S(1)}, f32[4,8,384]{2,1,0:T(8,128)S(1)}, u32[]{:S(2)}, u32[]{:S(2)}) %collective-permute-start.14) | collective-permute-done | bytes 49184 | tf_op jit(solution)/shard_map/ppermute | solution.py:583
  50.3 2.3 %collective-permute-done.13.refs_1_ = f32[4,8,384]{2,1,0:T(8,128)S(1)} collective-permute-done((f32[4,8,384]{2,1,0:T(8,128)S(1)}, f32[4,8,384]{2,1,0:T(8,128)S(1)}, u32[]{:S(2)}, u32[]{:S(2)}) %collective-permute-start.13) | collective-permute-done | bytes 49184 | tf_op jit(solution)/shard_map/ppermute | solution.py:583
  52.6 0.0 collective-permute-done.12.refs_0_
  52.6 0.1 shard_map.82
  52.7 3.7 %collective-permute-start.17 = (f32[4,8,384]{2,1,0:T(8,128)S(1)}, f32[4,8,384]{2,1,0:T(8,128)S(1)}, u32[]{:S(2)}, u32[]{:S(2)}) collective-permute-start(f32[4,8,384]{2,1,0:T(8,128)S(1)} %get-tuple-element.82.mine), channel_id=1, source_target_pairs={{0,25},{1,24},{2,27},{3,26},{4,29},{5,28},{6,31},{7,30},{8,17},{9,... | collective-permute-start | bytes 147464 | tf_op jit(solution)/shard_map/ppermute | solution.py:583
  56.4 0.4 collective-permute-start.16
  56.7 0.6 collective-permute-start.15
  57.3 1.3 %collective-permute-done.17.refs_2_ = f32[4,8,384]{2,1,0:T(8,128)S(1)} collective-permute-done((f32[4,8,384]{2,1,0:T(8,128)S(1)}, f32[4,8,384]{2,1,0:T(8,128)S(1)}, u32[]{:S(2)}, u32[]{:S(2)}) %collective-permute-start.17) | collective-permute-done | bytes 49184 | tf_op jit(solution)/shard_map/ppermute | solution.py:583
  58.6 2.2 %collective-permute-done.16.refs_1_ = f32[4,8,384]{2,1,0:T(8,128)S(1)} collective-permute-done((f32[4,8,384]{2,1,0:T(8,128)S(1)}, f32[4,8,384]{2,1,0:T(8,128)S(1)}, u32[]{:S(2)}, u32[]{:S(2)}) %collective-permute-start.16) | collective-permute-done | bytes 49184 | tf_op jit(solution)/shard_map/ppermute | solution.py:583
  60.9 0.0 collective-permute-done.15.refs_0_
  60.9 0.1 shard_map.83
  61.0 0.4 collective-permute-start.18
  61.4 0.9 %collective-permute-done.18.other = f32[4,8,384]{2,1,0:T(8,128)S(1)} collective-permute-done((f32[4,8,384]{2,1,0:T(8,128)S(1)}, f32[4,8,384]{2,1,0:T(8,128)S(1)}, u32[]{:S(2)}, u32[]{:S(2)}) %collective-permute-start.18) | collective-permute-done | bytes 49184 | tf_op jit(solution)/shard_map/ppermute | solution.py:583
  62.3 1.4 %shard_map.84 = f32[32,32,384]{2,1,0:T(8,128)} custom-call(f32[4,8,384]{2,1,0:T(8,128)S(1)} %get-tuple-element.86.own, f32[4,8,384]{2,1,0:T(8,128)S(1)} %collective-permute-done.18.other, f32[32,32,384]{2,1,0:T(8,128)S(1)} %get-tuple-element.50.g_ref, f32[32,32,384]{2,1,0:T(8,128)S(1)} %get-tuple-element.51.r_ref, ...), custom_call_target="tpu_custom_call" | custom-call | flops 2000000 | bytes 3000000 | tf_op jit(solution)/shard_map/pallas_call | solution.py:572
  (1 shorter events, 0.0 us)
Async XLA Ops:
  2.3 9.2 %collective-permute-start.1 = (f32[5,32,384]{2,1,0:T(8,128)S(1)}, f32[5,32,384]{2,1,0:T(8,128)S(1)}, u32[]{:S(2)}, u32[]{:S(2)}) collective-permute-start(f32[5,32,384]{2,1,0:T(8,128)S(1)} %get-tuple-element.47.own_lo), channel_id=1, source_target_pairs={{32,0},{64,32},{96,64},{0,96},{33,1},{65,33},{97,65},{1,97},{34,2}... | collective-permute-start | bytes 737288 | tf_op jit(solution)/shard_map/ppermute | solution.py:605
  5.7 7.7 %collective-permute-start = (f32[5,32,384]{2,1,0:T(8,128)S(1)}, f32[5,32,384]{2,1,0:T(8,128)S(1)}, u32[]{:S(2)}, u32[]{:S(2)}) collective-permute-start(f32[5,32,384]{2,1,0:T(8,128)S(1)} %get-tuple-element.48.own_hi), channel_id=1, source_target_pairs={{0,32},{32,64},{64,96},{96,0},{1,33},{33,65},{65,97},{97,1},{2,34}... | collective-permute-start | bytes 737288 | tf_op jit(solution)/shard_map/ppermute | solution.py:604
  5.7 5.8 %collective-permute-start.2 = (f32[32,384]{1,0:T(8,128)S(1)}, f32[32,384]{1,0:T(8,128)S(1)}, u32[]{:S(2)}, u32[]{:S(2)}) collective-permute-start(f32[32,384]{1,0:T(8,128)S(1)} %get-tuple-element.55), channel_id=1, source_target_pairs={{1,0},{2,1},{3,2},{4,3},{5,4},{6,5},{7,6},{8,7},{9,8},{10,9},{11,1... | collective-permute-start | bytes 147464 | tf_op jit(solution)/shard_map/ppermute | solution.py:606
  14.3 4.9 %collective-permute-start.3 = (f32[11,8,384]{2,1,0:T(8,128)S(1)}, f32[11,8,384]{2,1,0:T(8,128)S(1)}, u32[]{:S(2)}, u32[]{:S(2)}) collective-permute-start(f32[11,8,384]{2,1,0:T(8,128)S(1)} %get-tuple-element.57), channel_id=1, source_target_pairs={{0,1},{1,0},{2,3},{3,2},{4,5},{5,4},{6,7},{7,6},{8,9},{9,8},{10,11... | collective-permute-start | bytes 405512 | tf_op jit(solution)/shard_map/ppermute | solution.py:583
  19.2 9.9 %collective-permute-start.6 = (f32[11,8,384]{2,1,0:T(8,128)S(1)}, f32[11,8,384]{2,1,0:T(8,128)S(1)}, u32[]{:S(2)}, u32[]{:S(2)}) collective-permute-start(f32[11,8,384]{2,1,0:T(8,128)S(1)} %get-tuple-element.63.mine), channel_id=1, source_target_pairs={{0,7},{1,6},{2,5},{3,4},{4,3},{5,2},{6,1},{7,0},{8,15},{9,14},{10,... | collective-permute-start | bytes 405512 | tf_op jit(solution)/shard_map/ppermute | solution.py:583
  21.4 7.7 %collective-permute-start.5 = (f32[11,8,384]{2,1,0:T(8,128)S(1)}, f32[11,8,384]{2,1,0:T(8,128)S(1)}, u32[]{:S(2)}, u32[]{:S(2)}) collective-permute-start(f32[11,8,384]{2,1,0:T(8,128)S(1)} %get-tuple-element.63.mine), channel_id=1, source_target_pairs={{0,4},{1,5},{2,6},{3,7},{4,0},{5,1},{6,2},{7,3},{8,12},{9,13},{10,... | collective-permute-start | bytes 405512 | tf_op jit(solution)/shard_map/ppermute | solution.py:583
  21.4 8.2 %collective-permute-start.4 = (f32[11,8,384]{2,1,0:T(8,128)S(1)}, f32[11,8,384]{2,1,0:T(8,128)S(1)}, u32[]{:S(2)}, u32[]{:S(2)}) collective-permute-start(f32[11,8,384]{2,1,0:T(8,128)S(1)} %get-tuple-element.63.mine), channel_id=1, source_target_pairs={{0,3},{1,2},{2,1},{3,0},{4,7},{5,6},{6,5},{7,4},{8,11},{9,10},{10,... | collective-permute-start | bytes 405512 | tf_op jit(solution)/shard_map/ppermute | solution.py:583
  29.8 9.6 %collective-permute-start.9 = (f32[11,8,384]{2,1,0:T(8,128)S(1)}, f32[11,8,384]{2,1,0:T(8,128)S(1)}, u32[]{:S(2)}, u32[]{:S(2)}) collective-permute-start(f32[11,8,384]{2,1,0:T(8,128)S(1)} %get-tuple-element.64.mine), channel_id=1, source_target_pairs={{0,25},{1,24},{2,27},{3,26},{4,29},{5,28},{6,31},{7,30},{8,17},{9,... | collective-permute-start | bytes 405512 | tf_op jit(solution)/shard_map/ppermute | solution.py:583
  32.4 7.1 %collective-permute-start.8 = (f32[11,8,384]{2,1,0:T(8,128)S(1)}, f32[11,8,384]{2,1,0:T(8,128)S(1)}, u32[]{:S(2)}, u32[]{:S(2)}) collective-permute-start(f32[11,8,384]{2,1,0:T(8,128)S(1)} %get-tuple-element.64.mine), channel_id=1, source_target_pairs={{0,16},{1,17},{2,18},{3,19},{4,20},{5,21},{6,22},{7,23},{8,24},{9,... | collective-permute-start | bytes 405512 | tf_op jit(solution)/shard_map/ppermute | solution.py:583
  32.7 7.2 %collective-permute-start.7 = (f32[11,8,384]{2,1,0:T(8,128)S(1)}, f32[11,8,384]{2,1,0:T(8,128)S(1)}, u32[]{:S(2)}, u32[]{:S(2)}) collective-permute-start(f32[11,8,384]{2,1,0:T(8,128)S(1)} %get-tuple-element.64.mine), channel_id=1, source_target_pairs={{0,9},{1,8},{2,11},{3,10},{4,13},{5,12},{6,15},{7,14},{8,1},{9,0},... | collective-permute-start | bytes 405512 | tf_op jit(solution)/shard_map/ppermute | solution.py:583
  40.2 1.3 %collective-permute-start.10 = (f32[5,8,384]{2,1,0:T(8,128)S(1)}, f32[5,8,384]{2,1,0:T(8,128)S(1)}, u32[]{:S(2)}, u32[]{:S(2)}) collective-permute-start(f32[5,8,384]{2,1,0:T(8,128)S(1)} %get-tuple-element.72), channel_id=1, source_target_pairs={{0,1},{1,0},{2,3},{3,2},{4,5},{5,4},{6,7},{7,6},{8,9},{9,8},{10,11... | collective-permute-start | bytes 184328 | tf_op jit(solution)/shard_map/ppermute | solution.py:583
  44.1 1.3 %collective-permute-start.11 = (f32[4,8,384]{2,1,0:T(8,128)S(1)}, f32[4,8,384]{2,1,0:T(8,128)S(1)}, u32[]{:S(2)}, u32[]{:S(2)}) collective-permute-start(f32[4,8,384]{2,1,0:T(8,128)S(1)} %get-tuple-element.80), channel_id=1, source_target_pairs={{0,1},{1,0},{2,3},{3,2},{4,5},{5,4},{6,7},{7,6},{8,9},{9,8},{10,11... | collective-permute-start | bytes 147464 | tf_op jit(solution)/shard_map/ppermute | solution.py:583
  45.4 4.9 %collective-permute-start.14 = (f32[4,8,384]{2,1,0:T(8,128)S(1)}, f32[4,8,384]{2,1,0:T(8,128)S(1)}, u32[]{:S(2)}, u32[]{:S(2)}) collective-permute-start(f32[4,8,384]{2,1,0:T(8,128)S(1)} %get-tuple-element.81.mine), channel_id=1, source_target_pairs={{0,7},{1,6},{2,5},{3,4},{4,3},{5,2},{6,1},{7,0},{8,15},{9,14},{10,... | collective-permute-start | bytes 147464 | tf_op jit(solution)/shard_map/ppermute | solution.py:583
  48.2 4.4 %collective-permute-start.13 = (f32[4,8,384]{2,1,0:T(8,128)S(1)}, f32[4,8,384]{2,1,0:T(8,128)S(1)}, u32[]{:S(2)}, u32[]{:S(2)}) collective-permute-start(f32[4,8,384]{2,1,0:T(8,128)S(1)} %get-tuple-element.81.mine), channel_id=1, source_target_pairs={{0,4},{1,5},{2,6},{3,7},{4,0},{5,1},{6,2},{7,3},{8,12},{9,13},{10,... | collective-permute-start | bytes 147464 | tf_op jit(solution)/shard_map/ppermute | solution.py:583
  48.2 4.4 %collective-permute-start.12 = (f32[4,8,384]{2,1,0:T(8,128)S(1)}, f32[4,8,384]{2,1,0:T(8,128)S(1)}, u32[]{:S(2)}, u32[]{:S(2)}) collective-permute-start(f32[4,8,384]{2,1,0:T(8,128)S(1)} %get-tuple-element.81.mine), channel_id=1, source_target_pairs={{0,3},{1,2},{2,1},{3,0},{4,7},{5,6},{6,5},{7,4},{8,11},{9,10},{10,... | collective-permute-start | bytes 147464 | tf_op jit(solution)/shard_map/ppermute | solution.py:583
  52.7 6.0 %collective-permute-start.17 = (f32[4,8,384]{2,1,0:T(8,128)S(1)}, f32[4,8,384]{2,1,0:T(8,128)S(1)}, u32[]{:S(2)}, u32[]{:S(2)}) collective-permute-start(f32[4,8,384]{2,1,0:T(8,128)S(1)} %get-tuple-element.82.mine), channel_id=1, source_target_pairs={{0,25},{1,24},{2,27},{3,26},{4,29},{5,28},{6,31},{7,30},{8,17},{9,... | collective-permute-start | bytes 147464 | tf_op jit(solution)/shard_map/ppermute | solution.py:583
  56.4 4.5 %collective-permute-start.16 = (f32[4,8,384]{2,1,0:T(8,128)S(1)}, f32[4,8,384]{2,1,0:T(8,128)S(1)}, u32[]{:S(2)}, u32[]{:S(2)}) collective-permute-start(f32[4,8,384]{2,1,0:T(8,128)S(1)} %get-tuple-element.82.mine), channel_id=1, source_target_pairs={{0,16},{1,17},{2,18},{3,19},{4,20},{5,21},{6,22},{7,23},{8,24},{9,... | collective-permute-start | bytes 147464 | tf_op jit(solution)/shard_map/ppermute | solution.py:583
  56.7 4.1 %collective-permute-start.15 = (f32[4,8,384]{2,1,0:T(8,128)S(1)}, f32[4,8,384]{2,1,0:T(8,128)S(1)}, u32[]{:S(2)}, u32[]{:S(2)}) collective-permute-start(f32[4,8,384]{2,1,0:T(8,128)S(1)} %get-tuple-element.82.mine), channel_id=1, source_target_pairs={{0,9},{1,8},{2,11},{3,10},{4,13},{5,12},{6,15},{7,14},{8,1},{9,0},... | collective-permute-start | bytes 147464 | tf_op jit(solution)/shard_map/ppermute | solution.py:583
  61.0 1.3 %collective-permute-start.18 = (f32[4,8,384]{2,1,0:T(8,128)S(1)}, f32[4,8,384]{2,1,0:T(8,128)S(1)}, u32[]{:S(2)}, u32[]{:S(2)}) collective-permute-start(f32[4,8,384]{2,1,0:T(8,128)S(1)} %get-tuple-element.87), channel_id=1, source_target_pairs={{0,1},{1,0},{2,3},{3,2},{4,5},{5,4},{6,7},{7,6},{8,9},{9,8},{10,11... | collective-permute-start | bytes 147464 | tf_op jit(solution)/shard_map/ppermute | solution.py:583

commit v3 on v2

--- a/solution.py
+++ b/solution.py
@@ -14,7 +14,7 @@
 CHUNK = 8
 PLANES = 5
 JOIN_COEFS = 9
-ORDER = (1, 2, 3)
+ORDER = (1, 3, 2)
 
 
 def at_vmem(*shape):
@@ -91,7 +91,7 @@
 
 def edge_kernel(
     slab, cols,
-    diff_table, uptake_table, conc_hbm, mask_hbm, layer_hbm, stiff_hbm, prod_hbm,
+    diff_table, conc_hbm, mask_hbm, layer_hbm, stiff_hbm,
     lo_out, hi_out, first_out,
     mask, layer, floats, mask_row, layer_row, stiff_row, sems, row_sems,
 ):
@@ -102,7 +102,6 @@
             x = depth if side == 0 else slab - 1 - depth
             sources += [(mask_hbm.at[:, x], mask.at[side, depth]), (layer_hbm.at[:, x], layer.at[side, depth]),
                         (stiff_hbm.at[:, x], floats.at[side, depth]), (conc_hbm.at[:, x], floats.at[side, 2 + depth])]
-        sources.append((prod_hbm.at[:, 0 if side == 0 else slab - 1], floats.at[side, 4]))
         copies.append([
             pltpu.make_async_copy(source, target, sems.at[side, k]) for k, (source, target) in enumerate(sources)])
     copies.append([
@@ -111,7 +110,7 @@
     for group in copies:
         for copy in group:
             copy.start()
-    table, uptakes = read_table(diff_table), read_table(uptake_table)
+    table = read_table(diff_table)
     for side, out in ((0, lo_out), (1, hi_out)):
         for copy in copies[side]:
             copy.wait()
@@ -119,12 +118,9 @@
         state = floats[side, 2]
         ssum = inner + along_cols(s)
         vsum = inner * floats[side, 3] + along_cols(s * state)
-        weight = mask[side, 0].astype(jnp.float32)
         out[0] = s
         out[1] = state
         out[2] = state + SECTION_RATE * s * (vsum - state * ssum)
-        out[3] = 1.0 - weight * lookup(layer[side, 0], uptakes)
-        out[4] = weight * floats[side, 4]
     for copy in copies[2]:
         copy.wait()
     first_out[...] = root_diffusivity(mask_row[...], layer_row[...], stiff_row[...], table)
@@ -132,28 +128,13 @@
 
 def setup_kernel(
     rows, slab, cols,
-    table, conc_hbm, mask_hbm, layer_hbm, stiff_hbm,
+    table, conc, mask, layer, stiff,
     s_out, g_out, r_out, gp_out, ssum_out, part_out, ends_out,
-    conc, mask, layer, stiff, sems,
 ):
-    pairs = ((mask_hbm, mask), (layer_hbm, layer), (stiff_hbm, stiff), (conc_hbm, conc))
-    copies = []
-    for chunk in range(rows // CHUNK):
-        here = pl.ds(chunk * CHUNK, CHUNK)
-        copies.append([
-            pltpu.make_async_copy(source.at[here], target.at[here], sems.at[k, chunk])
-            for k, (source, target) in enumerate(pairs)
-        ])
-    for group in copies:
-        for copy in group:
-            copy.start()
     weights = read_table(table)
     grid = [(t, c) for t in range(slab // 8) for c in range(cols // 128)]
     s = m = gp = alpha = None
     for z in range(rows):
-        if z % CHUNK == 0:
-            for copy in copies[z // CHUNK]:
-                copy.wait()
         w, lab, sti, st = [tiles_of(ref, z, slab, cols) for ref in (mask, layer, stiff, conc)]
         s_next = [[root_diffusivity(w[t][c], lab[t][c], sti[t][c], weights)
                    for c in range(cols // 128)] for t in range(slab // 8)]
@@ -188,25 +169,18 @@
         ends_out[(1,) + here] = alpha[t, c]
 
 
-def reaction_kernel(rows, uptake_table, mask_hbm, layer_hbm, prod_hbm, keep_out, source_out, mask, layer, prod, sems):
-    copies = []
-    for chunk in range(rows // CHUNK):
-        here = pl.ds(chunk * CHUNK, CHUNK)
-        copies.append([
-            pltpu.make_async_copy(source.at[here], target.at[here], sems.at[k, chunk])
-            for k, (source, target) in enumerate(((mask_hbm, mask), (layer_hbm, layer), (prod_hbm, prod)))
-        ])
-    for group in copies:
-        for copy in group:
-            copy.start()
+def reaction_kernel(rows, uptake_table, mask, layer, prod, keep_out, source_out, lo_out, hi_out):
     tab = read_table(uptake_table)
     for z in range(rows):
-        if z % CHUNK == 0:
-            for copy in copies[z // CHUNK]:
-                copy.wait()
         weight = mask[z].astype(jnp.float32)
-        keep_out[z] = 1.0 - weight * lookup(layer[z], tab)
-        source_out[z] = weight * prod[z]
+        keep = 1.0 - weight * lookup(layer[z], tab)
+        source = weight * prod[z]
+        keep_out[z] = keep
+        source_out[z] = source
+        lo_out[0, z:z + 1] = keep[0:1]
+        lo_out[1, z:z + 1] = source[0:1]
+        hi_out[0, z:z + 1] = keep[-1:]
+        hi_out[1, z:z + 1] = source[-1:]
 
 
 def tile_of(tiles, k):
@@ -241,8 +215,6 @@
         lines[side, 1] = halo[2] - flux
         lines[side, 2] = RZ * s * pltpu.roll(s, rows - 1, 0)
         lines[side, 3] = flux
-        lines[side, 4] = halo[3]
-        lines[side, 5] = halo[4]
 
     row = lax.broadcasted_iota(jnp.int32, (8, cols), 0)
     is_lo = row == 7
@@ -281,7 +253,7 @@
         grb = gpb * rb
         ab = grb * gpb if z == 0 else ab + grb * gpb
         pb = grb * eb if z == 0 else pb + grb * eb
-        for k, value in enumerate((sb, gb, rb, gpb, fb, border(4, z), border(5, z))):
+        for k, value in enumerate((sb, gb, rb, gpb, fb)):
             border_ref[k, z] = value
     ports_ref[0] = total
     ports_ref[1] = last_g * prev
@@ -316,7 +288,8 @@
 
 
 def ordered(index, mine, received):
-    return [pick(index ^ j, [mine] + received) for j in range(1 + len(received))]
+    options = [mine] + [received[ORDER.index(step)] for step in range(1, 1 + len(received))] if len(received) > 1 else [mine, *received]
+    return [pick(index ^ j, options) for j in range(1 + len(received))]
 
 
 def main_planes(stack, planes):
@@ -493,6 +466,7 @@
 def middle_kernel(
     rows, slab, cols,
     own, other, s_ref, g_ref, r_ref, gp_ref, fwd_in, last_ref, keep_ref, source_ref, ssum_ref, border_ref,
+    reaction_lo, reaction_hi,
     fwd_ref, mine_ref, send_ref, ports_ref,
 ):
     q, u = whole_ports(own, other)
@@ -510,7 +484,8 @@
         g = g_ref[z] if z < rows - 1 else last_ref[0]
         u = r * (fwd_in[z] + gp_ref[z] * inflow) + g * u
         state = source_ref[z] + keep_ref[z] * u
-        sb, gb, rb, gpb, fb, keep_b, source_b = [border_ref[k, z] for k in range(7)]
+        sb, gb, rb, gpb, fb = [border_ref[k, z] for k in range(5)]
+        keep_b, source_b = [jnp.where(row == 7, reaction_lo[k, z:z + 1], reaction_hi[k, z:z + 1]) for k in (0, 1)]
         rhs = fb + gpb * inflow_b
         ub = rb * (rhs + top_b) if z == rows - 1 else rb * rhs + gb * ub
         flow_b = split_cols(sb * (source_b + keep_b * ub))
@@ -581,7 +556,7 @@
 
     def exchange(block, stage):
         received = {step: lax.ppermute(block, "ax", route) for step, route in partners[stage]}
-        return [received[step] for step in sorted(received)]
+        return [received[step] for step, _ in partners[stage]]
 
     def f32(*shape):
         return pltpu.VMEM(shape, jnp.float32)
@@ -589,37 +564,39 @@
     def i32(*shape):
         return pltpu.VMEM(shape, jnp.int32)
 
-    conc, mask, layer, stiff, prod = [
-        in_hbm(x) for x in (concentration, tissue_mask, wall_layer, stiffness, production)]
+    conc, mask, layer, stiff = [
+        in_hbm(x) for x in (concentration, tissue_mask, wall_layer, stiffness)]
     diff_table, uptake_rate = in_hbm(layer_diffusivity), in_hbm(uptake_rate)
     lo, hi, first_s = call(
         functools.partial(edge_kernel, slab, cols),
-        [at_vmem(5, rows, cols), at_vmem(5, rows, cols), at_vmem(slab, cols)],
-        [diff_table, uptake_rate, conc, mask, layer, stiff, prod],
-        scratch=[i32(2, 2, rows, cols), i32(2, 2, rows, cols), f32(2, 5, rows, cols),
+        [at_vmem(3, rows, cols), at_vmem(3, rows, cols), at_vmem(slab, cols)],
+        [diff_table, conc, mask, layer, stiff],
+        scratch=[i32(2, 2, rows, cols), i32(2, 2, rows, cols), f32(2, 4, rows, cols),
                  i32(slab, cols), i32(slab, cols), f32(slab, cols),
-                 pltpu.SemaphoreType.DMA((2, 9)), pltpu.SemaphoreType.DMA((3,))],
-        specs=[smem, smem] + [hbm] * 5,
-    )
-    from_lo = lax.ppermute(hi, "xs", [(i, (i + 1) % nx) for i in range(nx)])
-    from_hi = lax.ppermute(lo, "xs", [((i + 1) % nx, i) for i in range(nx)])
+                 pltpu.SemaphoreType.DMA((2, 8)), pltpu.SemaphoreType.DMA((3,))],
+        specs=[smem] + [hbm] * 4,
+    )
+    def from_neighbours(lo, hi):
+        return (lax.ppermute(hi, "xs", [(i, (i + 1) % nx) for i in range(nx)]),
+                lax.ppermute(lo, "xs", [((i + 1) % nx, i) for i in range(nx)]))
+
+    from_lo, from_hi = from_neighbours(lo, hi)
     above_s = lax.ppermute(first_s, "ax", [((i + 1) % nax, i) for i in range(nax)])
 
     s, g, r, gp, ssum, part, ends = call(
         functools.partial(setup_kernel, rows, slab, cols),
         [at_vmem(*block)] * 6 + [at_vmem(2, slab, cols)],
-        [diff_table, conc, mask, layer, stiff],
-        scratch=[f32(*block), i32(*block), i32(*block), f32(*block), pltpu.SemaphoreType.DMA((4, rows // CHUNK))],
-        specs=[smem] + [hbm] * 4,
+        [diff_table, concentration, tissue_mask, wall_layer, stiffness],
+        specs=[smem] + [vspec()] * 4,
         us=5.0,
     )
     stack, pair = 2 * PLANES + 1, (5, 8, cols)
     fwd, last, mine, send, border = call(
         functools.partial(first_forward_kernel, rows, slab, cols, nx, nax),
         [at_vmem(*block), at_vmem(2, slab, cols), at_vmem(stack, 8, cols), at_vmem(stack, 8, cols),
-         at_vmem(7, rows, 8, cols)],
+         at_vmem(5, rows, 8, cols)],
         [lo, hi, s, g, r, gp, part, ends, from_lo, from_hi, above_s],
-        scratch=[f32(PLANES, slab, cols), f32(2, 8, cols), f32(2, 6, rows, cols)],
+        scratch=[f32(PLANES, slab, cols), f32(2, 8, cols), f32(2, 4, rows, cols)],
     )
     levs, values, border_levs = [], [], []
     for stage in (0, 1):
@@ -627,14 +604,14 @@
         joins = len(received)
         if stage == 1:
             uptake_late, mine = lax.optimization_barrier((uptake_rate, mine))
-            keep, source = call(
+            keep, source, lo, hi = call(
                 functools.partial(reaction_kernel, rows),
-                [at_vmem(*block)] * 2,
-                [uptake_late, mask, layer, prod],
-                scratch=[i32(*block), i32(*block), f32(*block), pltpu.SemaphoreType.DMA((3, rows // CHUNK))],
-                specs=[smem] + [hbm] * 3,
+                [at_vmem(*block)] * 2 + [at_vmem(2, rows, cols)] * 2,
+                [uptake_late, tissue_mask, wall_layer, production],
+                specs=[smem] + [vspec()] * 3,
                 us=2.0,
             )
+            reaction_lo, reaction_hi = from_neighbours(lo, hi)
             mine, keep, source = lax.optimization_barrier((mine, keep, source))
         mine, lev, value, border_lev = call(
             functools.partial(first_join_kernel, stage, joins),
@@ -659,7 +636,7 @@
     fwd, mine, send = call(
         functools.partial(middle_kernel, rows, slab, cols),
         [at_vmem(*block), at_vmem(4, 8, cols), at_vmem(4, 8, cols)],
-        [own, other, s, g, r, gp, fwd, last, keep, source, ssum, border],
+        [own, other, s, g, r, gp, fwd, last, keep, source, ssum, border, reaction_lo, reaction_hi],
         scratch=[f32(2, slab, cols)],
         us=3.0,
     )

time: 64 us -> 60.9 us (0.952)
  Pallas kernels: 15.9 us -> 12.4 us
  waiting for transfers between devices: 22.1 us -> 23 us
    pallas_call x12, Pallas kernels: 15.9 us -> 12.4 us  [call(): pl.pallas_call(kernel, out_shape=outs, in_specs=specs or [vspec()] * len(...]
    ppermute x16, starting transfers between devices: 21.3 us -> 18.2 us  [exchange(): lax.ppermute(block, 'ax', route)]
    ppermute x2 -> x4, starting transfers between devices: 3.38 us -> 6.06 us  [the longest x2 5.88 us: from_neighbours(): lax.ppermute(lo, 'xs', [((i + 1) % nx, i) for i in range(nx)])]
    ppermute x16, waiting for transfers between devices: 20.2 us -> 21.6 us  [exchange(): lax.ppermute(block, 'ax', route)]
    ppermute x2 -> x4, waiting for transfers between devices: 1.87 us -> 1.36 us  [the longest x2 1.35 us: from_neighbours(): lax.ppermute(hi, 'xs', [(i, (i + 1) % nx) for i in range(nx)])]
  transfers between devices with their start and end apart: 19 -> 21, of which waited for: 13 -> 13; matrix products, arithmetic and copies ran while one was open for 0% -> 0% of each run, Pallas kernels for 13% -> 8%
where the time goes in v3:
time: 60.9 us; the launch traced here: 60.8 us
  starting transfers between devices  25.3 us (42%)
  waiting for transfers between devices  23 us (38%)
  Pallas kernels  12.4 us (20%)
    ppermute x16, waiting for transfers between devices, exchange(): lax.ppermute(block, 'ax', route)  21.6 us
    ppermute x16, starting transfers between devices, exchange(): lax.ppermute(block, 'ax', route)  18.2 us
    pallas_call x12, Pallas kernels, call(): pl.pallas_call(kernel, out_shape=outs, in_specs=specs or [vspec()] * len(...  12.4 us
    ppermute x2, starting transfers between devices, from_neighbours(): lax.ppermute(lo, 'xs', [((i + 1) % nx, i) for i in range(nx)])  5.88 us
    ppermute x2, waiting for transfers between devices, from_neighbours(): lax.ppermute(hi, 'xs', [(i, (i + 1) % nx) for i in range(nx)])  1.35 us
  transfers between devices with their start and end apart: 21, of which 13 were waited for; matrix products, arithmetic and copies ran while one was open for 0% of the time, Pallas kernels for 8%

profile of v3, /device:TPU:1, one launch (start us, length us, event | category | flops | bytes accessed | tf_op | source)
XLA Modules:
  0.0 60.8 jit_solution(12712569501764520586)
XLA Ops:
  0.0 0.0 copy-start.1
  0.0 0.0 copy-start
  0.0 0.0 copy-start.3
  0.0 0.0 copy-start.2
  0.0 2.8 %shard_map.73 = (f32[3,32,384]{2,1,0:T(8,128)S(1)}, f32[3,32,384]{2,1,0:T(8,128)S(1)}, f32[32,384]{1,0:T(8,128)S(1)}) custom-call(f32[4]{0:T(128)} %table.1, f32[32,32,384]{2,1,0:T(8,128)} %conc.1, s32[32,32,384]{2,1,0:T(8,128)} %mask.3, s32[32,32,384]{2,1,0:T(8,128)} %layer.3, f32[32,32,384]{2,1,0:T(8,128)} %stiff.1), custom_call_target="tpu_custom_call" | custom-call | flops 2000000 | bytes 3000000 | tf_op jit(solution)/shard_map/pallas_call | solution.py:547
  2.8 3.4 %collective-permute-start.1 = (f32[3,32,384]{2,1,0:T(8,128)S(1)}, f32[3,32,384]{2,1,0:T(8,128)S(1)}, u32[]{:S(2)}, u32[]{:S(2)}) collective-permute-start(f32[3,32,384]{2,1,0:T(8,128)S(1)} %get-tuple-element.49.own_lo), channel_id=1, source_target_pairs={{32,0},{64,32},{96,64},{0,96},{33,1},{65,33},{97,65},{1,97},{34,2}... | collective-permute-start | bytes 442376 | tf_op jit(solution)/shard_map/ppermute | solution.py:581
  6.2 0.0 collective-permute-start
  6.2 1.0 %collective-permute-start.2 = (f32[32,384]{1,0:T(8,128)S(1)}, f32[32,384]{1,0:T(8,128)S(1)}, u32[]{:S(2)}, u32[]{:S(2)}) collective-permute-start(f32[32,384]{1,0:T(8,128)S(1)} %get-tuple-element.57), channel_id=1, source_target_pairs={{1,0},{2,1},{3,2},{4,3},{5,4},{6,5},{7,6},{8,7},{9,8},{10,9},{11,1... | collective-permute-start | bytes 147464 | tf_op jit(solution)/shard_map/ppermute | solution.py:584
  7.1 0.0 copy-done.1
  7.1 0.0 copy-done
  7.1 0.0 copy-done.3
  7.1 0.0 copy-done.2
  7.1 3.2 %shard_map.74 = (f32[32,32,384]{2,1,0:T(8,128)S(1)}, f32[32,32,384]{2,1,0:T(8,128)S(1)}, f32[32,32,384]{2,1,0:T(8,128)S(1)}, f32[32,32,384]{2,1,0:T(8,128)S(1)},...) custom-call(f32[4]{0:T(128)} %table.1, f32[32,32,384]{2,1,0:T(8,128)S(1)} %copy-done.2, ...), custom_call_target="tpu_custom_call" | custom-call | flops 10000000 | bytes 15000000 | tf_op jit(solution)/shard_map/pallas_call | solution.py:547
  10.4 0.0 collective-permute-done.2.above_ref
  10.4 0.0 collective-permute-done.1.from_hi
  10.4 1.4 %collective-permute-done.from_lo = f32[3,32,384]{2,1,0:T(8,128)S(1)} collective-permute-done((f32[3,32,384]{2,1,0:T(8,128)S(1)}, f32[3,32,384]{2,1,0:T(8,128)S(1)}, u32[]{:S(2)}, u32[]{:S(2)}) %collective-permute-start) | collective-permute-done | bytes 147488 | tf_op jit(solution)/shard_map/ppermute | solution.py:580
  11.8 0.0 copy-start.4
  11.8 0.7 %shard_map.75 = (f32[32,32,384]{2,1,0:T(8,128)S(1)}, f32[2,32,384]{2,1,0:T(8,128)S(1)}, f32[11,8,384]{2,1,0:T(8,128)S(1)}, f32[11,8,384]{2,1,0:T(8,128)S(1)}, f32[5,32,8,384]{3,2,1,0:T(8,128)S(1)}) custom-call(f32[3,32,384]{2,1,0:T(8,128)S(1)} %get-tuple-element.49.own_lo, f32[3,32,384]{2,1,0:T(8,128)S(1)} %get-tuple-element.50.own_hi, ...), custom_call_target="tpu_custom_call" | custom-call | flops 2000000 | bytes 3000000 | tf_op jit(solution)/shard_map/pallas_call | solution.py:547
  12.5 4.4 %collective-permute-start.3 = (f32[11,8,384]{2,1,0:T(8,128)S(1)}, f32[11,8,384]{2,1,0:T(8,128)S(1)}, u32[]{:S(2)}, u32[]{:S(2)}) collective-permute-start(f32[11,8,384]{2,1,0:T(8,128)S(1)} %get-tuple-element.59), channel_id=1, source_target_pairs={{0,1},{1,0},{2,3},{3,2},{4,5},{5,4},{6,7},{7,6},{8,9},{9,8},{10,11... | collective-permute-start | bytes 405512 | tf_op jit(solution)/shard_map/ppermute | solution.py:558
  16.8 1.0 %collective-permute-done.3.refs_0_ = f32[11,8,384]{2,1,0:T(8,128)S(1)} collective-permute-done((f32[11,8,384]{2,1,0:T(8,128)S(1)}, f32[11,8,384]{2,1,0:T(8,128)S(1)}, u32[]{:S(2)}, u32[]{:S(2)}) %collective-permute-start.3) | collective-permute-done | bytes 135200 | tf_op jit(solution)/shard_map/ppermute | solution.py:558
  17.8 0.1 shard_map.76
  17.9 1.2 %collective-permute-start.6 = (f32[11,8,384]{2,1,0:T(8,128)S(1)}, f32[11,8,384]{2,1,0:T(8,128)S(1)}, u32[]{:S(2)}, u32[]{:S(2)}) collective-permute-start(f32[11,8,384]{2,1,0:T(8,128)S(1)} %get-tuple-element.65.mine), channel_id=1, source_target_pairs={{0,4},{1,5},{2,6},{3,7},{4,0},{5,1},{6,2},{7,3},{8,12},{9,13},{10,... | collective-permute-start | bytes 405512 | tf_op jit(solution)/shard_map/ppermute | solution.py:558
  19.2 1.0 %collective-permute-start.5 = (f32[11,8,384]{2,1,0:T(8,128)S(1)}, f32[11,8,384]{2,1,0:T(8,128)S(1)}, u32[]{:S(2)}, u32[]{:S(2)}) collective-permute-start(f32[11,8,384]{2,1,0:T(8,128)S(1)} %get-tuple-element.65.mine), channel_id=1, source_target_pairs={{0,7},{1,6},{2,5},{3,4},{4,3},{5,2},{6,1},{7,0},{8,15},{9,14},{10,... | collective-permute-start | bytes 405512 | tf_op jit(solution)/shard_map/ppermute | solution.py:558
  20.1 0.8 %collective-permute-start.4 = (f32[11,8,384]{2,1,0:T(8,128)S(1)}, f32[11,8,384]{2,1,0:T(8,128)S(1)}, u32[]{:S(2)}, u32[]{:S(2)}) collective-permute-start(f32[11,8,384]{2,1,0:T(8,128)S(1)} %get-tuple-element.65.mine), channel_id=1, source_target_pairs={{0,3},{1,2},{2,1},{3,0},{4,7},{5,6},{6,5},{7,4},{8,11},{9,10},{10,... | collective-permute-start | bytes 405512 | tf_op jit(solution)/shard_map/ppermute | solution.py:558
  20.9 0.0 copy-done.4
  20.9 1.3 %shard_map.77 = (f32[32,32,384]{2,1,0:T(8,128)S(1)}, f32[32,32,384]{2,1,0:T(8,128)S(1)}, f32[2,32,384]{2,1,0:T(8,128)S(1)}, f32[2,32,384]{2,1,0:T(8,128)S(1)}) custom-call(f32[4]{0:T(128)} %uptake_table, s32[32,32,384]{2,1,0:T(8,128)S(1)} %copy-done, s32[32,32,384]{2,1,0:T(8,128)S(1)} %copy-done.1, f32[32,32,384]{2,1,0:T(8,128)S(1)} %copy-done.4), custom_call_target="tpu_custom_call" | custom-call | flops 4000000 | bytes 6000000 | tf_op jit(solution)/shard_map/pallas_call | solution.py:547
  22.2 2.1 %collective-permute-done.6.refs_2_ = f32[11,8,384]{2,1,0:T(8,128)S(1)} collective-permute-done((f32[11,8,384]{2,1,0:T(8,128)S(1)}, f32[11,8,384]{2,1,0:T(8,128)S(1)}, u32[]{:S(2)}, u32[]{:S(2)}) %collective-permute-start.6) | collective-permute-done | bytes 135200 | tf_op jit(solution)/shard_map/ppermute | solution.py:558
  24.3 3.7 %collective-permute-done.5.refs_1_ = f32[11,8,384]{2,1,0:T(8,128)S(1)} collective-permute-done((f32[11,8,384]{2,1,0:T(8,128)S(1)}, f32[11,8,384]{2,1,0:T(8,128)S(1)}, u32[]{:S(2)}, u32[]{:S(2)}) %collective-permute-start.5) | collective-permute-done | bytes 135200 | tf_op jit(solution)/shard_map/ppermute | solution.py:558
  28.0 0.0 collective-permute-done.4.refs_0_
  28.0 0.2 shard_map.78
  28.2 1.6 %collective-permute-start.9 = (f32[11,8,384]{2,1,0:T(8,128)S(1)}, f32[11,8,384]{2,1,0:T(8,128)S(1)}, u32[]{:S(2)}, u32[]{:S(2)}) collective-permute-start(f32[11,8,384]{2,1,0:T(8,128)S(1)} %get-tuple-element.66.mine), channel_id=1, source_target_pairs={{0,16},{1,17},{2,18},{3,19},{4,20},{5,21},{6,22},{7,23},{8,24},{9,... | collective-permute-start | bytes 405512 | tf_op jit(solution)/shard_map/ppermute | solution.py:558
  29.9 1.1 %collective-permute-start.8 = (f32[11,8,384]{2,1,0:T(8,128)S(1)}, f32[11,8,384]{2,1,0:T(8,128)S(1)}, u32[]{:S(2)}, u32[]{:S(2)}) collective-permute-start(f32[11,8,384]{2,1,0:T(8,128)S(1)} %get-tuple-element.66.mine), channel_id=1, source_target_pairs={{0,25},{1,24},{2,27},{3,26},{4,29},{5,28},{6,31},{7,30},{8,17},{9,... | collective-permute-start | bytes 405512 | tf_op jit(solution)/shard_map/ppermute | solution.py:558
  31.0 0.2 collective-permute-start.7
  31.2 0.2 collective-permute-start.11
  31.4 2.5 %collective-permute-start.12 = (f32[2,32,384]{2,1,0:T(8,128)S(1)}, f32[2,32,384]{2,1,0:T(8,128)S(1)}, u32[]{:S(2)}, u32[]{:S(2)}) collective-permute-start(f32[2,32,384]{2,1,0:T(8,128)S(1)} %get-tuple-element.82), channel_id=1, source_target_pairs={{32,0},{64,32},{96,64},{0,96},{33,1},{65,33},{97,65},{1,97},{34,2}... | collective-permute-start | bytes 294920 | tf_op jit(solution)/shard_map/ppermute | solution.py:581
  33.9 0.7 %collective-permute-done.9.refs_2_ = f32[11,8,384]{2,1,0:T(8,128)S(1)} collective-permute-done((f32[11,8,384]{2,1,0:T(8,128)S(1)}, f32[11,8,384]{2,1,0:T(8,128)S(1)}, u32[]{:S(2)}, u32[]{:S(2)}) %collective-permute-start.9) | collective-permute-done | bytes 135200 | tf_op jit(solution)/shard_map/ppermute | solution.py:558
  34.6 3.7 %collective-permute-done.8.refs_1_ = f32[11,8,384]{2,1,0:T(8,128)S(1)} collective-permute-done((f32[11,8,384]{2,1,0:T(8,128)S(1)}, f32[11,8,384]{2,1,0:T(8,128)S(1)}, u32[]{:S(2)}, u32[]{:S(2)}) %collective-permute-start.8) | collective-permute-done | bytes 135200 | tf_op jit(solution)/shard_map/ppermute | solution.py:558
  38.3 0.0 collective-permute-done.7.refs_0_
  38.3 0.2 shard_map.79
  38.5 0.5 collective-permute-start.10
  39.0 0.0 collective-permute-done.11.reaction_lo
  39.0 0.0 collective-permute-done.12.reaction_hi
  39.0 0.9 %collective-permute-done.10.other = f32[5,8,384]{2,1,0:T(8,128)S(1)} collective-permute-done((f32[5,8,384]{2,1,0:T(8,128)S(1)}, f32[5,8,384]{2,1,0:T(8,128)S(1)}, u32[]{:S(2)}, u32[]{:S(2)}) %collective-permute-start.10) | collective-permute-done | bytes 61472 | tf_op jit(solution)/shard_map/ppermute | solution.py:558
  39.9 2.3 %shard_map.80 = (f32[32,32,384]{2,1,0:T(8,128)S(1)}, f32[4,8,384]{2,1,0:T(8,128)S(1)}, f32[4,8,384]{2,1,0:T(8,128)S(1)}) custom-call(f32[5,8,384]{2,1,0:T(8,128)S(1)} %get-tuple-element.73.own, f32[5,8,384]{2,1,0:T(8,128)S(1)} %collective-permute-done.10.other, f32[32,32,384]{2,1,0:T(8,128)S(1)} %get-tuple-element.51.s_ref, ...), custom_call_target="tpu_custom_call" | custom-call | flops 6000000 | bytes 9000000 | tf_op jit(solution)/shard_map/pallas_call | solution.py:547
  42.2 0.4 collective-permute-start.13
  42.6 0.9 %collective-permute-done.13.refs_0_ = f32[4,8,384]{2,1,0:T(8,128)S(1)} collective-permute-done((f32[4,8,384]{2,1,0:T(8,128)S(1)}, f32[4,8,384]{2,1,0:T(8,128)S(1)}, u32[]{:S(2)}, u32[]{:S(2)}) %collective-permute-start.13) | collective-permute-done | bytes 49184 | tf_op jit(solution)/shard_map/ppermute | solution.py:558
  43.6 1.2 %collective-permute-start.16 = (f32[4,8,384]{2,1,0:T(8,128)S(1)}, f32[4,8,384]{2,1,0:T(8,128)S(1)}, u32[]{:S(2)}, u32[]{:S(2)}) collective-permute-start(f32[4,8,384]{2,1,0:T(8,128)S(1)} %get-tuple-element.85.mine), channel_id=1, source_target_pairs={{0,4},{1,5},{2,6},{3,7},{4,0},{5,1},{6,2},{7,3},{8,12},{9,13},{10,... | collective-permute-start | bytes 147464 | tf_op jit(solution)/shard_map/ppermute | solution.py:558
  44.8 1.0 %collective-permute-start.15 = (f32[4,8,384]{2,1,0:T(8,128)S(1)}, f32[4,8,384]{2,1,0:T(8,128)S(1)}, u32[]{:S(2)}, u32[]{:S(2)}) collective-permute-start(f32[4,8,384]{2,1,0:T(8,128)S(1)} %get-tuple-element.85.mine), channel_id=1, source_target_pairs={{0,7},{1,6},{2,5},{3,4},{4,3},{5,2},{6,1},{7,0},{8,15},{9,14},{10,... | collective-permute-start | bytes 147464 | tf_op jit(solution)/shard_map/ppermute | solution.py:558
  45.8 0.7 %collective-permute-start.14 = (f32[4,8,384]{2,1,0:T(8,128)S(1)}, f32[4,8,384]{2,1,0:T(8,128)S(1)}, u32[]{:S(2)}, u32[]{:S(2)}) collective-permute-start(f32[4,8,384]{2,1,0:T(8,128)S(1)} %get-tuple-element.85.mine), channel_id=1, source_target_pairs={{0,3},{1,2},{2,1},{3,0},{4,7},{5,6},{6,5},{7,4},{8,11},{9,10},{10,... | collective-permute-start | bytes 147464 | tf_op jit(solution)/shard_map/ppermute | solution.py:558
  46.6 1.5 %collective-permute-done.16.refs_2_ = f32[4,8,384]{2,1,0:T(8,128)S(1)} collective-permute-done((f32[4,8,384]{2,1,0:T(8,128)S(1)}, f32[4,8,384]{2,1,0:T(8,128)S(1)}, u32[]{:S(2)}, u32[]{:S(2)}) %collective-permute-start.16) | collective-permute-done | bytes 49184 | tf_op jit(solution)/shard_map/ppermute | solution.py:558
  48.1 2.1 %collective-permute-done.15.refs_1_ = f32[4,8,384]{2,1,0:T(8,128)S(1)} collective-permute-done((f32[4,8,384]{2,1,0:T(8,128)S(1)}, f32[4,8,384]{2,1,0:T(8,128)S(1)}, u32[]{:S(2)}, u32[]{:S(2)}) %collective-permute-start.15) | collective-permute-done | bytes 49184 | tf_op jit(solution)/shard_map/ppermute | solution.py:558
  50.2 0.0 collective-permute-done.14.refs_0_
  50.2 0.1 shard_map.82
  50.3 2.1 %collective-permute-start.19 = (f32[4,8,384]{2,1,0:T(8,128)S(1)}, f32[4,8,384]{2,1,0:T(8,128)S(1)}, u32[]{:S(2)}, u32[]{:S(2)}) collective-permute-start(f32[4,8,384]{2,1,0:T(8,128)S(1)} %get-tuple-element.86.mine), channel_id=1, source_target_pairs={{0,16},{1,17},{2,18},{3,19},{4,20},{5,21},{6,22},{7,23},{8,24},{9,... | collective-permute-start | bytes 147464 | tf_op jit(solution)/shard_map/ppermute | solution.py:558
  52.4 1.3 %collective-permute-start.18 = (f32[4,8,384]{2,1,0:T(8,128)S(1)}, f32[4,8,384]{2,1,0:T(8,128)S(1)}, u32[]{:S(2)}, u32[]{:S(2)}) collective-permute-start(f32[4,8,384]{2,1,0:T(8,128)S(1)} %get-tuple-element.86.mine), channel_id=1, source_target_pairs={{0,25},{1,24},{2,27},{3,26},{4,29},{5,28},{6,31},{7,30},{8,17},{9,... | collective-permute-start | bytes 147464 | tf_op jit(solution)/shard_map/ppermute | solution.py:558
  53.8 0.0 collective-permute-start.17
  53.8 1.1 %collective-permute-done.19.refs_2_ = f32[4,8,384]{2,1,0:T(8,128)S(1)} collective-permute-done((f32[4,8,384]{2,1,0:T(8,128)S(1)}, f32[4,8,384]{2,1,0:T(8,128)S(1)}, u32[]{:S(2)}, u32[]{:S(2)}) %collective-permute-start.19) | collective-permute-done | bytes 49184 | tf_op jit(solution)/shard_map/ppermute | solution.py:558
  54.8 3.1 %collective-permute-done.18.refs_1_ = f32[4,8,384]{2,1,0:T(8,128)S(1)} collective-permute-done((f32[4,8,384]{2,1,0:T(8,128)S(1)}, f32[4,8,384]{2,1,0:T(8,128)S(1)}, u32[]{:S(2)}, u32[]{:S(2)}) %collective-permute-start.18) | collective-permute-done | bytes 49184 | tf_op jit(solution)/shard_map/ppermute | solution.py:558
  57.9 0.0 collective-permute-done.17.refs_0_
  57.9 0.1 shard_map.83
  58.1 0.5 collective-permute-start.20
  58.5 0.9 %collective-permute-done.20.other = f32[4,8,384]{2,1,0:T(8,128)S(1)} collective-permute-done((f32[4,8,384]{2,1,0:T(8,128)S(1)}, f32[4,8,384]{2,1,0:T(8,128)S(1)}, u32[]{:S(2)}, u32[]{:S(2)}) %collective-permute-start.20) | collective-permute-done | bytes 49184 | tf_op jit(solution)/shard_map/ppermute | solution.py:558
  59.4 1.4 %shard_map.84 = f32[32,32,384]{2,1,0:T(8,128)} custom-call(f32[4,8,384]{2,1,0:T(8,128)S(1)} %get-tuple-element.90.own, f32[4,8,384]{2,1,0:T(8,128)S(1)} %collective-permute-done.20.other, f32[32,32,384]{2,1,0:T(8,128)S(1)} %get-tuple-element.52.g_ref, f32[32,32,384]{2,1,0:T(8,128)S(1)} %get-tuple-element.53.r_ref, ...), custom_call_target="tpu_custom_call" | custom-call | flops 2000000 | bytes 3000000 | tf_op jit(solution)/shard_map/pallas_call | solution.py:547
  (1 shorter events, 0.0 us)
Async XLA Ops:
  0.0 7.1 %copy-start.1 = (s32[32,32,384]{2,1,0:T(8,128)S(1)}, s32[32,32,384]{2,1,0:T(8,128)}, u32[]{:S(2)}) copy-start(s32[32,32,384]{2,1,0:T(8,128)} %layer.3) | copy-start | bytes 4718596
  0.0 7.1 %copy-start = (s32[32,32,384]{2,1,0:T(8,128)S(1)}, s32[32,32,384]{2,1,0:T(8,128)}, u32[]{:S(2)}) copy-start(s32[32,32,384]{2,1,0:T(8,128)} %mask.3) | copy-start | bytes 4718596
  0.0 7.1 %copy-start.3 = (f32[32,32,384]{2,1,0:T(8,128)S(1)}, f32[32,32,384]{2,1,0:T(8,128)}, u32[]{:S(2)}) copy-start(f32[32,32,384]{2,1,0:T(8,128)} %stiff.1) | copy-start | bytes 4718596
  0.0 7.1 %copy-start.2 = (f32[32,32,384]{2,1,0:T(8,128)S(1)}, f32[32,32,384]{2,1,0:T(8,128)}, u32[]{:S(2)}) copy-start(f32[32,32,384]{2,1,0:T(8,128)} %conc.1) | copy-start | bytes 4718596
  2.8 7.6 %collective-permute-start.1 = (f32[3,32,384]{2,1,0:T(8,128)S(1)}, f32[3,32,384]{2,1,0:T(8,128)S(1)}, u32[]{:S(2)}, u32[]{:S(2)}) collective-permute-start(f32[3,32,384]{2,1,0:T(8,128)S(1)} %get-tuple-element.49.own_lo), channel_id=1, source_target_pairs={{32,0},{64,32},{96,64},{0,96},{33,1},{65,33},{97,65},{1,97},{34,2}... | collective-permute-start | bytes 442376 | tf_op jit(solution)/shard_map/ppermute | solution.py:581
  6.2 5.6 %collective-permute-start = (f32[3,32,384]{2,1,0:T(8,128)S(1)}, f32[3,32,384]{2,1,0:T(8,128)S(1)}, u32[]{:S(2)}, u32[]{:S(2)}) collective-permute-start(f32[3,32,384]{2,1,0:T(8,128)S(1)} %get-tuple-element.50.own_hi), channel_id=1, source_target_pairs={{0,32},{32,64},{64,96},{96,0},{1,33},{33,65},{65,97},{97,1},{2,34}... | collective-permute-start | bytes 442376 | tf_op jit(solution)/shard_map/ppermute | solution.py:580
  6.2 4.3 %collective-permute-start.2 = (f32[32,384]{1,0:T(8,128)S(1)}, f32[32,384]{1,0:T(8,128)S(1)}, u32[]{:S(2)}, u32[]{:S(2)}) collective-permute-start(f32[32,384]{1,0:T(8,128)S(1)} %get-tuple-element.57), channel_id=1, source_target_pairs={{1,0},{2,1},{3,2},{4,3},{5,4},{6,5},{7,6},{8,7},{9,8},{10,9},{11,1... | collective-permute-start | bytes 147464 | tf_op jit(solution)/shard_map/ppermute | solution.py:584
  11.8 9.2 %copy-start.4 = (f32[32,32,384]{2,1,0:T(8,128)S(1)}, f32[32,32,384]{2,1,0:T(8,128)}, u32[]{:S(2)}) copy-start(f32[32,32,384]{2,1,0:T(8,128)} %prod.1) | copy-start | bytes 4718596
  12.5 5.4 %collective-permute-start.3 = (f32[11,8,384]{2,1,0:T(8,128)S(1)}, f32[11,8,384]{2,1,0:T(8,128)S(1)}, u32[]{:S(2)}, u32[]{:S(2)}) collective-permute-start(f32[11,8,384]{2,1,0:T(8,128)S(1)} %get-tuple-element.59), channel_id=1, source_target_pairs={{0,1},{1,0},{2,3},{3,2},{4,5},{5,4},{6,7},{7,6},{8,9},{9,8},{10,11... | collective-permute-start | bytes 405512 | tf_op jit(solution)/shard_map/ppermute | solution.py:558
  17.9 6.4 %collective-permute-start.6 = (f32[11,8,384]{2,1,0:T(8,128)S(1)}, f32[11,8,384]{2,1,0:T(8,128)S(1)}, u32[]{:S(2)}, u32[]{:S(2)}) collective-permute-start(f32[11,8,384]{2,1,0:T(8,128)S(1)} %get-tuple-element.65.mine), channel_id=1, source_target_pairs={{0,4},{1,5},{2,6},{3,7},{4,0},{5,1},{6,2},{7,3},{8,12},{9,13},{10,... | collective-permute-start | bytes 405512 | tf_op jit(solution)/shard_map/ppermute | solution.py:558
  19.2 8.8 %collective-permute-start.5 = (f32[11,8,384]{2,1,0:T(8,128)S(1)}, f32[11,8,384]{2,1,0:T(8,128)S(1)}, u32[]{:S(2)}, u32[]{:S(2)}) collective-permute-start(f32[11,8,384]{2,1,0:T(8,128)S(1)} %get-tuple-element.65.mine), channel_id=1, source_target_pairs={{0,7},{1,6},{2,5},{3,4},{4,3},{5,2},{6,1},{7,0},{8,15},{9,14},{10,... | collective-permute-start | bytes 405512 | tf_op jit(solution)/shard_map/ppermute | solution.py:558
  20.1 7.9 %collective-permute-start.4 = (f32[11,8,384]{2,1,0:T(8,128)S(1)}, f32[11,8,384]{2,1,0:T(8,128)S(1)}, u32[]{:S(2)}, u32[]{:S(2)}) collective-permute-start(f32[11,8,384]{2,1,0:T(8,128)S(1)} %get-tuple-element.65.mine), channel_id=1, source_target_pairs={{0,3},{1,2},{2,1},{3,0},{4,7},{5,6},{6,5},{7,4},{8,11},{9,10},{10,... | collective-permute-start | bytes 405512 | tf_op jit(solution)/shard_map/ppermute | solution.py:558
  28.2 6.3 %collective-permute-start.9 = (f32[11,8,384]{2,1,0:T(8,128)S(1)}, f32[11,8,384]{2,1,0:T(8,128)S(1)}, u32[]{:S(2)}, u32[]{:S(2)}) collective-permute-start(f32[11,8,384]{2,1,0:T(8,128)S(1)} %get-tuple-element.66.mine), channel_id=1, source_target_pairs={{0,16},{1,17},{2,18},{3,19},{4,20},{5,21},{6,22},{7,23},{8,24},{9,... | collective-permute-start | bytes 405512 | tf_op jit(solution)/shard_map/ppermute | solution.py:558
  29.9 8.4 %collective-permute-start.8 = (f32[11,8,384]{2,1,0:T(8,128)S(1)}, f32[11,8,384]{2,1,0:T(8,128)S(1)}, u32[]{:S(2)}, u32[]{:S(2)}) collective-permute-start(f32[11,8,384]{2,1,0:T(8,128)S(1)} %get-tuple-element.66.mine), channel_id=1, source_target_pairs={{0,25},{1,24},{2,27},{3,26},{4,29},{5,28},{6,31},{7,30},{8,17},{9,... | collective-permute-start | bytes 405512 | tf_op jit(solution)/shard_map/ppermute | solution.py:558
  31.0 7.3 %collective-permute-start.7 = (f32[11,8,384]{2,1,0:T(8,128)S(1)}, f32[11,8,384]{2,1,0:T(8,128)S(1)}, u32[]{:S(2)}, u32[]{:S(2)}) collective-permute-start(f32[11,8,384]{2,1,0:T(8,128)S(1)} %get-tuple-element.66.mine), channel_id=1, source_target_pairs={{0,9},{1,8},{2,11},{3,10},{4,13},{5,12},{6,15},{7,14},{8,1},{9,0},... | collective-permute-start | bytes 405512 | tf_op jit(solution)/shard_map/ppermute | solution.py:558
  31.2 7.8 %collective-permute-start.11 = (f32[2,32,384]{2,1,0:T(8,128)S(1)}, f32[2,32,384]{2,1,0:T(8,128)S(1)}, u32[]{:S(2)}, u32[]{:S(2)}) collective-permute-start(f32[2,32,384]{2,1,0:T(8,128)S(1)} %get-tuple-element.81), channel_id=1, source_target_pairs={{0,32},{32,64},{64,96},{96,0},{1,33},{33,65},{65,97},{97,1},{2,34}... | collective-permute-start | bytes 294920 | tf_op jit(solution)/shard_map/ppermute | solution.py:580
  31.4 7.6 %collective-permute-start.12 = (f32[2,32,384]{2,1,0:T(8,128)S(1)}, f32[2,32,384]{2,1,0:T(8,128)S(1)}, u32[]{:S(2)}, u32[]{:S(2)}) collective-permute-start(f32[2,32,384]{2,1,0:T(8,128)S(1)} %get-tuple-element.82), channel_id=1, source_target_pairs={{32,0},{64,32},{96,64},{0,96},{33,1},{65,33},{97,65},{1,97},{34,2}... | collective-permute-start | bytes 294920 | tf_op jit(solution)/shard_map/ppermute | solution.py:581
  38.5 1.4 %collective-permute-start.10 = (f32[5,8,384]{2,1,0:T(8,128)S(1)}, f32[5,8,384]{2,1,0:T(8,128)S(1)}, u32[]{:S(2)}, u32[]{:S(2)}) collective-permute-start(f32[5,8,384]{2,1,0:T(8,128)S(1)} %get-tuple-element.74), channel_id=1, source_target_pairs={{0,1},{1,0},{2,3},{3,2},{4,5},{5,4},{6,7},{7,6},{8,9},{9,8},{10,11... | collective-permute-start | bytes 184328 | tf_op jit(solution)/shard_map/ppermute | solution.py:558
  42.2 1.3 %collective-permute-start.13 = (f32[4,8,384]{2,1,0:T(8,128)S(1)}, f32[4,8,384]{2,1,0:T(8,128)S(1)}, u32[]{:S(2)}, u32[]{:S(2)}) collective-permute-start(f32[4,8,384]{2,1,0:T(8,128)S(1)} %get-tuple-element.84), channel_id=1, source_target_pairs={{0,1},{1,0},{2,3},{3,2},{4,5},{5,4},{6,7},{7,6},{8,9},{9,8},{10,11... | collective-permute-start | bytes 147464 | tf_op jit(solution)/shard_map/ppermute | solution.py:558
  43.6 4.5 %collective-permute-start.16 = (f32[4,8,384]{2,1,0:T(8,128)S(1)}, f32[4,8,384]{2,1,0:T(8,128)S(1)}, u32[]{:S(2)}, u32[]{:S(2)}) collective-permute-start(f32[4,8,384]{2,1,0:T(8,128)S(1)} %get-tuple-element.85.mine), channel_id=1, source_target_pairs={{0,4},{1,5},{2,6},{3,7},{4,0},{5,1},{6,2},{7,3},{8,12},{9,13},{10,... | collective-permute-start | bytes 147464 | tf_op jit(solution)/shard_map/ppermute | solution.py:558
  44.8 5.4 %collective-permute-start.15 = (f32[4,8,384]{2,1,0:T(8,128)S(1)}, f32[4,8,384]{2,1,0:T(8,128)S(1)}, u32[]{:S(2)}, u32[]{:S(2)}) collective-permute-start(f32[4,8,384]{2,1,0:T(8,128)S(1)} %get-tuple-element.85.mine), channel_id=1, source_target_pairs={{0,7},{1,6},{2,5},{3,4},{4,3},{5,2},{6,1},{7,0},{8,15},{9,14},{10,... | collective-permute-start | bytes 147464 | tf_op jit(solution)/shard_map/ppermute | solution.py:558
  45.8 4.4 %collective-permute-start.14 = (f32[4,8,384]{2,1,0:T(8,128)S(1)}, f32[4,8,384]{2,1,0:T(8,128)S(1)}, u32[]{:S(2)}, u32[]{:S(2)}) collective-permute-start(f32[4,8,384]{2,1,0:T(8,128)S(1)} %get-tuple-element.85.mine), channel_id=1, source_target_pairs={{0,3},{1,2},{2,1},{3,0},{4,7},{5,6},{6,5},{7,4},{8,11},{9,10},{10,... | collective-permute-start | bytes 147464 | tf_op jit(solution)/shard_map/ppermute | solution.py:558
  50.3 4.5 %collective-permute-start.19 = (f32[4,8,384]{2,1,0:T(8,128)S(1)}, f32[4,8,384]{2,1,0:T(8,128)S(1)}, u32[]{:S(2)}, u32[]{:S(2)}) collective-permute-start(f32[4,8,384]{2,1,0:T(8,128)S(1)} %get-tuple-element.86.mine), channel_id=1, source_target_pairs={{0,16},{1,17},{2,18},{3,19},{4,20},{5,21},{6,22},{7,23},{8,24},{9,... | collective-permute-start | bytes 147464 | tf_op jit(solution)/shard_map/ppermute | solution.py:558
  52.4 5.5 %collective-permute-start.18 = (f32[4,8,384]{2,1,0:T(8,128)S(1)}, f32[4,8,384]{2,1,0:T(8,128)S(1)}, u32[]{:S(2)}, u32[]{:S(2)}) collective-permute-start(f32[4,8,384]{2,1,0:T(8,128)S(1)} %get-tuple-element.86.mine), channel_id=1, source_target_pairs={{0,25},{1,24},{2,27},{3,26},{4,29},{5,28},{6,31},{7,30},{8,17},{9,... | collective-permute-start | bytes 147464 | tf_op jit(solution)/shard_map/ppermute | solution.py:558
  53.8 4.2 %collective-permute-start.17 = (f32[4,8,384]{2,1,0:T(8,128)S(1)}, f32[4,8,384]{2,1,0:T(8,128)S(1)}, u32[]{:S(2)}, u32[]{:S(2)}) collective-permute-start(f32[4,8,384]{2,1,0:T(8,128)S(1)} %get-tuple-element.86.mine), channel_id=1, source_target_pairs={{0,9},{1,8},{2,11},{3,10},{4,13},{5,12},{6,15},{7,14},{8,1},{9,0},... | collective-permute-start | bytes 147464 | tf_op jit(solution)/shard_map/ppermute | solution.py:558
  58.1 1.4 %collective-permute-start.20 = (f32[4,8,384]{2,1,0:T(8,128)S(1)}, f32[4,8,384]{2,1,0:T(8,128)S(1)}, u32[]{:S(2)}, u32[]{:S(2)}) collective-permute-start(f32[4,8,384]{2,1,0:T(8,128)S(1)} %get-tuple-element.91), channel_id=1, source_target_pairs={{0,1},{1,0},{2,3},{3,2},{4,5},{5,4},{6,7},{7,6},{8,9},{9,8},{10,11... | collective-permute-start | bytes 147464 | tf_op jit(solution)/shard_map/ppermute | solution.py:558

commit v4 on v3

--- a/solution.py
+++ b/solution.py
@@ -109,7 +109,7 @@
         for k, (source, target) in enumerate(((mask_hbm, mask_row), (layer_hbm, layer_row), (stiff_hbm, stiff_row)))])
     for group in copies:
         for copy in group:
-            copy.start()
+            copy.start(priority=1)
     table = read_table(diff_table)
     for side, out in ((0, lo_out), (1, hi_out)):
         for copy in copies[side]:
@@ -187,53 +187,71 @@
     return tiles[8 * k:8 * k + 8]
 
 
+def half_rows(slab, which):
+    return pl.ds(pl.multiple_of(which * (slab // 2), slab // 2), slab // 2)
+
+
+def put_rows(stack, k, value):
+    stack[2 * k], stack[2 * k + 1] = value[:8], value[8:]
+
+
+def half_sweep(rows, at, explicit, g_ref, r_ref, gp_ref, last_ref, fwd_ref, out):
+    total = e = None
+    for z in range(rows):
+        e = explicit(z) if z == 0 else explicit(z) + g_ref[z - 1, at] * e
+        fwd_ref[z] = e
+        term = gp_ref[z, at] * (r_ref[z, at] if z < rows - 1 else last_ref[1, at]) * e
+        total = term if z == 0 else total + term
+    put_rows(out, 0, total)
+    put_rows(out, 1, last_ref[0, at] * e)
+
+
+def first_half_sweep(rows, slab, cols, which, g_ref, r_ref, gp_ref, part_ref, ends_ref, flux_ref, last_ref, fwd_ref, out):
+    at = half_rows(slab, which)
+    row = lax.broadcasted_iota(jnp.int32, (8, cols), 0)
+    lo = jnp.where(row == jnp.where(which == 0, 0, -1), 1.0, 0.0)
+    hi = jnp.where(row == jnp.where(which == 1, 7, -1), 1.0, 0.0)
+
+    def explicit(z):
+        part = part_ref[z, at]
+        return jnp.concatenate(
+            [part[:8] + lo * flux_ref[0, z:z + 1], part[8:] + hi * flux_ref[1, z:z + 1]], axis=0)
+
+    half_sweep(rows, at, explicit, g_ref, r_ref, gp_ref, last_ref, fwd_ref, out)
+    last_g, last_r, gp = last_ref[0, at], last_ref[1, at], gp_ref[rows - 1, at]
+    put_rows(out, 2, ends_ref[1, at] + last_r * gp * gp)
+    put_rows(out, 3, last_g * gp)
+    put_rows(out, 4, last_g * ends_ref[0, at])
+
+
 def first_forward_kernel(
     rows, slab, cols, nx, nax,
     own_lo, own_hi, s_ref, g_ref, r_ref, gp_ref, part_ref, ends_ref, from_lo, from_hi, above_ref,
-    fwd_ref, last_ref, mine_ref, send_ref, border_ref,
-    ports_ref, border_ports, lines,
+    last_ref, flux_ref, fwd_ref, send_ref, border_ref, own_border_ref,
+    border_ports, lines,
 ):
     ix, ia = lax.axis_index("xs"), lax.axis_index("ax")
     above = jnp.where(ia < nax - 1, RZ, 0.0)
     c = above * s_ref[rows - 1] * above_ref[...]
-    m, alpha = ends_ref[0], ends_ref[1]
-    last_r = inverse(m + c)
-    last_g = c * last_r
-    gp = gp_ref[rows - 1]
-    last_ref[0] = last_g
+    last_r = inverse(ends_ref[0] + c)
+    last_ref[0] = c * last_r
     last_ref[1] = last_r
-    ports_ref[2] = alpha + last_r * gp * gp
-    ports_ref[3] = last_g * gp
-    ports_ref[4] = last_g * m
 
     for side, (own, halo, exists) in enumerate(((own_lo, from_lo, ix > 0), (own_hi, from_hi, ix < nx - 1))):
         s_own, state_own = own[0], own[1]
         s = jnp.where(exists, halo[0], 0.0)
-        state = halo[1]
-        flux = SECTION_RATE * s_own * s * (state - state_own)
+        flux = SECTION_RATE * s_own * s * (halo[1] - state_own)
         lines[side, 0] = s
         lines[side, 1] = halo[2] - flux
         lines[side, 2] = RZ * s * pltpu.roll(s, rows - 1, 0)
-        lines[side, 3] = flux
+        flux_ref[side] = flux
 
     row = lax.broadcasted_iota(jnp.int32, (8, cols), 0)
-    is_lo = row == 7
 
     def border(k, z):
-        return jnp.where(is_lo, lines[0, k, z:z + 1], lines[1, k, z:z + 1])
-
-    total = prev = None
+        return jnp.where(row == 7, lines[0, k, z:z + 1], lines[1, k, z:z + 1])
+
     for z in range(rows):
-        part = part_ref[z]
-        edges = (jnp.where(row == 0, lines[0, 3, z:z + 1], 0.0), jnp.where(row == 7, lines[1, 3, z:z + 1], 0.0))
-        e = jnp.concatenate([part[0:8] + edges[0], part[8:slab - 8], part[slab - 8:] + edges[1]], axis=0)
-        if z > 0:
-            e = e + g_ref[z - 1] * prev
-        fwd_ref[z] = e
-        term = gp_ref[z] * (r_ref[z] if z < rows - 1 else last_r) * e
-        total = term if z == 0 else total + term
-        prev = e
-
         sb, eb = border(0, z), border(1, z)
         if z == 0:
             mb = gpb = jnp.ones_like(sb)
@@ -255,23 +273,25 @@
         pb = grb * eb if z == 0 else pb + grb * eb
         for k, value in enumerate((sb, gb, rb, gpb, fb)):
             border_ref[k, z] = value
-    ports_ref[0] = total
-    ports_ref[1] = last_g * prev
     zero = jnp.zeros_like(sb)
     for k, value in enumerate((ab, grb, rb, pb, rb * fb, first, sb, zero)):
         border_ports[0, k:k + 1] = value[7:8]
         border_ports[1, k:k + 1] = value[0:1]
     half = place()[3]
-    for out, which in ((mine_ref, half), (send_ref, 1 - half)):
-        split_ports(slab, PLANES, ports_ref, out, which)
-        out[2 * PLANES] = border_ports[which]
-
-
-def split_ports(slab, planes, ports_ref, out, which):
-    for t in range(slab // 16):
-        at = pl.ds(pl.multiple_of(which * (slab // 2) + 8 * t, 8), 8)
-        for k in range(planes):
-            out[2 * k + t] = ports_ref[k, at]
+    first_half_sweep(rows, slab, cols, 1 - half, g_ref, r_ref, gp_ref, part_ref, ends_ref, flux_ref, last_ref, fwd_ref,
+                     send_ref)
+    send_ref[2 * PLANES] = border_ports[1 - half]
+    own_border_ref[...] = border_ports[half]
+
+
+def first_own_kernel(
+    rows, slab, cols,
+    g_ref, r_ref, gp_ref, part_ref, ends_ref, flux_ref, last_ref, own_border_ref,
+    fwd_ref, mine_ref,
+):
+    first_half_sweep(rows, slab, cols, place()[3], g_ref, r_ref, gp_ref, part_ref, ends_ref, flux_ref, last_ref, fwd_ref,
+                     mine_ref)
+    mine_ref[2 * PLANES] = own_border_ref[...]
 
 
 def place():
@@ -449,88 +469,142 @@
     descend((lev0, lev1, lev2), (val0, val1, val2), mine_out, send_out)
 
 
-def whole_ports(own, other):
-    second = place()[3] == 1
-    planes = []
-    for k in (0, 1):
-        low = [jnp.where(second, other[2 * k + t], own[2 * k + t]) for t in (0, 1)]
-        high = [jnp.where(second, own[2 * k + t], other[2 * k + t]) for t in (0, 1)]
-        planes.append(low + high)
-    return planes
+def half_state(rows, at, ports, g_ref, r_ref, gp_ref, fwd_ref, last_ref, keep_ref, source_ref, emit):
+    q = jnp.concatenate([ports[0], ports[1]], axis=0)
+    u = jnp.concatenate([ports[2], ports[3]], axis=0)
+    for z in range(rows - 1, -1, -1):
+        r = r_ref[z, at] if z < rows - 1 else last_ref[1, at]
+        g = g_ref[z, at] if z < rows - 1 else last_ref[0, at]
+        u = r * (fwd_ref[z] + gp_ref[z, at] * q) + g * u
+        emit(z, source_ref[z, at] + keep_ref[z, at] * u)
+
+
+def own_state_kernel(rows, slab, own, g_ref, r_ref, gp_ref, fwd_ref, last_ref, keep_ref, source_ref, state_ref):
+    def emit(z, state):
+        state_ref[z] = state
+
+    half_state(rows, half_rows(slab, place()[3]), own, g_ref, r_ref, gp_ref, fwd_ref, last_ref, keep_ref, source_ref, emit)
 
 
 def split_cols(tile):
     return [tile[:, c:c + 128] for c in range(0, tile.shape[-1], 128)]
 
 
+def half_tiles(plane):
+    return [split_cols(plane[t:t + 8]) for t in range(0, plane.shape[0], 8)]
+
+
+def products(left, right):
+    return [[x * y for x, y in zip(*lines)] for lines in zip(left, right)]
+
+
+def put_tiles(ref, z, tiles):
+    for t, line in enumerate(tiles):
+        for c, tile in enumerate(line):
+            ref[z, 8 * t:8 * t + 8, 128 * c:128 * c + 128] = tile
+
+
+def explicit_tiles(state, s, vsum, ssum):
+    return [[x + SECTION_RATE * w * (v - x * n) for x, w, v, n in zip(*lines)] for lines in zip(state, s, vsum, ssum)]
+
+
+def own_explicit_kernel(
+    rows, slab,
+    own, s_ref, g_ref, r_ref, gp_ref, fwd_ref, last_ref, keep_ref, source_ref, ssum_ref,
+    state_ref, part_ref,
+):
+    at = half_rows(slab, place()[3])
+
+    def emit(z, state):
+        state_ref[z] = state
+        state, s = half_tiles(state), half_tiles(s_ref[z, at])
+        put_tiles(part_ref, z, explicit_tiles(state, s, neighbour_sum(products(s, state)), half_tiles(ssum_ref[z, at])))
+
+    half_state(rows, at, own, g_ref, r_ref, gp_ref, fwd_ref, last_ref, keep_ref, source_ref, emit)
+
+
 def middle_kernel(
     rows, slab, cols,
-    own, other, s_ref, g_ref, r_ref, gp_ref, fwd_in, last_ref, keep_ref, source_ref, ssum_ref, border_ref,
-    reaction_lo, reaction_hi,
-    fwd_ref, mine_ref, send_ref, ports_ref,
+    own, other, state_own, part_own, s_ref, g_ref, r_ref, gp_ref, fwd_in, last_ref, keep_ref, source_ref, ssum_ref,
+    border_ref, reaction_lo, reaction_hi,
+    e_own, fwd_ref, send_ref,
+    e_other,
 ):
-    q, u = whole_ports(own, other)
-    inflow = jnp.concatenate(q, axis=0)
-    u = jnp.concatenate(u, axis=0)
     row = lax.broadcasted_iota(jnp.int32, (8, cols), 0)
-    second = place()[3] == 1
+    half = place()[3]
+    second = half == 1
     low_tile, high_tile = jnp.where(second, other[4], own[4]), jnp.where(second, own[4], other[4])
     inflow_b = jnp.where(row == 7, low_tile[0:1], high_tile[0:1])
-    top_b = jnp.where(row == 7, low_tile[1:2], high_tile[1:2])
+    border = [jnp.where(row == 7, low_tile[1:2], high_tile[1:2])]
     narrow = lax.broadcasted_iota(jnp.int32, (8, 128), 0)
-    last = slab // 8 - 1
-    for z in range(rows - 1, -1, -1):
-        r = r_ref[z] if z < rows - 1 else last_ref[1]
-        g = g_ref[z] if z < rows - 1 else last_ref[0]
-        u = r * (fwd_in[z] + gp_ref[z] * inflow) + g * u
-        state = source_ref[z] + keep_ref[z] * u
+    bottom = narrow == 7
+    mine, at = half_rows(slab, half), half_rows(slab, 1 - half)
+
+    def around(is_second, flow_b, neighbour):
+        return [jnp.where(is_second, jnp.where(bottom, high, b), jnp.where(bottom, b, low))
+                for b, low, high in zip(flow_b, neighbour[0], neighbour[1])]
+
+    def border_part(is_second, tile):
+        return [jnp.where(is_second, jnp.where(bottom, 0.0, x), jnp.where(bottom, x, 0.0)) for x in tile]
+
+    def to_rows(tile):
+        return ([jnp.where(narrow == 0, pltpu.roll(x, 1, 0), 0.0) for x in tile],
+                [jnp.where(narrow == 7, pltpu.roll(x, 7, 0), 0.0) for x in tile])
+
+    def explicit(z, new):
         sb, gb, rb, gpb, fb = [border_ref[k, z] for k in range(5)]
         keep_b, source_b = [jnp.where(row == 7, reaction_lo[k, z:z + 1], reaction_hi[k, z:z + 1]) for k in (0, 1)]
         rhs = fb + gpb * inflow_b
-        ub = rb * (rhs + top_b) if z == rows - 1 else rb * rhs + gb * ub
+        ub = border[0] = rb * (rhs + border[0]) if z == rows - 1 else rb * rhs + gb * border[0]
         flow_b = split_cols(sb * (source_b + keep_b * ub))
         sb = split_cols(sb)
-        state = [split_cols(tile_of(state, t)) for t in range(slab // 8)]
-        s, ssum = tiles_of(s_ref, z, slab, cols), tiles_of(ssum_ref, z, slab, cols)
-        ssum[0] = [x + jnp.where(narrow == 0, pltpu.roll(y, 1, 0), 0.0) for x, y in zip(ssum[0], sb)]
-        ssum[last] = [x + jnp.where(narrow == 7, pltpu.roll(y, 7, 0), 0.0) for x, y in zip(ssum[last], sb)]
-        vsum = neighbour_sum([[x * y for x, y in zip(*lines)] for lines in zip(s, state)], flow_b)
-        for t in range(slab // 8):
-            for c in range(cols // 128):
-                fwd_ref[z, 8 * t:8 * t + 8, 128 * c:128 * c + 128] = state[t][c] + SECTION_RATE * s[t][c] * (
-                    vsum[t][c] - state[t][c] * ssum[t][c])
-    e = fwd_ref[0]
-    total = gp_ref[0] * r_ref[0] * e
-    for z in range(1, rows):
-        e = fwd_ref[z] + g_ref[z - 1] * e
-        fwd_ref[z] = e
-        total = total + gp_ref[z] * (r_ref[z] if z < rows - 1 else last_ref[1]) * e
-    ports_ref[0] = total
-    ports_ref[1] = last_ref[0] * e
-    half = place()[3]
-    split_ports(slab, 2, ports_ref, mine_ref, half)
-    split_ports(slab, 2, ports_ref, send_ref, 1 - half)
+        kept, s_kept = half_tiles(state_own[z]), half_tiles(s_ref[z, mine])
+        state, s = half_tiles(new), half_tiles(s_ref[z, at])
+        flow_kept, flow = products(s_kept, kept), products(s, state)
+
+        ssum = half_tiles(ssum_ref[z, at])
+        ssum = [[x + y for x, y in zip(*lines)] for lines in zip(ssum, to_rows(border_part(half == 0, sb)))]
+        vsum = neighbour_sum(flow, around(half == 0, flow_b, flow_kept))
+        put_tiles(e_other, z, explicit_tiles(state, s, vsum, ssum))
+
+        v_more, s_more = to_rows(around(second, flow_b, flow)), to_rows(border_part(second, sb))
+        part = half_tiles(part_own[z])
+        put_tiles(e_own, z, [
+            [p + SECTION_RATE * w * (v - x * n) for p, w, v, x, n in zip(*lines)]
+            for lines in zip(part, s_kept, v_more, kept, s_more)])
+
+    half_state(rows, at, other, g_ref, r_ref, gp_ref, fwd_in, last_ref, keep_ref, source_ref, explicit)
+    half_sweep(rows, at, lambda z: e_other[z], g_ref, r_ref, gp_ref, last_ref, fwd_ref, send_ref)
+
+
+def second_own_kernel(rows, slab, e_ref, g_ref, r_ref, gp_ref, last_ref, fwd_ref, mine_ref):
+    at = half_rows(slab, place()[3])
+    half_sweep(rows, at, lambda z: e_ref[z], g_ref, r_ref, gp_ref, last_ref, fwd_ref, mine_ref)
 
 
 def final_kernel(
     rows, slab,
-    own, other, g_ref, r_ref, gp_ref, fwd_ref, last_ref, keep_ref, source_ref,
-    out_hbm, out, sems,
+    other, state_own, g_ref, r_ref, gp_ref, fwd_ref, last_ref, keep_ref, source_ref,
+    out_hbm, out, sems, own_sem,
 ):
-    q, u = [jnp.concatenate(tiles, axis=0) for tiles in whole_ports(own, other)]
+    half = place()[3]
+    own_copy = pltpu.make_async_copy(state_own, out_hbm.at[:, half_rows(slab, half)], own_sem)
+    own_copy.start()
+    at = half_rows(slab, 1 - half)
     copies = []
-    for z in range(rows - 1, -1, -1):
-        r = r_ref[z] if z < rows - 1 else last_ref[1]
-        g = g_ref[z] if z < rows - 1 else last_ref[0]
-        u = r * (fwd_ref[z] + gp_ref[z] * q) + g * u
-        out[z] = source_ref[z] + keep_ref[z] * u
+
+    def emit(z, state):
+        out[z] = state
         if z % CHUNK == 0:
             here = pl.ds(z, CHUNK)
-            copy = pltpu.make_async_copy(out.at[here], out_hbm.at[here], sems.at[z // CHUNK])
+            copy = pltpu.make_async_copy(out.at[here], out_hbm.at[here, at], sems.at[z // CHUNK])
             copy.start()
             copies.append(copy)
+
+    half_state(rows, at, other, g_ref, r_ref, gp_ref, fwd_ref, last_ref, keep_ref, source_ref, emit)
     for copy in copies:
         copy.wait()
+    own_copy.wait()
 
 
 def on_device(partners, concentration, tissue_mask, wall_layer, stiffness, production, layer_diffusivity, uptake_rate):
@@ -591,13 +665,20 @@
         us=5.0,
     )
     stack, pair = 2 * PLANES + 1, (5, 8, cols)
-    fwd, last, mine, send, border = call(
+    half_block = (rows, slab // 2, cols)
+    last, flux, fwd_other, send, border, own_border = call(
         functools.partial(first_forward_kernel, rows, slab, cols, nx, nax),
-        [at_vmem(*block), at_vmem(2, slab, cols), at_vmem(stack, 8, cols), at_vmem(stack, 8, cols),
-         at_vmem(5, rows, 8, cols)],
+        [at_vmem(2, slab, cols), at_vmem(2, rows, cols), at_vmem(*half_block), at_vmem(stack, 8, cols),
+         at_vmem(5, rows, 8, cols), at_vmem(8, cols)],
         [lo, hi, s, g, r, gp, part, ends, from_lo, from_hi, above_s],
-        scratch=[f32(PLANES, slab, cols), f32(2, 8, cols), f32(2, 4, rows, cols)],
-    )
+        scratch=[f32(2, 8, cols), f32(2, 3, rows, cols)],
+    )
+    fwd_own, mine = call(
+        functools.partial(first_own_kernel, rows, slab, cols),
+        [at_vmem(*half_block), at_vmem(stack, 8, cols)],
+        [g, r, gp, part, ends, flux, last, own_border],
+    )
+
     levs, values, border_levs = [], [], []
     for stage in (0, 1):
         received = exchange(mine if stage else send, stage)
@@ -632,13 +713,23 @@
     )
     levs.append(lev)
     (other,) = exchange(send, 0)
-
-    fwd, mine, send = call(
+    state_own, part_own = call(
+        functools.partial(own_explicit_kernel, rows, slab),
+        [at_vmem(*half_block)] * 2,
+        [own, s, g, r, gp, fwd_own, last, keep, source, ssum],
+    )
+    e, fwd_other, send = call(
         functools.partial(middle_kernel, rows, slab, cols),
-        [at_vmem(*block), at_vmem(4, 8, cols), at_vmem(4, 8, cols)],
-        [own, other, s, g, r, gp, fwd, last, keep, source, ssum, border, reaction_lo, reaction_hi],
-        scratch=[f32(2, slab, cols)],
+        [at_vmem(*half_block), at_vmem(*half_block), at_vmem(4, 8, cols)],
+        [own, other, state_own, part_own, s, g, r, gp, fwd_other, last, keep, source, ssum, border,
+         reaction_lo, reaction_hi],
+        scratch=[f32(*half_block)],
         us=3.0,
+    )
+    fwd_own, mine = call(
+        functools.partial(second_own_kernel, rows, slab),
+        [at_vmem(*half_block), at_vmem(4, 8, cols)],
+        [e, g, r, gp, last],
     )
     values = []
     for stage in (0, 1):
@@ -659,11 +750,16 @@
         scratch=[f32(4 * joins, 8, cols)],
     )
     (other,) = exchange(send, 0)
+    (state_own,) = call(
+        functools.partial(own_state_kernel, rows, slab),
+        [at_vmem(*half_block)],
+        [own, g, r, gp, fwd_own, last, keep, source],
+    )
     (out,) = call(
         functools.partial(final_kernel, rows, slab),
         [jax.ShapeDtypeStruct(block, jnp.float32)],
-        [own, other, g, r, gp, fwd, last, keep, source],
-        scratch=[f32(*block), pltpu.SemaphoreType.DMA((rows // CHUNK,))],
+        [other, state_own, g, r, gp, fwd_other, last, keep, source],
+        scratch=[f32(*half_block), pltpu.SemaphoreType.DMA((rows // CHUNK,)), pltpu.SemaphoreType.DMA],
         out_specs=[hbm],
     )
     return out

time: 60.9 us -> 60.3 us (level)
  waiting for transfers between devices: 23 us -> 21.2 us
  Pallas kernels: 12.4 us -> 13.2 us
    ppermute x16, waiting for transfers between devices: 21.6 us -> 20 us  [exchange(): lax.ppermute(block, 'ax', route)]
    pallas_call x12 -> x16, Pallas kernels: 12.4 us -> 13.2 us  [call(): pl.pallas_call(kernel, out_shape=outs, in_specs=specs or [vspec()] * len(...]
  transfers between devices with their start and end apart: 21 -> 21, of which waited for: 13 -> 13; matrix products, arithmetic and copies ran while one was open for 0% -> 0% of each run, Pallas kernels for 8% -> 11%
where the time goes in v4:
time: 60.3 us; the launch traced here: 60.2 us
  starting transfers between devices  25.5 us (42%)
  waiting for transfers between devices  21.2 us (35%)
  Pallas kernels  13.2 us (22%)
    ppermute x16, waiting for transfers between devices, exchange(): lax.ppermute(block, 'ax', route)  20 us
    ppermute x16, starting transfers between devices, exchange(): lax.ppermute(block, 'ax', route)  18.5 us
    pallas_call x16, Pallas kernels, call(): pl.pallas_call(kernel, out_shape=outs, in_specs=specs or [vspec()] * len(...  13.2 us
    ppermute x2, starting transfers between devices, from_neighbours(): lax.ppermute(lo, 'xs', [((i + 1) % nx, i) for i in range(nx)])  5.88 us
  transfers between devices with their start and end apart: 21, of which 13 were waited for; matrix products, arithmetic and copies ran while one was open for 0% of the time, Pallas kernels for 11%

profile of v4, /device:TPU:1, one launch (start us, length us, event | category | flops | bytes accessed | tf_op | source)
XLA Modules:
  0.0 60.2 jit_solution(6612640470216211012)
XLA Ops:
  0.0 0.0 copy-start.1
  0.0 0.0 copy-start.2
  0.0 2.8 %shard_map.74 = (f32[3,32,384]{2,1,0:T(8,128)S(1)}, f32[3,32,384]{2,1,0:T(8,128)S(1)}, f32[32,384]{1,0:T(8,128)S(1)}) custom-call(f32[4]{0:T(128)} %diff_table.1, f32[32,32,384]{2,1,0:T(8,128)} %conc_hbm.1, s32[32,32,384]{2,1,0:T(8,128)} %mask.3, s32[32,32,384]{2,1,0:T(8,128)} %layer.3, f32[32,32,384]{2,1,0:T(8,128)} %stiff_hbm.1), custom_call_target="tpu_custom_call" | custom-call | flops 2000000 | bytes 3000000 | tf_op jit(solution)/shard_map/pallas_call | solution.py:621
  2.8 3.4 %collective-permute-start.1 = (f32[3,32,384]{2,1,0:T(8,128)S(1)}, f32[3,32,384]{2,1,0:T(8,128)S(1)}, u32[]{:S(2)}, u32[]{:S(2)}) collective-permute-start(f32[3,32,384]{2,1,0:T(8,128)S(1)} %get-tuple-element.61.own_lo), channel_id=1, source_target_pairs={{32,0},{64,32},{96,64},{0,96},{33,1},{65,33},{97,65},{1,97},{34,2}... | collective-permute-start | bytes 442376 | tf_op jit(solution)/shard_map/ppermute | solution.py:655
  6.2 0.0 collective-permute-start
  6.2 1.0 %collective-permute-start.2 = (f32[32,384]{1,0:T(8,128)S(1)}, f32[32,384]{1,0:T(8,128)S(1)}, u32[]{:S(2)}, u32[]{:S(2)}) collective-permute-start(f32[32,384]{1,0:T(8,128)S(1)} %get-tuple-element.64), channel_id=1, source_target_pairs={{1,0},{2,1},{3,2},{4,3},{5,4},{6,5},{7,6},{8,7},{9,8},{10,9},{11,1... | collective-permute-start | bytes 147464 | tf_op jit(solution)/shard_map/ppermute | solution.py:658
  7.1 0.0 copy-done.1
  7.1 0.0 copy-done
  7.1 0.0 copy-done.3
  7.1 0.0 copy-done.2
  7.1 3.4 %shard_map.73 = (f32[32,32,384]{2,1,0:T(8,128)S(1)}, f32[32,32,384]{2,1,0:T(8,128)S(1)}, f32[32,32,384]{2,1,0:T(8,128)S(1)}, f32[32,32,384]{2,1,0:T(8,128)S(1)},...) custom-call(f32[4]{0:T(128)} %diff_table.1, f32[32,32,384]{2,1,0:T(8,128)S(1)} %copy-done.2, ...), custom_call_target="tpu_custom_call" | custom-call | flops 10000000 | bytes 15000000 | tf_op jit(solution)/shard_map/pallas_call | solution.py:621
  10.6 0.0 collective-permute-done.2.above_ref
  10.6 0.0 collective-permute-done.1.from_hi
  10.6 1.2 %collective-permute-done.from_lo = f32[3,32,384]{2,1,0:T(8,128)S(1)} collective-permute-done((f32[3,32,384]{2,1,0:T(8,128)S(1)}, f32[3,32,384]{2,1,0:T(8,128)S(1)}, u32[]{:S(2)}, u32[]{:S(2)}) %collective-permute-start) | collective-permute-done | bytes 147488 | tf_op jit(solution)/shard_map/ppermute | solution.py:654
  11.8 0.6 %shard_map.75 = (f32[2,32,384]{2,1,0:T(8,128)S(1)}, f32[2,32,384]{2,1,0:T(8,128)S(1)}, f32[32,16,384]{2,1,0:T(8,128)S(1)}, f32[11,8,384]{2,1,0:T(8,128)S(1)}, f3...) custom-call(f32[3,32,384]{2,1,0:T(8,128)S(1)} %get-tuple-element.61.own_lo, ...), custom_call_target="tpu_custom_call" | custom-call | flops 2000000 | bytes 3000000 | tf_op jit(solution)/shard_map/pallas_call | solution.py:621
  12.4 4.6 %collective-permute-start.3 = (f32[11,8,384]{2,1,0:T(8,128)S(1)}, f32[11,8,384]{2,1,0:T(8,128)S(1)}, u32[]{:S(2)}, u32[]{:S(2)}) collective-permute-start(f32[11,8,384]{2,1,0:T(8,128)S(1)} %get-tuple-element.69), channel_id=1, source_target_pairs={{0,1},{1,0},{2,3},{3,2},{4,5},{5,4},{6,7},{7,6},{8,9},{9,8},{10,11... | collective-permute-start | bytes 405512 | tf_op jit(solution)/shard_map/ppermute | solution.py:632
  17.0 0.2 shard_map.76
  17.2 0.8 %collective-permute-done.3.refs_0_ = f32[11,8,384]{2,1,0:T(8,128)S(1)} collective-permute-done((f32[11,8,384]{2,1,0:T(8,128)S(1)}, f32[11,8,384]{2,1,0:T(8,128)S(1)}, u32[]{:S(2)}, u32[]{:S(2)}) %collective-permute-start.3) | collective-permute-done | bytes 135200 | tf_op jit(solution)/shard_map/ppermute | solution.py:632
  18.0 0.1 shard_map.77
  18.1 1.1 %collective-permute-start.6 = (f32[11,8,384]{2,1,0:T(8,128)S(1)}, f32[11,8,384]{2,1,0:T(8,128)S(1)}, u32[]{:S(2)}, u32[]{:S(2)}) collective-permute-start(f32[11,8,384]{2,1,0:T(8,128)S(1)} %get-tuple-element.75.mine), channel_id=1, source_target_pairs={{0,4},{1,5},{2,6},{3,7},{4,0},{5,1},{6,2},{7,3},{8,12},{9,13},{10,... | collective-permute-start | bytes 405512 | tf_op jit(solution)/shard_map/ppermute | solution.py:632
  19.1 1.0 %collective-permute-start.5 = (f32[11,8,384]{2,1,0:T(8,128)S(1)}, f32[11,8,384]{2,1,0:T(8,128)S(1)}, u32[]{:S(2)}, u32[]{:S(2)}) collective-permute-start(f32[11,8,384]{2,1,0:T(8,128)S(1)} %get-tuple-element.75.mine), channel_id=1, source_target_pairs={{0,7},{1,6},{2,5},{3,4},{4,3},{5,2},{6,1},{7,0},{8,15},{9,14},{10,... | collective-permute-start | bytes 405512 | tf_op jit(solution)/shard_map/ppermute | solution.py:632
  20.1 1.0 %collective-permute-start.4 = (f32[11,8,384]{2,1,0:T(8,128)S(1)}, f32[11,8,384]{2,1,0:T(8,128)S(1)}, u32[]{:S(2)}, u32[]{:S(2)}) collective-permute-start(f32[11,8,384]{2,1,0:T(8,128)S(1)} %get-tuple-element.75.mine), channel_id=1, source_target_pairs={{0,3},{1,2},{2,1},{3,0},{4,7},{5,6},{6,5},{7,4},{8,11},{9,10},{10,... | collective-permute-start | bytes 405512 | tf_op jit(solution)/shard_map/ppermute | solution.py:632
  21.1 0.0 copy-done.4
  21.1 1.3 %shard_map.78 = (f32[32,32,384]{2,1,0:T(8,128)S(1)}, f32[32,32,384]{2,1,0:T(8,128)S(1)}, f32[2,32,384]{2,1,0:T(8,128)S(1)}, f32[2,32,384]{2,1,0:T(8,128)S(1)}) custom-call(f32[4]{0:T(128)} %uptake_table, s32[32,32,384]{2,1,0:T(8,128)S(1)} %copy-done, s32[32,32,384]{2,1,0:T(8,128)S(1)} %copy-done.1, f32[32,32,384]{2,1,0:T(8,128)S(1)} %copy-done.4), custom_call_target="tpu_custom_call" | custom-call | flops 4000000 | bytes 6000000 | tf_op jit(solution)/shard_map/pallas_call | solution.py:621
  22.4 2.1 %collective-permute-done.6.refs_2_ = f32[11,8,384]{2,1,0:T(8,128)S(1)} collective-permute-done((f32[11,8,384]{2,1,0:T(8,128)S(1)}, f32[11,8,384]{2,1,0:T(8,128)S(1)}, u32[]{:S(2)}, u32[]{:S(2)}) %collective-permute-start.6) | collective-permute-done | bytes 135200 | tf_op jit(solution)/shard_map/ppermute | solution.py:632
  24.5 3.7 %collective-permute-done.5.refs_1_ = f32[11,8,384]{2,1,0:T(8,128)S(1)} collective-permute-done((f32[11,8,384]{2,1,0:T(8,128)S(1)}, f32[11,8,384]{2,1,0:T(8,128)S(1)}, u32[]{:S(2)}, u32[]{:S(2)}) %collective-permute-start.5) | collective-permute-done | bytes 135200 | tf_op jit(solution)/shard_map/ppermute | solution.py:632
  28.1 0.0 collective-permute-done.4.refs_0_
  28.1 0.2 shard_map.79
  28.4 1.4 %collective-permute-start.9 = (f32[11,8,384]{2,1,0:T(8,128)S(1)}, f32[11,8,384]{2,1,0:T(8,128)S(1)}, u32[]{:S(2)}, u32[]{:S(2)}) collective-permute-start(f32[11,8,384]{2,1,0:T(8,128)S(1)} %get-tuple-element.76.mine), channel_id=1, source_target_pairs={{0,16},{1,17},{2,18},{3,19},{4,20},{5,21},{6,22},{7,23},{8,24},{9,... | collective-permute-start | bytes 405512 | tf_op jit(solution)/shard_map/ppermute | solution.py:632
  29.8 1.1 %collective-permute-start.8 = (f32[11,8,384]{2,1,0:T(8,128)S(1)}, f32[11,8,384]{2,1,0:T(8,128)S(1)}, u32[]{:S(2)}, u32[]{:S(2)}) collective-permute-start(f32[11,8,384]{2,1,0:T(8,128)S(1)} %get-tuple-element.76.mine), channel_id=1, source_target_pairs={{0,25},{1,24},{2,27},{3,26},{4,29},{5,28},{6,31},{7,30},{8,17},{9,... | collective-permute-start | bytes 405512 | tf_op jit(solution)/shard_map/ppermute | solution.py:632
  31.0 0.4 collective-permute-start.7
  31.4 0.2 collective-permute-start.11
  31.5 2.5 %collective-permute-start.12 = (f32[2,32,384]{2,1,0:T(8,128)S(1)}, f32[2,32,384]{2,1,0:T(8,128)S(1)}, u32[]{:S(2)}, u32[]{:S(2)}) collective-permute-start(f32[2,32,384]{2,1,0:T(8,128)S(1)} %get-tuple-element.94), channel_id=1, source_target_pairs={{32,0},{64,32},{96,64},{0,96},{33,1},{65,33},{97,65},{1,97},{34,2}... | collective-permute-start | bytes 294920 | tf_op jit(solution)/shard_map/ppermute | solution.py:655
  34.1 0.7 %collective-permute-done.9.refs_2_ = f32[11,8,384]{2,1,0:T(8,128)S(1)} collective-permute-done((f32[11,8,384]{2,1,0:T(8,128)S(1)}, f32[11,8,384]{2,1,0:T(8,128)S(1)}, u32[]{:S(2)}, u32[]{:S(2)}) %collective-permute-start.9) | collective-permute-done | bytes 135200 | tf_op jit(solution)/shard_map/ppermute | solution.py:632
  34.7 3.7 %collective-permute-done.8.refs_1_ = f32[11,8,384]{2,1,0:T(8,128)S(1)} collective-permute-done((f32[11,8,384]{2,1,0:T(8,128)S(1)}, f32[11,8,384]{2,1,0:T(8,128)S(1)}, u32[]{:S(2)}, u32[]{:S(2)}) %collective-permute-start.8) | collective-permute-done | bytes 135200 | tf_op jit(solution)/shard_map/ppermute | solution.py:632
  38.4 0.0 collective-permute-done.7.refs_0_
  38.4 0.2 shard_map.80
  38.7 0.5 collective-permute-start.10
  39.2 0.7 %shard_map.81 = (f32[32,16,384]{2,1,0:T(8,128)S(1)}, f32[32,16,384]{2,1,0:T(8,128)S(1)}) custom-call(f32[5,8,384]{2,1,0:T(8,128)S(1)} %get-tuple-element.83.own, f32[32,32,384]{2,1,0:T(8,128)S(1)} %get-tuple-element.63.s_ref, f32[32,32,384]{2,1,0:T(8,128)S(1)} %get-tuple-element.56.g_ref, f32[32,32,384]{2,1,0:T(8,128)S(1)} %get-tuple-element.57.r_ref, ...), custom_call_target="tpu_custom_call" | custom-call | flops 2000000 | bytes 3000000 | tf_op jit(solution)/shard_map/pallas_call | solution.py:621
  39.9 0.0 collective-permute-done.11.reaction_lo
  39.9 0.0 collective-permute-done.12.reaction_hi
  39.9 0.2 collective-permute-done.10.other
  40.0 1.8 %shard_map.82 = (f32[32,16,384]{2,1,0:T(8,128)S(1)}, f32[32,16,384]{2,1,0:T(8,128)S(1)}, f32[4,8,384]{2,1,0:T(8,128)S(1)}) custom-call(f32[5,8,384]{2,1,0:T(8,128)S(1)} %get-tuple-element.83.own, f32[5,8,384]{2,1,0:T(8,128)S(1)} %collective-permute-done.10.other, f32[32,16,384]{2,1,0:T(8,128)S(1)} %get-tuple-element.89.state_own, ...), custom_call_target="tpu_custom_call" | custom-call | flops 6000000 | bytes 9000000 | tf_op jit(solution)/shard_map/pallas_call | solution.py:621
  41.9 0.5 collective-permute-start.13
  42.4 0.2 shard_map.83
  42.6 0.8 %collective-permute-done.13.refs_0_ = f32[4,8,384]{2,1,0:T(8,128)S(1)} collective-permute-done((f32[4,8,384]{2,1,0:T(8,128)S(1)}, f32[4,8,384]{2,1,0:T(8,128)S(1)}, u32[]{:S(2)}, u32[]{:S(2)}) %collective-permute-start.13) | collective-permute-done | bytes 49184 | tf_op jit(solution)/shard_map/ppermute | solution.py:632
  43.4 1.0 %collective-permute-start.16 = (f32[4,8,384]{2,1,0:T(8,128)S(1)}, f32[4,8,384]{2,1,0:T(8,128)S(1)}, u32[]{:S(2)}, u32[]{:S(2)}) collective-permute-start(f32[4,8,384]{2,1,0:T(8,128)S(1)} %get-tuple-element.98.mine), channel_id=1, source_target_pairs={{0,4},{1,5},{2,6},{3,7},{4,0},{5,1},{6,2},{7,3},{8,12},{9,13},{10,... | collective-permute-start | bytes 147464 | tf_op jit(solution)/shard_map/ppermute | solution.py:632
  44.4 1.0 %collective-permute-start.15 = (f32[4,8,384]{2,1,0:T(8,128)S(1)}, f32[4,8,384]{2,1,0:T(8,128)S(1)}, u32[]{:S(2)}, u32[]{:S(2)}) collective-permute-start(f32[4,8,384]{2,1,0:T(8,128)S(1)} %get-tuple-element.98.mine), channel_id=1, source_target_pairs={{0,7},{1,6},{2,5},{3,4},{4,3},{5,2},{6,1},{7,0},{8,15},{9,14},{10,... | collective-permute-start | bytes 147464 | tf_op jit(solution)/shard_map/ppermute | solution.py:632
  45.5 0.9 %collective-permute-start.14 = (f32[4,8,384]{2,1,0:T(8,128)S(1)}, f32[4,8,384]{2,1,0:T(8,128)S(1)}, u32[]{:S(2)}, u32[]{:S(2)}) collective-permute-start(f32[4,8,384]{2,1,0:T(8,128)S(1)} %get-tuple-element.98.mine), channel_id=1, source_target_pairs={{0,3},{1,2},{2,1},{3,0},{4,7},{5,6},{6,5},{7,4},{8,11},{9,10},{10,... | collective-permute-start | bytes 147464 | tf_op jit(solution)/shard_map/ppermute | solution.py:632
  46.4 1.5 %collective-permute-done.16.refs_2_ = f32[4,8,384]{2,1,0:T(8,128)S(1)} collective-permute-done((f32[4,8,384]{2,1,0:T(8,128)S(1)}, f32[4,8,384]{2,1,0:T(8,128)S(1)}, u32[]{:S(2)}, u32[]{:S(2)}) %collective-permute-start.16) | collective-permute-done | bytes 49184 | tf_op jit(solution)/shard_map/ppermute | solution.py:632
  47.9 2.1 %collective-permute-done.15.refs_1_ = f32[4,8,384]{2,1,0:T(8,128)S(1)} collective-permute-done((f32[4,8,384]{2,1,0:T(8,128)S(1)}, f32[4,8,384]{2,1,0:T(8,128)S(1)}, u32[]{:S(2)}, u32[]{:S(2)}) %collective-permute-start.15) | collective-permute-done | bytes 49184 | tf_op jit(solution)/shard_map/ppermute | solution.py:632
  50.0 0.0 collective-permute-done.14.refs_0_
  50.0 0.1 shard_map.85
  50.0 1.8 %collective-permute-start.19 = (f32[4,8,384]{2,1,0:T(8,128)S(1)}, f32[4,8,384]{2,1,0:T(8,128)S(1)}, u32[]{:S(2)}, u32[]{:S(2)}) collective-permute-start(f32[4,8,384]{2,1,0:T(8,128)S(1)} %get-tuple-element.99.mine), channel_id=1, source_target_pairs={{0,16},{1,17},{2,18},{3,19},{4,20},{5,21},{6,22},{7,23},{8,24},{9,... | collective-permute-start | bytes 147464 | tf_op jit(solution)/shard_map/ppermute | solution.py:632
  51.9 1.6 %collective-permute-start.18 = (f32[4,8,384]{2,1,0:T(8,128)S(1)}, f32[4,8,384]{2,1,0:T(8,128)S(1)}, u32[]{:S(2)}, u32[]{:S(2)}) collective-permute-start(f32[4,8,384]{2,1,0:T(8,128)S(1)} %get-tuple-element.99.mine), channel_id=1, source_target_pairs={{0,25},{1,24},{2,27},{3,26},{4,29},{5,28},{6,31},{7,30},{8,17},{9,... | collective-permute-start | bytes 147464 | tf_op jit(solution)/shard_map/ppermute | solution.py:632
  53.5 0.0 collective-permute-start.17
  53.5 1.1 %collective-permute-done.19.refs_2_ = f32[4,8,384]{2,1,0:T(8,128)S(1)} collective-permute-done((f32[4,8,384]{2,1,0:T(8,128)S(1)}, f32[4,8,384]{2,1,0:T(8,128)S(1)}, u32[]{:S(2)}, u32[]{:S(2)}) %collective-permute-start.19) | collective-permute-done | bytes 49184 | tf_op jit(solution)/shard_map/ppermute | solution.py:632
  54.6 2.8 %collective-permute-done.18.refs_1_ = f32[4,8,384]{2,1,0:T(8,128)S(1)} collective-permute-done((f32[4,8,384]{2,1,0:T(8,128)S(1)}, f32[4,8,384]{2,1,0:T(8,128)S(1)}, u32[]{:S(2)}, u32[]{:S(2)}) %collective-permute-start.18) | collective-permute-done | bytes 49184 | tf_op jit(solution)/shard_map/ppermute | solution.py:632
  57.4 0.0 collective-permute-done.17.refs_0_
  57.4 0.1 shard_map.86
  57.5 0.5 collective-permute-start.20
  58.0 0.2 shard_map.87.state_own
  58.2 0.7 %collective-permute-done.20.other = f32[4,8,384]{2,1,0:T(8,128)S(1)} collective-permute-done((f32[4,8,384]{2,1,0:T(8,128)S(1)}, f32[4,8,384]{2,1,0:T(8,128)S(1)}, u32[]{:S(2)}, u32[]{:S(2)}) %collective-permute-start.20) | collective-permute-done | bytes 49184 | tf_op jit(solution)/shard_map/ppermute | solution.py:632
  58.9 1.2 %shard_map.88 = f32[32,32,384]{2,1,0:T(8,128)} custom-call(f32[4,8,384]{2,1,0:T(8,128)S(1)} %collective-permute-done.20.other, f32[32,16,384]{2,1,0:T(8,128)S(1)} %shard_map.87.state_own, f32[32,32,384]{2,1,0:T(8,128)S(1)} %get-tuple-element.56.g_ref, f32[32,32,384]{2,1,0:T(8,128)S(1)} %get-tuple-element.57.r_ref, ...), custom_call_target="tpu_custom_call" | custom-call | flops 2000000 | bytes 3000000 | tf_op jit(solution)/shard_map/pallas_call | solution.py:621
  (4 shorter events, 0.0 us)
Async XLA Ops:
  0.0 7.1 %copy-start.1 = (s32[32,32,384]{2,1,0:T(8,128)S(1)}, s32[32,32,384]{2,1,0:T(8,128)}, u32[]{:S(2)}) copy-start(s32[32,32,384]{2,1,0:T(8,128)} %layer.3) | copy-start | bytes 4718596
  0.0 7.1 %copy-start = (s32[32,32,384]{2,1,0:T(8,128)S(1)}, s32[32,32,384]{2,1,0:T(8,128)}, u32[]{:S(2)}) copy-start(s32[32,32,384]{2,1,0:T(8,128)} %mask.3) | copy-start | bytes 4718596
  0.0 7.1 %copy-start.3 = (f32[32,32,384]{2,1,0:T(8,128)S(1)}, f32[32,32,384]{2,1,0:T(8,128)}, u32[]{:S(2)}) copy-start(f32[32,32,384]{2,1,0:T(8,128)} %stiff_hbm.1) | copy-start | bytes 4718596
  0.0 7.1 %copy-start.2 = (f32[32,32,384]{2,1,0:T(8,128)S(1)}, f32[32,32,384]{2,1,0:T(8,128)}, u32[]{:S(2)}) copy-start(f32[32,32,384]{2,1,0:T(8,128)} %conc_hbm.1) | copy-start | bytes 4718596
  2.8 7.8 %collective-permute-start.1 = (f32[3,32,384]{2,1,0:T(8,128)S(1)}, f32[3,32,384]{2,1,0:T(8,128)S(1)}, u32[]{:S(2)}, u32[]{:S(2)}) collective-permute-start(f32[3,32,384]{2,1,0:T(8,128)S(1)} %get-tuple-element.61.own_lo), channel_id=1, source_target_pairs={{32,0},{64,32},{96,64},{0,96},{33,1},{65,33},{97,65},{1,97},{34,2}... | collective-permute-start | bytes 442376 | tf_op jit(solution)/shard_map/ppermute | solution.py:655
  6.2 5.6 %collective-permute-start = (f32[3,32,384]{2,1,0:T(8,128)S(1)}, f32[3,32,384]{2,1,0:T(8,128)S(1)}, u32[]{:S(2)}, u32[]{:S(2)}) collective-permute-start(f32[3,32,384]{2,1,0:T(8,128)S(1)} %get-tuple-element.62.own_hi), channel_id=1, source_target_pairs={{0,32},{32,64},{64,96},{96,0},{1,33},{33,65},{65,97},{97,1},{2,34}... | collective-permute-start | bytes 442376 | tf_op jit(solution)/shard_map/ppermute | solution.py:654
  6.2 4.4 %collective-permute-start.2 = (f32[32,384]{1,0:T(8,128)S(1)}, f32[32,384]{1,0:T(8,128)S(1)}, u32[]{:S(2)}, u32[]{:S(2)}) collective-permute-start(f32[32,384]{1,0:T(8,128)S(1)} %get-tuple-element.64), channel_id=1, source_target_pairs={{1,0},{2,1},{3,2},{4,3},{5,4},{6,5},{7,6},{8,7},{9,8},{10,9},{11,1... | collective-permute-start | bytes 147464 | tf_op jit(solution)/shard_map/ppermute | solution.py:658
  12.4 5.6 %collective-permute-start.3 = (f32[11,8,384]{2,1,0:T(8,128)S(1)}, f32[11,8,384]{2,1,0:T(8,128)S(1)}, u32[]{:S(2)}, u32[]{:S(2)}) collective-permute-start(f32[11,8,384]{2,1,0:T(8,128)S(1)} %get-tuple-element.69), channel_id=1, source_target_pairs={{0,1},{1,0},{2,3},{3,2},{4,5},{5,4},{6,7},{7,6},{8,9},{9,8},{10,11... | collective-permute-start | bytes 405512 | tf_op jit(solution)/shard_map/ppermute | solution.py:632
  17.0 4.1 %copy-start.4 = (f32[32,32,384]{2,1,0:T(8,128)S(1)}, f32[32,32,384]{2,1,0:T(8,128)}, u32[]{:S(2)}) copy-start(f32[32,32,384]{2,1,0:T(8,128)} %prod.1) | copy-start | bytes 4718596
  18.1 6.4 %collective-permute-start.6 = (f32[11,8,384]{2,1,0:T(8,128)S(1)}, f32[11,8,384]{2,1,0:T(8,128)S(1)}, u32[]{:S(2)}, u32[]{:S(2)}) collective-permute-start(f32[11,8,384]{2,1,0:T(8,128)S(1)} %get-tuple-element.75.mine), channel_id=1, source_target_pairs={{0,4},{1,5},{2,6},{3,7},{4,0},{5,1},{6,2},{7,3},{8,12},{9,13},{10,... | collective-permute-start | bytes 405512 | tf_op jit(solution)/shard_map/ppermute | solution.py:632
  19.1 9.0 %collective-permute-start.5 = (f32[11,8,384]{2,1,0:T(8,128)S(1)}, f32[11,8,384]{2,1,0:T(8,128)S(1)}, u32[]{:S(2)}, u32[]{:S(2)}) collective-permute-start(f32[11,8,384]{2,1,0:T(8,128)S(1)} %get-tuple-element.75.mine), channel_id=1, source_target_pairs={{0,7},{1,6},{2,5},{3,4},{4,3},{5,2},{6,1},{7,0},{8,15},{9,14},{10,... | collective-permute-start | bytes 405512 | tf_op jit(solution)/shard_map/ppermute | solution.py:632
  20.1 8.1 %collective-permute-start.4 = (f32[11,8,384]{2,1,0:T(8,128)S(1)}, f32[11,8,384]{2,1,0:T(8,128)S(1)}, u32[]{:S(2)}, u32[]{:S(2)}) collective-permute-start(f32[11,8,384]{2,1,0:T(8,128)S(1)} %get-tuple-element.75.mine), channel_id=1, source_target_pairs={{0,3},{1,2},{2,1},{3,0},{4,7},{5,6},{6,5},{7,4},{8,11},{9,10},{10,... | collective-permute-start | bytes 405512 | tf_op jit(solution)/shard_map/ppermute | solution.py:632
  28.4 6.3 %collective-permute-start.9 = (f32[11,8,384]{2,1,0:T(8,128)S(1)}, f32[11,8,384]{2,1,0:T(8,128)S(1)}, u32[]{:S(2)}, u32[]{:S(2)}) collective-permute-start(f32[11,8,384]{2,1,0:T(8,128)S(1)} %get-tuple-element.76.mine), channel_id=1, source_target_pairs={{0,16},{1,17},{2,18},{3,19},{4,20},{5,21},{6,22},{7,23},{8,24},{9,... | collective-permute-start | bytes 405512 | tf_op jit(solution)/shard_map/ppermute | solution.py:632
  29.8 8.6 %collective-permute-start.8 = (f32[11,8,384]{2,1,0:T(8,128)S(1)}, f32[11,8,384]{2,1,0:T(8,128)S(1)}, u32[]{:S(2)}, u32[]{:S(2)}) collective-permute-start(f32[11,8,384]{2,1,0:T(8,128)S(1)} %get-tuple-element.76.mine), channel_id=1, source_target_pairs={{0,25},{1,24},{2,27},{3,26},{4,29},{5,28},{6,31},{7,30},{8,17},{9,... | collective-permute-start | bytes 405512 | tf_op jit(solution)/shard_map/ppermute | solution.py:632
  31.0 7.5 %collective-permute-start.7 = (f32[11,8,384]{2,1,0:T(8,128)S(1)}, f32[11,8,384]{2,1,0:T(8,128)S(1)}, u32[]{:S(2)}, u32[]{:S(2)}) collective-permute-start(f32[11,8,384]{2,1,0:T(8,128)S(1)} %get-tuple-element.76.mine), channel_id=1, source_target_pairs={{0,9},{1,8},{2,11},{3,10},{4,13},{5,12},{6,15},{7,14},{8,1},{9,0},... | collective-permute-start | bytes 405512 | tf_op jit(solution)/shard_map/ppermute | solution.py:632
  31.4 8.5 %collective-permute-start.11 = (f32[2,32,384]{2,1,0:T(8,128)S(1)}, f32[2,32,384]{2,1,0:T(8,128)S(1)}, u32[]{:S(2)}, u32[]{:S(2)}) collective-permute-start(f32[2,32,384]{2,1,0:T(8,128)S(1)} %get-tuple-element.93), channel_id=1, source_target_pairs={{0,32},{32,64},{64,96},{96,0},{1,33},{33,65},{65,97},{97,1},{2,34}... | collective-permute-start | bytes 294920 | tf_op jit(solution)/shard_map/ppermute | solution.py:654
  31.5 8.3 %collective-permute-start.12 = (f32[2,32,384]{2,1,0:T(8,128)S(1)}, f32[2,32,384]{2,1,0:T(8,128)S(1)}, u32[]{:S(2)}, u32[]{:S(2)}) collective-permute-start(f32[2,32,384]{2,1,0:T(8,128)S(1)} %get-tuple-element.94), channel_id=1, source_target_pairs={{32,0},{64,32},{96,64},{0,96},{33,1},{65,33},{97,65},{1,97},{34,2}... | collective-permute-start | bytes 294920 | tf_op jit(solution)/shard_map/ppermute | solution.py:655
  38.7 1.4 %collective-permute-start.10 = (f32[5,8,384]{2,1,0:T(8,128)S(1)}, f32[5,8,384]{2,1,0:T(8,128)S(1)}, u32[]{:S(2)}, u32[]{:S(2)}) collective-permute-start(f32[5,8,384]{2,1,0:T(8,128)S(1)} %get-tuple-element.84), channel_id=1, source_target_pairs={{0,1},{1,0},{2,3},{3,2},{4,5},{5,4},{6,7},{7,6},{8,9},{9,8},{10,11... | collective-permute-start | bytes 184328 | tf_op jit(solution)/shard_map/ppermute | solution.py:632
  41.9 1.5 %collective-permute-start.13 = (f32[4,8,384]{2,1,0:T(8,128)S(1)}, f32[4,8,384]{2,1,0:T(8,128)S(1)}, u32[]{:S(2)}, u32[]{:S(2)}) collective-permute-start(f32[4,8,384]{2,1,0:T(8,128)S(1)} %get-tuple-element.97), channel_id=1, source_target_pairs={{0,1},{1,0},{2,3},{3,2},{4,5},{5,4},{6,7},{7,6},{8,9},{9,8},{10,11... | collective-permute-start | bytes 147464 | tf_op jit(solution)/shard_map/ppermute | solution.py:632
  43.4 4.5 %collective-permute-start.16 = (f32[4,8,384]{2,1,0:T(8,128)S(1)}, f32[4,8,384]{2,1,0:T(8,128)S(1)}, u32[]{:S(2)}, u32[]{:S(2)}) collective-permute-start(f32[4,8,384]{2,1,0:T(8,128)S(1)} %get-tuple-element.98.mine), channel_id=1, source_target_pairs={{0,4},{1,5},{2,6},{3,7},{4,0},{5,1},{6,2},{7,3},{8,12},{9,13},{10,... | collective-permute-start | bytes 147464 | tf_op jit(solution)/shard_map/ppermute | solution.py:632
  44.4 5.5 %collective-permute-start.15 = (f32[4,8,384]{2,1,0:T(8,128)S(1)}, f32[4,8,384]{2,1,0:T(8,128)S(1)}, u32[]{:S(2)}, u32[]{:S(2)}) collective-permute-start(f32[4,8,384]{2,1,0:T(8,128)S(1)} %get-tuple-element.98.mine), channel_id=1, source_target_pairs={{0,7},{1,6},{2,5},{3,4},{4,3},{5,2},{6,1},{7,0},{8,15},{9,14},{10,... | collective-permute-start | bytes 147464 | tf_op jit(solution)/shard_map/ppermute | solution.py:632
  45.5 4.5 %collective-permute-start.14 = (f32[4,8,384]{2,1,0:T(8,128)S(1)}, f32[4,8,384]{2,1,0:T(8,128)S(1)}, u32[]{:S(2)}, u32[]{:S(2)}) collective-permute-start(f32[4,8,384]{2,1,0:T(8,128)S(1)} %get-tuple-element.98.mine), channel_id=1, source_target_pairs={{0,3},{1,2},{2,1},{3,0},{4,7},{5,6},{6,5},{7,4},{8,11},{9,10},{10,... | collective-permute-start | bytes 147464 | tf_op jit(solution)/shard_map/ppermute | solution.py:632
  50.0 4.5 %collective-permute-start.19 = (f32[4,8,384]{2,1,0:T(8,128)S(1)}, f32[4,8,384]{2,1,0:T(8,128)S(1)}, u32[]{:S(2)}, u32[]{:S(2)}) collective-permute-start(f32[4,8,384]{2,1,0:T(8,128)S(1)} %get-tuple-element.99.mine), channel_id=1, source_target_pairs={{0,16},{1,17},{2,18},{3,19},{4,20},{5,21},{6,22},{7,23},{8,24},{9,... | collective-permute-start | bytes 147464 | tf_op jit(solution)/shard_map/ppermute | solution.py:632
  51.9 5.5 %collective-permute-start.18 = (f32[4,8,384]{2,1,0:T(8,128)S(1)}, f32[4,8,384]{2,1,0:T(8,128)S(1)}, u32[]{:S(2)}, u32[]{:S(2)}) collective-permute-start(f32[4,8,384]{2,1,0:T(8,128)S(1)} %get-tuple-element.99.mine), channel_id=1, source_target_pairs={{0,25},{1,24},{2,27},{3,26},{4,29},{5,28},{6,31},{7,30},{8,17},{9,... | collective-permute-start | bytes 147464 | tf_op jit(solution)/shard_map/ppermute | solution.py:632
  53.5 3.9 %collective-permute-start.17 = (f32[4,8,384]{2,1,0:T(8,128)S(1)}, f32[4,8,384]{2,1,0:T(8,128)S(1)}, u32[]{:S(2)}, u32[]{:S(2)}) collective-permute-start(f32[4,8,384]{2,1,0:T(8,128)S(1)} %get-tuple-element.99.mine), channel_id=1, source_target_pairs={{0,9},{1,8},{2,11},{3,10},{4,13},{5,12},{6,15},{7,14},{8,1},{9,0},... | collective-permute-start | bytes 147464 | tf_op jit(solution)/shard_map/ppermute | solution.py:632
  57.5 1.4 %collective-permute-start.20 = (f32[4,8,384]{2,1,0:T(8,128)S(1)}, f32[4,8,384]{2,1,0:T(8,128)S(1)}, u32[]{:S(2)}, u32[]{:S(2)}) collective-permute-start(f32[4,8,384]{2,1,0:T(8,128)S(1)} %get-tuple-element.103), channel_id=1, source_target_pairs={{0,1},{1,0},{2,3},{3,2},{4,5},{5,4},{6,7},{7,6},{8,9},{9,8},{10,11... | collective-permute-start | bytes 147464 | tf_op jit(solution)/shard_map/ppermute | solution.py:632

commit v5 on v4

--- a/solution.py
+++ b/solution.py
@@ -651,8 +651,10 @@
         specs=[smem] + [hbm] * 4,
     )
     def from_neighbours(lo, hi):
-        return (lax.ppermute(hi, "xs", [(i, (i + 1) % nx) for i in range(nx)]),
-                lax.ppermute(lo, "xs", [((i + 1) % nx, i) for i in range(nx)]))
+        odd = lax.rem(lax.axis_index("xs"), 2) == 1
+        first = lax.ppermute(jnp.where(odd, lo, hi), "xs", [(i, i ^ 1) for i in range(nx)])
+        second = lax.ppermute(jnp.where(odd, hi, lo), "xs", [(i, nx - 1 - i) for i in range(nx)])
+        return jnp.where(odd, first, second), jnp.where(odd, second, first)
 
     from_lo, from_hi = from_neighbours(lo, hi)
     above_s = lax.ppermute(first_s, "ax", [((i + 1) % nax, i) for i in range(nax)])

time: 60.3 us -> 59.6 us (0.988)
    ppermute x4, waiting for transfers between devices: 1.18 us -> 0.01 us  [the longest x2 0.01 us: from_neighbours(): lax.ppermute(jnp.where(odd, hi, lo), 'xs', [(i, nx - 1 - i) for i in rang...]
    ppermute x4, starting transfers between devices: 6.06 us -> 5.03 us  [the longest x2 4.29 us: from_neighbours(): lax.ppermute(jnp.where(odd, hi, lo), 'xs', [(i, nx - 1 - i) for i in rang...]
where the time goes in v5:
time: 59.6 us; the launch traced here: 59.4 us
  starting transfers between devices  25.2 us (42%)
  waiting for transfers between devices  20.6 us (35%)
  Pallas kernels  13.2 us (22%)
    ppermute x16, waiting for transfers between devices, exchange(): lax.ppermute(block, 'ax', route)  20.6 us
    ppermute x16, starting transfers between devices, exchange(): lax.ppermute(block, 'ax', route)  19 us
    pallas_call x16, Pallas kernels, call(): pl.pallas_call(kernel, out_shape=outs, in_specs=specs or [vspec()] * len(...  13.2 us
    ppermute x2, starting transfers between devices, from_neighbours(): lax.ppermute(jnp.where(odd, hi, lo), 'xs', [(i, nx - 1 - i) for i in rang...  4.29 us
  transfers between devices with their start and end apart: 21, of which 13 were waited for; matrix products, arithmetic and copies ran while one was open for 0% of the time, Pallas kernels for 11%

profile of v5, /device:TPU:1, one launch (start us, length us, event | category | flops | bytes accessed | tf_op | source)
XLA Modules:
  0.0 59.4 jit_solution(11801246072207318520)
XLA Ops:
  0.0 0.0 copy-start
  0.0 0.0 copy-start.3
  0.0 2.8 %shard_map.74 = (f32[3,32,384]{2,1,0:T(8,128)S(1)}, f32[3,32,384]{2,1,0:T(8,128)S(1)}, f32[32,384]{1,0:T(8,128)S(1)}) custom-call(f32[4]{0:T(128)} %diff_table.1, f32[32,32,384]{2,1,0:T(8,128)} %conc_hbm.1, s32[32,32,384]{2,1,0:T(8,128)} %mask.3, s32[32,32,384]{2,1,0:T(8,128)} %layer.3, f32[32,32,384]{2,1,0:T(8,128)} %stiff_hbm.1), custom_call_target="tpu_custom_call" | custom-call | flops 2000000 | bytes 3000000 | tf_op jit(solution)/shard_map/pallas_call | solution.py:621
  2.8 3.4 %collective-permute-start.1 = (f32[3,32,384]{2,1,0:T(8,128)S(1)}, f32[3,32,384]{2,1,0:T(8,128)S(1)}, u32[]{:S(2)}, u32[]{:S(2)}) collective-permute-start(f32[3,32,384]{2,1,0:T(8,128)S(1)} %get-tuple-element.109), channel_id=1, source_target_pairs={{0,96},{32,64},{64,32},{96,0},{1,97},{33,65},{65,33},{97,1},{2,98}... | collective-permute-start | bytes 442376 | tf_op jit(solution)/shard_map/ppermute | solution.py:656
  6.2 0.0 collective-permute-start
  6.2 1.2 %collective-permute-start.2 = (f32[32,384]{1,0:T(8,128)S(1)}, f32[32,384]{1,0:T(8,128)S(1)}, u32[]{:S(2)}, u32[]{:S(2)}) collective-permute-start(f32[32,384]{1,0:T(8,128)S(1)} %get-tuple-element.64), channel_id=1, source_target_pairs={{1,0},{2,1},{3,2},{4,3},{5,4},{6,5},{7,6},{8,7},{9,8},{10,9},{11,1... | collective-permute-start | bytes 147464 | tf_op jit(solution)/shard_map/ppermute | solution.py:660
  7.4 0.0 copy-done
  7.4 0.0 copy-done.1
  7.4 0.0 copy-done.2
  7.4 0.0 copy-done.3
  7.4 3.4 %shard_map.73 = (f32[32,32,384]{2,1,0:T(8,128)S(1)}, f32[32,32,384]{2,1,0:T(8,128)S(1)}, f32[32,32,384]{2,1,0:T(8,128)S(1)}, f32[32,32,384]{2,1,0:T(8,128)S(1)},...) custom-call(f32[4]{0:T(128)} %diff_table.1, f32[32,32,384]{2,1,0:T(8,128)S(1)} %copy-done.2, ...), custom_call_target="tpu_custom_call" | custom-call | flops 10000000 | bytes 15000000 | tf_op jit(solution)/shard_map/pallas_call | solution.py:621
  10.8 0.0 collective-permute-done.1
  10.9 0.0 collective-permute-done
  10.9 0.1 collective-permute-done.2.above_ref
  11.0 0.6 %shard_map.75 = (f32[2,32,384]{2,1,0:T(8,128)S(1)}, f32[2,32,384]{2,1,0:T(8,128)S(1)}, f32[32,16,384]{2,1,0:T(8,128)S(1)}, f32[11,8,384]{2,1,0:T(8,128)S(1)}, f3...) custom-call(f32[3,32,384]{2,1,0:T(8,128)S(1)} %get-tuple-element.61.own_lo, ...), custom_call_target="tpu_custom_call" | custom-call | flops 2000000 | bytes 3000000 | tf_op jit(solution)/shard_map/pallas_call | solution.py:621
  11.6 5.4 %collective-permute-start.3 = (f32[11,8,384]{2,1,0:T(8,128)S(1)}, f32[11,8,384]{2,1,0:T(8,128)S(1)}, u32[]{:S(2)}, u32[]{:S(2)}) collective-permute-start(f32[11,8,384]{2,1,0:T(8,128)S(1)} %get-tuple-element.69), channel_id=1, source_target_pairs={{0,1},{1,0},{2,3},{3,2},{4,5},{5,4},{6,7},{7,6},{8,9},{9,8},{10,11... | collective-permute-start | bytes 405512 | tf_op jit(solution)/shard_map/ppermute | solution.py:632
  17.1 0.2 shard_map.76
  17.3 0.8 %collective-permute-done.3.refs_0_ = f32[11,8,384]{2,1,0:T(8,128)S(1)} collective-permute-done((f32[11,8,384]{2,1,0:T(8,128)S(1)}, f32[11,8,384]{2,1,0:T(8,128)S(1)}, u32[]{:S(2)}, u32[]{:S(2)}) %collective-permute-start.3) | collective-permute-done | bytes 135200 | tf_op jit(solution)/shard_map/ppermute | solution.py:632
  18.1 0.1 shard_map.77
  18.1 0.1 collective-permute-start.6
  18.2 0.7 %collective-permute-start.5 = (f32[11,8,384]{2,1,0:T(8,128)S(1)}, f32[11,8,384]{2,1,0:T(8,128)S(1)}, u32[]{:S(2)}, u32[]{:S(2)}) collective-permute-start(f32[11,8,384]{2,1,0:T(8,128)S(1)} %get-tuple-element.75.mine), channel_id=1, source_target_pairs={{0,7},{1,6},{2,5},{3,4},{4,3},{5,2},{6,1},{7,0},{8,15},{9,14},{10,... | collective-permute-start | bytes 405512 | tf_op jit(solution)/shard_map/ppermute | solution.py:632
  18.9 2.2 %collective-permute-start.4 = (f32[11,8,384]{2,1,0:T(8,128)S(1)}, f32[11,8,384]{2,1,0:T(8,128)S(1)}, u32[]{:S(2)}, u32[]{:S(2)}) collective-permute-start(f32[11,8,384]{2,1,0:T(8,128)S(1)} %get-tuple-element.75.mine), channel_id=1, source_target_pairs={{0,3},{1,2},{2,1},{3,0},{4,7},{5,6},{6,5},{7,4},{8,11},{9,10},{10,... | collective-permute-start | bytes 405512 | tf_op jit(solution)/shard_map/ppermute | solution.py:632
  21.1 0.0 copy-done.4
  21.1 1.3 %shard_map.78 = (f32[32,32,384]{2,1,0:T(8,128)S(1)}, f32[32,32,384]{2,1,0:T(8,128)S(1)}, f32[2,32,384]{2,1,0:T(8,128)S(1)}, f32[2,32,384]{2,1,0:T(8,128)S(1)}) custom-call(f32[4]{0:T(128)} %uptake_table, s32[32,32,384]{2,1,0:T(8,128)S(1)} %copy-done, s32[32,32,384]{2,1,0:T(8,128)S(1)} %copy-done.1, f32[32,32,384]{2,1,0:T(8,128)S(1)} %copy-done.4), custom_call_target="tpu_custom_call" | custom-call | flops 4000000 | bytes 6000000 | tf_op jit(solution)/shard_map/pallas_call | solution.py:621
  22.4 2.1 %collective-permute-done.6.refs_2_ = f32[11,8,384]{2,1,0:T(8,128)S(1)} collective-permute-done((f32[11,8,384]{2,1,0:T(8,128)S(1)}, f32[11,8,384]{2,1,0:T(8,128)S(1)}, u32[]{:S(2)}, u32[]{:S(2)}) %collective-permute-start.6) | collective-permute-done | bytes 135200 | tf_op jit(solution)/shard_map/ppermute | solution.py:632
  24.6 3.6 %collective-permute-done.5.refs_1_ = f32[11,8,384]{2,1,0:T(8,128)S(1)} collective-permute-done((f32[11,8,384]{2,1,0:T(8,128)S(1)}, f32[11,8,384]{2,1,0:T(8,128)S(1)}, u32[]{:S(2)}, u32[]{:S(2)}) %collective-permute-start.5) | collective-permute-done | bytes 135200 | tf_op jit(solution)/shard_map/ppermute | solution.py:632
  28.2 0.0 collective-permute-done.4.refs_0_
  28.2 0.2 shard_map.79
  28.4 0.5 collective-permute-start.9
  28.9 1.3 %collective-permute-start.8 = (f32[11,8,384]{2,1,0:T(8,128)S(1)}, f32[11,8,384]{2,1,0:T(8,128)S(1)}, u32[]{:S(2)}, u32[]{:S(2)}) collective-permute-start(f32[11,8,384]{2,1,0:T(8,128)S(1)} %get-tuple-element.76.mine), channel_id=1, source_target_pairs={{0,25},{1,24},{2,27},{3,26},{4,29},{5,28},{6,31},{7,30},{8,17},{9,... | collective-permute-start | bytes 405512 | tf_op jit(solution)/shard_map/ppermute | solution.py:632
  30.2 1.2 %collective-permute-start.7 = (f32[11,8,384]{2,1,0:T(8,128)S(1)}, f32[11,8,384]{2,1,0:T(8,128)S(1)}, u32[]{:S(2)}, u32[]{:S(2)}) collective-permute-start(f32[11,8,384]{2,1,0:T(8,128)S(1)} %get-tuple-element.76.mine), channel_id=1, source_target_pairs={{0,9},{1,8},{2,11},{3,10},{4,13},{5,12},{6,15},{7,14},{8,1},{9,0},... | collective-permute-start | bytes 405512 | tf_op jit(solution)/shard_map/ppermute | solution.py:632
  31.4 0.9 %collective-permute-start.12 = (f32[2,32,384]{2,1,0:T(8,128)S(1)}, f32[2,32,384]{2,1,0:T(8,128)S(1)}, u32[]{:S(2)}, u32[]{:S(2)}) collective-permute-start(f32[2,32,384]{2,1,0:T(8,128)S(1)} %get-tuple-element.113), channel_id=1, source_target_pairs={{0,96},{32,64},{64,32},{96,0},{1,97},{33,65},{65,33},{97,1},{2,98}... | collective-permute-start | bytes 294920 | tf_op jit(solution)/shard_map/ppermute | solution.py:656
  32.3 0.7 %collective-permute-start.11 = (f32[2,32,384]{2,1,0:T(8,128)S(1)}, f32[2,32,384]{2,1,0:T(8,128)S(1)}, u32[]{:S(2)}, u32[]{:S(2)}) collective-permute-start(f32[2,32,384]{2,1,0:T(8,128)S(1)} %get-tuple-element.114), channel_id=1, source_target_pairs={{0,32},{32,0},{64,96},{96,64},{1,33},{33,1},{65,97},{97,65},{2,34}... | collective-permute-start | bytes 294920 | tf_op jit(solution)/shard_map/ppermute | solution.py:655
  33.1 1.7 %collective-permute-done.9.refs_2_ = f32[11,8,384]{2,1,0:T(8,128)S(1)} collective-permute-done((f32[11,8,384]{2,1,0:T(8,128)S(1)}, f32[11,8,384]{2,1,0:T(8,128)S(1)}, u32[]{:S(2)}, u32[]{:S(2)}) %collective-permute-start.9) | collective-permute-done | bytes 135200 | tf_op jit(solution)/shard_map/ppermute | solution.py:632
  34.8 3.7 %collective-permute-done.8.refs_1_ = f32[11,8,384]{2,1,0:T(8,128)S(1)} collective-permute-done((f32[11,8,384]{2,1,0:T(8,128)S(1)}, f32[11,8,384]{2,1,0:T(8,128)S(1)}, u32[]{:S(2)}, u32[]{:S(2)}) %collective-permute-start.8) | collective-permute-done | bytes 135200 | tf_op jit(solution)/shard_map/ppermute | solution.py:632
  38.5 0.0 collective-permute-done.7.refs_0_
  38.5 0.2 shard_map.80
  38.7 0.5 collective-permute-start.10
  39.2 0.0 collective-permute-done.12
  39.2 0.0 collective-permute-done.11
  39.2 0.7 %shard_map.81 = (f32[32,16,384]{2,1,0:T(8,128)S(1)}, f32[32,16,384]{2,1,0:T(8,128)S(1)}) custom-call(f32[5,8,384]{2,1,0:T(8,128)S(1)} %get-tuple-element.83.own, f32[32,32,384]{2,1,0:T(8,128)S(1)} %get-tuple-element.63.s_ref, f32[32,32,384]{2,1,0:T(8,128)S(1)} %get-tuple-element.56.g_ref, f32[32,32,384]{2,1,0:T(8,128)S(1)} %get-tuple-element.57.r_ref, ...), custom_call_target="tpu_custom_call" | custom-call | flops 2000000 | bytes 3000000 | tf_op jit(solution)/shard_map/pallas_call | solution.py:621
  40.0 0.1 collective-permute-done.10.other
  40.1 1.8 %shard_map.82 = (f32[32,16,384]{2,1,0:T(8,128)S(1)}, f32[32,16,384]{2,1,0:T(8,128)S(1)}, f32[4,8,384]{2,1,0:T(8,128)S(1)}) custom-call(f32[5,8,384]{2,1,0:T(8,128)S(1)} %get-tuple-element.83.own, f32[5,8,384]{2,1,0:T(8,128)S(1)} %collective-permute-done.10.other, f32[32,16,384]{2,1,0:T(8,128)S(1)} %get-tuple-element.89.state_own, ...), custom_call_target="tpu_custom_call" | custom-call | flops 6000000 | bytes 9000000 | tf_op jit(solution)/shard_map/pallas_call | solution.py:621
  41.9 0.3 collective-permute-start.13
  42.3 0.2 shard_map.83
  42.5 0.8 %collective-permute-done.13.refs_0_ = f32[4,8,384]{2,1,0:T(8,128)S(1)} collective-permute-done((f32[4,8,384]{2,1,0:T(8,128)S(1)}, f32[4,8,384]{2,1,0:T(8,128)S(1)}, u32[]{:S(2)}, u32[]{:S(2)}) %collective-permute-start.13) | collective-permute-done | bytes 49184 | tf_op jit(solution)/shard_map/ppermute | solution.py:632
  43.3 0.3 collective-permute-start.16
  43.5 1.1 %collective-permute-start.15 = (f32[4,8,384]{2,1,0:T(8,128)S(1)}, f32[4,8,384]{2,1,0:T(8,128)S(1)}, u32[]{:S(2)}, u32[]{:S(2)}) collective-permute-start(f32[4,8,384]{2,1,0:T(8,128)S(1)} %get-tuple-element.98.mine), channel_id=1, source_target_pairs={{0,7},{1,6},{2,5},{3,4},{4,3},{5,2},{6,1},{7,0},{8,15},{9,14},{10,... | collective-permute-start | bytes 147464 | tf_op jit(solution)/shard_map/ppermute | solution.py:632
  44.7 1.8 %collective-permute-start.14 = (f32[4,8,384]{2,1,0:T(8,128)S(1)}, f32[4,8,384]{2,1,0:T(8,128)S(1)}, u32[]{:S(2)}, u32[]{:S(2)}) collective-permute-start(f32[4,8,384]{2,1,0:T(8,128)S(1)} %get-tuple-element.98.mine), channel_id=1, source_target_pairs={{0,3},{1,2},{2,1},{3,0},{4,7},{5,6},{6,5},{7,4},{8,11},{9,10},{10,... | collective-permute-start | bytes 147464 | tf_op jit(solution)/shard_map/ppermute | solution.py:632
  46.5 1.6 %collective-permute-done.16.refs_2_ = f32[4,8,384]{2,1,0:T(8,128)S(1)} collective-permute-done((f32[4,8,384]{2,1,0:T(8,128)S(1)}, f32[4,8,384]{2,1,0:T(8,128)S(1)}, u32[]{:S(2)}, u32[]{:S(2)}) %collective-permute-start.16) | collective-permute-done | bytes 49184 | tf_op jit(solution)/shard_map/ppermute | solution.py:632
  48.0 1.8 %collective-permute-done.15.refs_1_ = f32[4,8,384]{2,1,0:T(8,128)S(1)} collective-permute-done((f32[4,8,384]{2,1,0:T(8,128)S(1)}, f32[4,8,384]{2,1,0:T(8,128)S(1)}, u32[]{:S(2)}, u32[]{:S(2)}) %collective-permute-start.15) | collective-permute-done | bytes 49184 | tf_op jit(solution)/shard_map/ppermute | solution.py:632
  49.8 0.0 collective-permute-done.14.refs_0_
  49.8 0.1 shard_map.85
  49.9 0.9 %collective-permute-start.19 = (f32[4,8,384]{2,1,0:T(8,128)S(1)}, f32[4,8,384]{2,1,0:T(8,128)S(1)}, u32[]{:S(2)}, u32[]{:S(2)}) collective-permute-start(f32[4,8,384]{2,1,0:T(8,128)S(1)} %get-tuple-element.99.mine), channel_id=1, source_target_pairs={{0,16},{1,17},{2,18},{3,19},{4,20},{5,21},{6,22},{7,23},{8,24},{9,... | collective-permute-start | bytes 147464 | tf_op jit(solution)/shard_map/ppermute | solution.py:632
  50.8 1.7 %collective-permute-start.18 = (f32[4,8,384]{2,1,0:T(8,128)S(1)}, f32[4,8,384]{2,1,0:T(8,128)S(1)}, u32[]{:S(2)}, u32[]{:S(2)}) collective-permute-start(f32[4,8,384]{2,1,0:T(8,128)S(1)} %get-tuple-element.99.mine), channel_id=1, source_target_pairs={{0,25},{1,24},{2,27},{3,26},{4,29},{5,28},{6,31},{7,30},{8,17},{9,... | collective-permute-start | bytes 147464 | tf_op jit(solution)/shard_map/ppermute | solution.py:632
  52.5 0.4 collective-permute-start.17
  52.9 1.5 %collective-permute-done.19.refs_2_ = f32[4,8,384]{2,1,0:T(8,128)S(1)} collective-permute-done((f32[4,8,384]{2,1,0:T(8,128)S(1)}, f32[4,8,384]{2,1,0:T(8,128)S(1)}, u32[]{:S(2)}, u32[]{:S(2)}) %collective-permute-start.19) | collective-permute-done | bytes 49184 | tf_op jit(solution)/shard_map/ppermute | solution.py:632
  54.4 2.2 %collective-permute-done.18.refs_1_ = f32[4,8,384]{2,1,0:T(8,128)S(1)} collective-permute-done((f32[4,8,384]{2,1,0:T(8,128)S(1)}, f32[4,8,384]{2,1,0:T(8,128)S(1)}, u32[]{:S(2)}, u32[]{:S(2)}) %collective-permute-start.18) | collective-permute-done | bytes 49184 | tf_op jit(solution)/shard_map/ppermute | solution.py:632
  56.6 0.0 collective-permute-done.17.refs_0_
  56.6 0.1 shard_map.86
  56.7 0.5 collective-permute-start.20
  57.2 0.2 shard_map.87.state_own
  57.5 0.7 %collective-permute-done.20.other = f32[4,8,384]{2,1,0:T(8,128)S(1)} collective-permute-done((f32[4,8,384]{2,1,0:T(8,128)S(1)}, f32[4,8,384]{2,1,0:T(8,128)S(1)}, u32[]{:S(2)}, u32[]{:S(2)}) %collective-permute-start.20) | collective-permute-done | bytes 49184 | tf_op jit(solution)/shard_map/ppermute | solution.py:632
  58.1 1.2 %shard_map.88 = f32[32,32,384]{2,1,0:T(8,128)} custom-call(f32[4,8,384]{2,1,0:T(8,128)S(1)} %collective-permute-done.20.other, f32[32,16,384]{2,1,0:T(8,128)S(1)} %shard_map.87.state_own, f32[32,32,384]{2,1,0:T(8,128)S(1)} %get-tuple-element.56.g_ref, f32[32,32,384]{2,1,0:T(8,128)S(1)} %get-tuple-element.57.r_ref, ...), custom_call_target="tpu_custom_call" | custom-call | flops 2000000 | bytes 3000000 | tf_op jit(solution)/shard_map/pallas_call | solution.py:621
  (8 shorter events, 0.1 us)
Async XLA Ops:
  0.0 7.4 %copy-start = (s32[32,32,384]{2,1,0:T(8,128)S(1)}, s32[32,32,384]{2,1,0:T(8,128)}, u32[]{:S(2)}) copy-start(s32[32,32,384]{2,1,0:T(8,128)} %mask.3) | copy-start | bytes 4718596
  0.0 7.4 %copy-start.1 = (s32[32,32,384]{2,1,0:T(8,128)S(1)}, s32[32,32,384]{2,1,0:T(8,128)}, u32[]{:S(2)}) copy-start(s32[32,32,384]{2,1,0:T(8,128)} %layer.3) | copy-start | bytes 4718596
  0.0 7.4 %copy-start.2 = (f32[32,32,384]{2,1,0:T(8,128)S(1)}, f32[32,32,384]{2,1,0:T(8,128)}, u32[]{:S(2)}) copy-start(f32[32,32,384]{2,1,0:T(8,128)} %conc_hbm.1) | copy-start | bytes 4718596
  0.0 7.4 %copy-start.3 = (f32[32,32,384]{2,1,0:T(8,128)S(1)}, f32[32,32,384]{2,1,0:T(8,128)}, u32[]{:S(2)}) copy-start(f32[32,32,384]{2,1,0:T(8,128)} %stiff_hbm.1) | copy-start | bytes 4718596
  2.8 8.0 %collective-permute-start.1 = (f32[3,32,384]{2,1,0:T(8,128)S(1)}, f32[3,32,384]{2,1,0:T(8,128)S(1)}, u32[]{:S(2)}, u32[]{:S(2)}) collective-permute-start(f32[3,32,384]{2,1,0:T(8,128)S(1)} %get-tuple-element.109), channel_id=1, source_target_pairs={{0,96},{32,64},{64,32},{96,0},{1,97},{33,65},{65,33},{97,1},{2,98}... | collective-permute-start | bytes 442376 | tf_op jit(solution)/shard_map/ppermute | solution.py:656
  6.2 4.7 %collective-permute-start = (f32[3,32,384]{2,1,0:T(8,128)S(1)}, f32[3,32,384]{2,1,0:T(8,128)S(1)}, u32[]{:S(2)}, u32[]{:S(2)}) collective-permute-start(f32[3,32,384]{2,1,0:T(8,128)S(1)} %get-tuple-element.110), channel_id=1, source_target_pairs={{0,32},{32,0},{64,96},{96,64},{1,33},{33,1},{65,97},{97,65},{2,34}... | collective-permute-start | bytes 442376 | tf_op jit(solution)/shard_map/ppermute | solution.py:655
  6.2 4.8 %collective-permute-start.2 = (f32[32,384]{1,0:T(8,128)S(1)}, f32[32,384]{1,0:T(8,128)S(1)}, u32[]{:S(2)}, u32[]{:S(2)}) collective-permute-start(f32[32,384]{1,0:T(8,128)S(1)} %get-tuple-element.64), channel_id=1, source_target_pairs={{1,0},{2,1},{3,2},{4,3},{5,4},{6,5},{7,6},{8,7},{9,8},{10,9},{11,1... | collective-permute-start | bytes 147464 | tf_op jit(solution)/shard_map/ppermute | solution.py:660
  11.6 6.4 %collective-permute-start.3 = (f32[11,8,384]{2,1,0:T(8,128)S(1)}, f32[11,8,384]{2,1,0:T(8,128)S(1)}, u32[]{:S(2)}, u32[]{:S(2)}) collective-permute-start(f32[11,8,384]{2,1,0:T(8,128)S(1)} %get-tuple-element.69), channel_id=1, source_target_pairs={{0,1},{1,0},{2,3},{3,2},{4,5},{5,4},{6,7},{7,6},{8,9},{9,8},{10,11... | collective-permute-start | bytes 405512 | tf_op jit(solution)/shard_map/ppermute | solution.py:632
  17.1 4.1 %copy-start.4 = (f32[32,32,384]{2,1,0:T(8,128)S(1)}, f32[32,32,384]{2,1,0:T(8,128)}, u32[]{:S(2)}) copy-start(f32[32,32,384]{2,1,0:T(8,128)} %prod.1) | copy-start | bytes 4718596
  18.1 6.4 %collective-permute-start.6 = (f32[11,8,384]{2,1,0:T(8,128)S(1)}, f32[11,8,384]{2,1,0:T(8,128)S(1)}, u32[]{:S(2)}, u32[]{:S(2)}) collective-permute-start(f32[11,8,384]{2,1,0:T(8,128)S(1)} %get-tuple-element.75.mine), channel_id=1, source_target_pairs={{0,4},{1,5},{2,6},{3,7},{4,0},{5,1},{6,2},{7,3},{8,12},{9,13},{10,... | collective-permute-start | bytes 405512 | tf_op jit(solution)/shard_map/ppermute | solution.py:632
  18.2 10.0 %collective-permute-start.5 = (f32[11,8,384]{2,1,0:T(8,128)S(1)}, f32[11,8,384]{2,1,0:T(8,128)S(1)}, u32[]{:S(2)}, u32[]{:S(2)}) collective-permute-start(f32[11,8,384]{2,1,0:T(8,128)S(1)} %get-tuple-element.75.mine), channel_id=1, source_target_pairs={{0,7},{1,6},{2,5},{3,4},{4,3},{5,2},{6,1},{7,0},{8,15},{9,14},{10,... | collective-permute-start | bytes 405512 | tf_op jit(solution)/shard_map/ppermute | solution.py:632
  18.9 9.2 %collective-permute-start.4 = (f32[11,8,384]{2,1,0:T(8,128)S(1)}, f32[11,8,384]{2,1,0:T(8,128)S(1)}, u32[]{:S(2)}, u32[]{:S(2)}) collective-permute-start(f32[11,8,384]{2,1,0:T(8,128)S(1)} %get-tuple-element.75.mine), channel_id=1, source_target_pairs={{0,3},{1,2},{2,1},{3,0},{4,7},{5,6},{6,5},{7,4},{8,11},{9,10},{10,... | collective-permute-start | bytes 405512 | tf_op jit(solution)/shard_map/ppermute | solution.py:632
  28.4 6.4 %collective-permute-start.9 = (f32[11,8,384]{2,1,0:T(8,128)S(1)}, f32[11,8,384]{2,1,0:T(8,128)S(1)}, u32[]{:S(2)}, u32[]{:S(2)}) collective-permute-start(f32[11,8,384]{2,1,0:T(8,128)S(1)} %get-tuple-element.76.mine), channel_id=1, source_target_pairs={{0,16},{1,17},{2,18},{3,19},{4,20},{5,21},{6,22},{7,23},{8,24},{9,... | collective-permute-start | bytes 405512 | tf_op jit(solution)/shard_map/ppermute | solution.py:632
  28.9 9.6 %collective-permute-start.8 = (f32[11,8,384]{2,1,0:T(8,128)S(1)}, f32[11,8,384]{2,1,0:T(8,128)S(1)}, u32[]{:S(2)}, u32[]{:S(2)}) collective-permute-start(f32[11,8,384]{2,1,0:T(8,128)S(1)} %get-tuple-element.76.mine), channel_id=1, source_target_pairs={{0,25},{1,24},{2,27},{3,26},{4,29},{5,28},{6,31},{7,30},{8,17},{9,... | collective-permute-start | bytes 405512 | tf_op jit(solution)/shard_map/ppermute | solution.py:632
  30.2 8.3 %collective-permute-start.7 = (f32[11,8,384]{2,1,0:T(8,128)S(1)}, f32[11,8,384]{2,1,0:T(8,128)S(1)}, u32[]{:S(2)}, u32[]{:S(2)}) collective-permute-start(f32[11,8,384]{2,1,0:T(8,128)S(1)} %get-tuple-element.76.mine), channel_id=1, source_target_pairs={{0,9},{1,8},{2,11},{3,10},{4,13},{5,12},{6,15},{7,14},{8,1},{9,0},... | collective-permute-start | bytes 405512 | tf_op jit(solution)/shard_map/ppermute | solution.py:632
  31.4 7.8 %collective-permute-start.12 = (f32[2,32,384]{2,1,0:T(8,128)S(1)}, f32[2,32,384]{2,1,0:T(8,128)S(1)}, u32[]{:S(2)}, u32[]{:S(2)}) collective-permute-start(f32[2,32,384]{2,1,0:T(8,128)S(1)} %get-tuple-element.113), channel_id=1, source_target_pairs={{0,96},{32,64},{64,32},{96,0},{1,97},{33,65},{65,33},{97,1},{2,98}... | collective-permute-start | bytes 294920 | tf_op jit(solution)/shard_map/ppermute | solution.py:656
  32.3 6.9 %collective-permute-start.11 = (f32[2,32,384]{2,1,0:T(8,128)S(1)}, f32[2,32,384]{2,1,0:T(8,128)S(1)}, u32[]{:S(2)}, u32[]{:S(2)}) collective-permute-start(f32[2,32,384]{2,1,0:T(8,128)S(1)} %get-tuple-element.114), channel_id=1, source_target_pairs={{0,32},{32,0},{64,96},{96,64},{1,33},{33,1},{65,97},{97,65},{2,34}... | collective-permute-start | bytes 294920 | tf_op jit(solution)/shard_map/ppermute | solution.py:655
  38.7 1.4 %collective-permute-start.10 = (f32[5,8,384]{2,1,0:T(8,128)S(1)}, f32[5,8,384]{2,1,0:T(8,128)S(1)}, u32[]{:S(2)}, u32[]{:S(2)}) collective-permute-start(f32[5,8,384]{2,1,0:T(8,128)S(1)} %get-tuple-element.84), channel_id=1, source_target_pairs={{0,1},{1,0},{2,3},{3,2},{4,5},{5,4},{6,7},{7,6},{8,9},{9,8},{10,11... | collective-permute-start | bytes 184328 | tf_op jit(solution)/shard_map/ppermute | solution.py:632
  41.9 1.3 %collective-permute-start.13 = (f32[4,8,384]{2,1,0:T(8,128)S(1)}, f32[4,8,384]{2,1,0:T(8,128)S(1)}, u32[]{:S(2)}, u32[]{:S(2)}) collective-permute-start(f32[4,8,384]{2,1,0:T(8,128)S(1)} %get-tuple-element.97), channel_id=1, source_target_pairs={{0,1},{1,0},{2,3},{3,2},{4,5},{5,4},{6,7},{7,6},{8,9},{9,8},{10,11... | collective-permute-start | bytes 147464 | tf_op jit(solution)/shard_map/ppermute | solution.py:632
  43.3 4.7 %collective-permute-start.16 = (f32[4,8,384]{2,1,0:T(8,128)S(1)}, f32[4,8,384]{2,1,0:T(8,128)S(1)}, u32[]{:S(2)}, u32[]{:S(2)}) collective-permute-start(f32[4,8,384]{2,1,0:T(8,128)S(1)} %get-tuple-element.98.mine), channel_id=1, source_target_pairs={{0,4},{1,5},{2,6},{3,7},{4,0},{5,1},{6,2},{7,3},{8,12},{9,13},{10,... | collective-permute-start | bytes 147464 | tf_op jit(solution)/shard_map/ppermute | solution.py:632
  43.5 6.3 %collective-permute-start.15 = (f32[4,8,384]{2,1,0:T(8,128)S(1)}, f32[4,8,384]{2,1,0:T(8,128)S(1)}, u32[]{:S(2)}, u32[]{:S(2)}) collective-permute-start(f32[4,8,384]{2,1,0:T(8,128)S(1)} %get-tuple-element.98.mine), channel_id=1, source_target_pairs={{0,7},{1,6},{2,5},{3,4},{4,3},{5,2},{6,1},{7,0},{8,15},{9,14},{10,... | collective-permute-start | bytes 147464 | tf_op jit(solution)/shard_map/ppermute | solution.py:632
  44.7 5.1 %collective-permute-start.14 = (f32[4,8,384]{2,1,0:T(8,128)S(1)}, f32[4,8,384]{2,1,0:T(8,128)S(1)}, u32[]{:S(2)}, u32[]{:S(2)}) collective-permute-start(f32[4,8,384]{2,1,0:T(8,128)S(1)} %get-tuple-element.98.mine), channel_id=1, source_target_pairs={{0,3},{1,2},{2,1},{3,0},{4,7},{5,6},{6,5},{7,4},{8,11},{9,10},{10,... | collective-permute-start | bytes 147464 | tf_op jit(solution)/shard_map/ppermute | solution.py:632
  49.9 4.5 %collective-permute-start.19 = (f32[4,8,384]{2,1,0:T(8,128)S(1)}, f32[4,8,384]{2,1,0:T(8,128)S(1)}, u32[]{:S(2)}, u32[]{:S(2)}) collective-permute-start(f32[4,8,384]{2,1,0:T(8,128)S(1)} %get-tuple-element.99.mine), channel_id=1, source_target_pairs={{0,16},{1,17},{2,18},{3,19},{4,20},{5,21},{6,22},{7,23},{8,24},{9,... | collective-permute-start | bytes 147464 | tf_op jit(solution)/shard_map/ppermute | solution.py:632
  50.8 5.8 %collective-permute-start.18 = (f32[4,8,384]{2,1,0:T(8,128)S(1)}, f32[4,8,384]{2,1,0:T(8,128)S(1)}, u32[]{:S(2)}, u32[]{:S(2)}) collective-permute-start(f32[4,8,384]{2,1,0:T(8,128)S(1)} %get-tuple-element.99.mine), channel_id=1, source_target_pairs={{0,25},{1,24},{2,27},{3,26},{4,29},{5,28},{6,31},{7,30},{8,17},{9,... | collective-permute-start | bytes 147464 | tf_op jit(solution)/shard_map/ppermute | solution.py:632
  52.5 4.1 %collective-permute-start.17 = (f32[4,8,384]{2,1,0:T(8,128)S(1)}, f32[4,8,384]{2,1,0:T(8,128)S(1)}, u32[]{:S(2)}, u32[]{:S(2)}) collective-permute-start(f32[4,8,384]{2,1,0:T(8,128)S(1)} %get-tuple-element.99.mine), channel_id=1, source_target_pairs={{0,9},{1,8},{2,11},{3,10},{4,13},{5,12},{6,15},{7,14},{8,1},{9,0},... | collective-permute-start | bytes 147464 | tf_op jit(solution)/shard_map/ppermute | solution.py:632
  56.7 1.4 %collective-permute-start.20 = (f32[4,8,384]{2,1,0:T(8,128)S(1)}, f32[4,8,384]{2,1,0:T(8,128)S(1)}, u32[]{:S(2)}, u32[]{:S(2)}) collective-permute-start(f32[4,8,384]{2,1,0:T(8,128)S(1)} %get-tuple-element.103), channel_id=1, source_target_pairs={{0,1},{1,0},{2,3},{3,2},{4,5},{5,4},{6,7},{7,6},{8,9},{9,8},{10,11... | collective-permute-start | bytes 147464 | tf_op jit(solution)/shard_map/ppermute | solution.py:632
